TPU v7x, 128 devices: a whole 4x4x4 slice. The times are simulated.
128 devices in a mesh: seq: 8 (over y, x_lo), fsdp: 16 (over z, x_hi, core).
Axes of the slice: x: 4 (x_hi: 2, x_lo: 2; x = x_hi * 2 + x_lo), y: 4, z: 4, core: 2. Of those that a mesh axis runs over, the one named last changes fastest.
Arguments:
- latents: bfloat16 [16, 1024, 1152], P('fsdp', 'seq'), may hold values from -6 to 6
- timestep: bfloat16 [16, 6912], P('fsdp'), may hold values from -0.5 to 0.5
- caption: bfloat16 [16, 120, 1152], P('fsdp'), may hold values from -6 to 6
- shift_table: bfloat16 [6912], P('fsdp'), may hold values from -0.5 to 0.5
- qkv_weight: bfloat16 [1152, 3456], P('fsdp'), may hold values from -0.1875 to 0.1875
- query_bias: bfloat16 [1152], P('fsdp'), may hold values from -2.5 to 2.5
- value_bias: bfloat16 [1152], P('fsdp'), may hold values from -2.5 to 2.5
- proj_weight: bfloat16 [1152, 1152], P('fsdp'), may hold values from -1.5 to 1.5
- proj_bias: bfloat16 [1152], P('fsdp'), may hold values from -2.5 to 2.5
- cross_query: bfloat16 [1152, 1152], P('fsdp'), may hold values from -0.1875 to 0.1875
- cross_qbias: bfloat16 [1152], P('fsdp'), may hold values from -2.5 to 2.5
- cross_kv: bfloat16 [1152, 2304], P('fsdp'), may hold values from -0.1875 to 0.1875
- cross_vbias: bfloat16 [1152], P('fsdp'), may hold values from -2.5 to 2.5
- cross_proj: bfloat16 [1152, 1152], P('fsdp'), may hold values from -0.75 to 0.75
- cross_pbias: bfloat16 [1152], P('fsdp'), may hold values from -2.5 to 2.5
- up_weight: bfloat16 [1152, 4608], P('fsdp'), may hold values from -0.1875 to 0.1875
- up_bias: bfloat16 [4608], P('fsdp'), may hold values from -2.5 to 2.5
- down_weight: bfloat16 [4608, 1152], P('fsdp'), may hold values from -0.09375 to 0.09375
- down_bias: bfloat16 [1152], P('fsdp'), may hold values from -2.5 to 2.5
- cotangent: bfloat16 [16, 1024, 1152], P('fsdp', 'seq'), may hold values from -6 to 6
Outputs:
- block_out: bfloat16 [16, 1024, 1152], P('fsdp', 'seq')
- grad_latents: float32 [16, 1024, 1152], P('fsdp', 'seq')
- grad_timestep: float32 [16, 6912], P('fsdp')
- grad_caption: float32 [16, 120, 1152], P('fsdp')
- grad_table: float32 [6912], P('fsdp')
- grad_qkv: float32 [1152, 3456], P('fsdp')
- grad_qbias: float32 [1152], P('fsdp')
- grad_vbias: float32 [1152], P('fsdp')
- grad_proj: float32 [1152, 1152], P('fsdp')
- grad_pbias: float32 [1152], P('fsdp')
- grad_cquery: float32 [1152, 1152], P('fsdp')
- grad_cqbias: float32 [1152], P('fsdp')
- grad_ckv: float32 [1152, 2304], P('fsdp')
- grad_cvbias: float32 [1152], P('fsdp')
- grad_cproj: float32 [1152, 1152], P('fsdp')
- grad_cpbias: float32 [1152], P('fsdp')
- grad_up: float32 [1152, 4608], P('fsdp')
- grad_ubias: float32 [4608], P('fsdp')
- grad_down: float32 [4608, 1152], P('fsdp')
- grad_dbias: float32 [1152], P('fsdp')
All inputs are finite; a program needn't handle non-finite values.
Results may differ from a plain program's by a relative error of at most 0.03.
Values may be sent and summed in bfloat16 or wider, within the bound.
A program may use at most 192 MiB of HBM per device.

v0:
```python
import jax
import jax.numpy as jnp
from jax import lax
from jax.sharding import PartitionSpec as P

HD = 72


epsilon = 1e-06


def for_sending(array):

    def short(part):
        return part.astype(jnp.bfloat16) if part.dtype == jnp.float32 else part

    return jax.tree.map(short, array)


def normalize(values):
    centre = values - jnp.mean(values, axis=-1, keepdims=True)
    spread = jnp.mean(centre * centre, axis=-1, keepdims=True)
    return centre * lax.rsqrt(spread + epsilon)


def modulate(values, shift, scale):
    return normalize(values) * (1.0 + scale) + shift


def project(former, latter):
    return jnp.dot(former, latter, preferred_element_type=jnp.float32)


def weight_grad(former, latter):
    return jnp.einsum("bli,blo->io", former, latter, preferred_element_type=jnp.float32)


def token_sum(values):
    return jnp.sum(values.astype(jnp.float32), axis=(0, 1))


def by_heads(matrix):
    return matrix.reshape(matrix.shape[:-1] + (matrix.shape[-1] // HD, HD))


def attend_forward(queries, key_rows, values):
    factor = HD ** (-0.5)
    scores = (
        jnp.einsum("qhd,khd->hqk", queries, key_rows, preferred_element_type=jnp.float32) * factor
    )
    largest = jnp.max(scores, axis=-1, keepdims=True)
    exponent = jnp.exp(scores - largest)
    partition = jnp.sum(exponent, axis=-1, keepdims=True)
    weights = (exponent / partition).astype(jnp.bfloat16)
    output = jnp.einsum("hqk,khd->qhd", weights, values, preferred_element_type=jnp.float32)
    return (output.astype(jnp.bfloat16), largest + jnp.log(partition))


def attend_backward(queries, key_rows, values, logsum, grad_out):
    factor = HD ** (-0.5)
    scores = (
        jnp.einsum("qhd,khd->hqk", queries, key_rows, preferred_element_type=jnp.float32) * factor
    )
    weights = jnp.exp(scores - logsum)
    grad_weights = jnp.einsum("qhd,khd->hqk", grad_out, values, preferred_element_type=jnp.float32)
    inner = jnp.sum(weights * grad_weights, axis=-1, keepdims=True)
    grad_scores = (weights * (grad_weights - inner)).astype(jnp.bfloat16)
    grad_q = (
        jnp.einsum("hqk,khd->qhd", grad_scores, key_rows, preferred_element_type=jnp.float32)
        * factor
    )
    grad_k = (
        jnp.einsum("hqk,qhd->khd", grad_scores, queries, preferred_element_type=jnp.float32)
        * factor
    )
    grad_v = jnp.einsum(
        "hqk,qhd->khd", weights.astype(jnp.bfloat16), grad_out, preferred_element_type=jnp.float32
    )
    return (grad_q, grad_k, grad_v)


def self_forward(gathered):
    output, logsum = attend_forward(
        by_heads(gathered[:, 0]), by_heads(gathered[:, 1]), by_heads(gathered[:, 2])
    )
    return (output.reshape(gathered.shape[0], -1), logsum)


def self_backward(pieces):
    gathered, logsum, grad_rows = pieces
    grad_q, grad_k, grad_v = attend_backward(
        by_heads(gathered[:, 0]),
        by_heads(gathered[:, 1]),
        by_heads(gathered[:, 2]),
        logsum,
        by_heads(grad_rows),
    )
    stacked = jnp.stack([grad_q, grad_k, grad_v], axis=1)
    return stacked.reshape(gathered.shape[0], 3, -1).astype(jnp.bfloat16)


def reduce_bucket(gradients):
    owner_part = jax.tree.map(
        lambda part: part.astype(jnp.float32),
        lax.psum_scatter(for_sending(gradients), "fsdp", scatter_dimension=0, tiled=True),
    )
    return jax.tree.map(
        lambda part: part.astype(jnp.float32), lax.psum(for_sending(owner_part), "seq")
    )


def on_device(
    latents,
    timestep,
    caption,
    shift_table,
    qkv_weight,
    query_bias,
    value_bias,
    proj_weight,
    proj_bias,
    cross_query,
    cross_qbias,
    cross_kv,
    cross_vbias,
    cross_proj,
    cross_pbias,
    up_weight,
    up_bias,
    down_weight,
    down_bias,
    cotangent,
):
    (
        full_table,
        full_qkv,
        full_qbias,
        full_vbias,
        full_proj,
        full_pbias,
        full_cquery,
        full_cqbias,
        full_ckv,
        full_cvbias,
        full_cproj,
        full_cpbias,
        full_up,
        full_ubias,
        full_down,
        full_dbias,
    ) = (
        lax.all_gather(shift_table, "fsdp", axis=0, tiled=True),
        lax.all_gather(qkv_weight, "fsdp", axis=0, tiled=True),
        lax.all_gather(query_bias, "fsdp", axis=0, tiled=True),
        lax.all_gather(value_bias, "fsdp", axis=0, tiled=True),
        lax.all_gather(proj_weight, "fsdp", axis=0, tiled=True),
        lax.all_gather(proj_bias, "fsdp", axis=0, tiled=True),
        lax.all_gather(cross_query, "fsdp", axis=0, tiled=True),
        lax.all_gather(cross_qbias, "fsdp", axis=0, tiled=True),
        lax.all_gather(cross_kv, "fsdp", axis=0, tiled=True),
        lax.all_gather(cross_vbias, "fsdp", axis=0, tiled=True),
        lax.all_gather(cross_proj, "fsdp", axis=0, tiled=True),
        lax.all_gather(cross_pbias, "fsdp", axis=0, tiled=True),
        lax.all_gather(up_weight, "fsdp", axis=0, tiled=True),
        lax.all_gather(up_bias, "fsdp", axis=0, tiled=True),
        lax.all_gather(down_weight, "fsdp", axis=0, tiled=True),
        lax.all_gather(down_bias, "fsdp", axis=0, tiled=True),
    )
    latent_count, local_len, model_width = latents.shape
    inputs = latents.astype(jnp.float32)
    modulation = (full_table.astype(jnp.float32) + timestep.astype(jnp.float32)).reshape(
        latent_count, 6, 1, model_width
    )
    shift_one, scale_one, gate_one = (modulation[:, 0], modulation[:, 1], modulation[:, 2])
    shift_two, scale_two, gate_two = (modulation[:, 3], modulation[:, 4], modulation[:, 5])
    pre_one, pull_one = jax.vjp(modulate, inputs, shift_one, scale_one)
    normed_one = pre_one.astype(jnp.bfloat16)
    qkv_bias = jnp.concatenate([full_qbias, jnp.zeros_like(full_qbias), full_vbias]).astype(
        jnp.float32
    )
    packed = (project(normed_one, full_qkv) + qkv_bias).astype(jnp.bfloat16)
    packed = packed.reshape(latent_count, local_len, 3, model_width)
    head_major = lax.all_to_all(packed, "seq", split_axis=3, concat_axis=1, tiled=True)
    attended, logsum = lax.map(self_forward, head_major)
    tok_major = lax.all_to_all(attended, "seq", split_axis=1, concat_axis=2, tiled=True)
    branch_one = project(tok_major, full_proj) + full_pbias.astype(jnp.float32)
    after_one = inputs + gate_one * branch_one
    middle = after_one.astype(jnp.bfloat16)
    cross_rows = (project(middle, full_cquery) + full_cqbias.astype(jnp.float32)).astype(
        jnp.bfloat16
    )
    kv_bias = jnp.concatenate([jnp.zeros_like(full_cvbias), full_cvbias]).astype(jnp.float32)
    text_kv = (project(caption, full_ckv) + kv_bias).astype(jnp.bfloat16)
    text_keys = by_heads(text_kv[..., :model_width])
    text_values = by_heads(text_kv[..., model_width:])
    cross_heads, cross_logsum = jax.vmap(attend_forward)(
        by_heads(cross_rows), text_keys, text_values
    )
    crossed = cross_heads.reshape(latent_count, local_len, model_width)
    branch_two = project(crossed, full_cproj) + full_cpbias.astype(jnp.float32)
    after_two = after_one + branch_two
    pre_two, pull_two = jax.vjp(modulate, after_two, shift_two, scale_two)
    normed_two = pre_two.astype(jnp.bfloat16)
    hidden = project(normed_two, full_up) + full_ubias.astype(jnp.float32)
    activated, gelu_pull = jax.vjp(jax.nn.gelu, hidden)
    act_rows = activated.astype(jnp.bfloat16)
    branch_three = project(act_rows, full_down) + full_dbias.astype(jnp.float32)
    block_out = (after_two + gate_two * branch_three).astype(jnp.bfloat16)
    grad_out = cotangent.astype(jnp.float32)
    grad_gate_two = jnp.sum(grad_out * branch_three, axis=1, keepdims=True)
    grad_three = (gate_two * grad_out).astype(jnp.bfloat16)
    down_grad = weight_grad(act_rows, grad_three)
    down_bgrad = token_sum(grad_three)
    grad_act = project(grad_three, full_down.T)
    grad_hidden = gelu_pull(grad_act)[0].astype(jnp.bfloat16)
    up_grad = weight_grad(normed_two, grad_hidden)
    up_bgrad = token_sum(grad_hidden)
    grad_pre_two = project(grad_hidden, full_up.T)
    grad_mid_two, grad_shift_two, grad_scale_two = pull_two(grad_pre_two)
    grad_after_two = grad_out + grad_mid_two
    mlp_parts = reduce_bucket((up_grad, up_bgrad, down_grad, down_bgrad))
    grad_branch_two = grad_after_two.astype(jnp.bfloat16)
    cproj_grad = weight_grad(crossed, grad_branch_two)
    cproj_bgrad = token_sum(grad_branch_two)
    grad_crossed = project(grad_branch_two, full_cproj.T).astype(jnp.bfloat16)
    grad_cq, grad_ck, grad_cv = jax.vmap(attend_backward)(
        by_heads(cross_rows), text_keys, text_values, cross_logsum, by_heads(grad_crossed)
    )
    grad_cross_rows = grad_cq.reshape(latent_count, local_len, model_width).astype(jnp.bfloat16)
    cquery_grad = weight_grad(middle, grad_cross_rows)
    cquery_bgrad = token_sum(grad_cross_rows)
    grad_after_one = grad_after_two + project(grad_cross_rows, full_cquery.T)
    text_partial = jnp.concatenate(
        [
            grad_ck.reshape(grad_ck.shape[:2] + (model_width,)),
            grad_cv.reshape(grad_cv.shape[:2] + (model_width,)),
        ],
        axis=-1,
    )
    grad_gate_one = jnp.sum(grad_after_one * branch_one, axis=1, keepdims=True)
    grad_branch_one = (gate_one * grad_after_one).astype(jnp.bfloat16)
    proj_grad = weight_grad(tok_major, grad_branch_one)
    proj_bgrad = token_sum(grad_branch_one)
    grad_tok = project(grad_branch_one, full_proj.T).astype(jnp.bfloat16)
    grad_heads = lax.all_to_all(grad_tok, "seq", split_axis=2, concat_axis=1, tiled=True)
    grad_packed_heads = lax.map(self_backward, (head_major, logsum, grad_heads))
    grad_packed = lax.all_to_all(grad_packed_heads, "seq", split_axis=1, concat_axis=3, tiled=True)
    grad_flat = grad_packed.reshape(latent_count, local_len, 3 * model_width)
    qkv_grad = weight_grad(normed_one, grad_flat)
    qbias_grad = token_sum(grad_packed[:, :, 0])
    vbias_grad = token_sum(grad_packed[:, :, 2])
    grad_pre_one = project(grad_flat, full_qkv.T)
    grad_norm_one, grad_shift_one, grad_scale_one = pull_one(grad_pre_one)
    grad_latents = grad_after_one + grad_norm_one
    grad_mod = jnp.concatenate(
        [
            grad_shift_one,
            grad_scale_one,
            grad_gate_one,
            grad_shift_two,
            grad_scale_two,
            grad_gate_two,
        ],
        axis=1,
    )
    grad_mod = grad_mod.reshape(latent_count, 6 * model_width)
    table_part = jnp.sum(grad_mod, axis=0)
    text_sum, mod_sum = (
        lax.psum_scatter(
            text_partial.astype(jnp.bfloat16), "seq", scatter_dimension=1, tiled=True
        ).astype(jnp.float32),
        lax.psum_scatter(
            grad_mod.astype(jnp.bfloat16), "seq", scatter_dimension=1, tiled=True
        ).astype(jnp.float32),
    )
    text_grad = text_sum.astype(jnp.bfloat16)
    text_piece = text_grad.shape[1]
    caption_part = lax.dynamic_slice_in_dim(
        caption, lax.axis_index("seq") * text_piece, text_piece, 1
    )
    ckv_grad = weight_grad(caption_part, text_grad)
    cvalue_bgrad = token_sum(text_grad[..., model_width:])
    caption_piece = project(text_grad, full_ckv.T)
    caption_grad, timestep_grad = (
        lax.all_gather(caption_piece.astype(jnp.bfloat16), "seq", axis=1, tiled=True).astype(
            caption_piece.dtype
        ),
        lax.all_gather(mod_sum.astype(jnp.bfloat16), "seq", axis=1, tiled=True).astype(
            mod_sum.dtype
        ),
    )
    rest = reduce_bucket(
        (
            table_part,
            qkv_grad,
            qbias_grad,
            vbias_grad,
            proj_grad,
            proj_bgrad,
            cquery_grad,
            cquery_bgrad,
            ckv_grad,
            cvalue_bgrad,
            cproj_grad,
            cproj_bgrad,
        )
    )
    return (
        block_out,
        grad_latents,
        timestep_grad,
        caption_grad,
        rest[0],
        rest[1],
        rest[2],
        rest[3],
        rest[4],
        rest[5],
        rest[6],
        rest[7],
        rest[8],
        rest[9],
        rest[10],
        rest[11],
        mlp_parts[0],
        mlp_parts[1],
        mlp_parts[2],
        mlp_parts[3],
    )


def solution(mesh):
    placed = (
        P("fsdp", "seq", None),
        P("fsdp", None),
        P("fsdp", None, None),
        P("fsdp"),
        P("fsdp", None),
        P("fsdp"),
        P("fsdp"),
        P("fsdp", None),
        P("fsdp"),
        P("fsdp", None),
        P("fsdp"),
        P("fsdp", None),
        P("fsdp"),
        P("fsdp", None),
        P("fsdp"),
        P("fsdp", None),
        P("fsdp"),
        P("fsdp", None),
        P("fsdp"),
        P("fsdp", "seq", None),
    )
    return jax.shard_map(
        on_device,
        mesh=mesh,
        in_specs=placed,
        out_specs=(
            P("fsdp", "seq", None),
            P("fsdp", "seq", None),
            P("fsdp", None),
            P("fsdp", None, None),
            P("fsdp"),
            P("fsdp", None),
            P("fsdp"),
            P("fsdp"),
            P("fsdp", None),
            P("fsdp"),
            P("fsdp", None),
            P("fsdp"),
            P("fsdp", None),
            P("fsdp"),
            P("fsdp", None),
            P("fsdp"),
            P("fsdp", None),
            P("fsdp"),
            P("fsdp", None),
            P("fsdp"),
        ),
        check_vma=False,
    )
```

profile of v0, /device:TPU:0, one launch (start us, length us, event | category | flops | bytes accessed | tf_op | source)
XLA Modules:
  0.0 1436.7 jit_solution(17479862089825871687)
XLA Ops:
  16.9 71.7 %all-reduce.26 = (bf16[1152]{0:T(1024)(128)(2,1)S(1)}, bf16[1152]{0:T(1024)(128)(2,1)S(1)}, bf16[1152]{0:T(1024)(128)(2,1)S(1)}, bf16[6912]{0:T(1024)(128)(2,1)S...) all-reduce(bf16[1152]{0:T(1024)(128)(2,1)S(1)} %dynamic-update-slic, ...), channel_id=1, replica_groups=mesh['seq'=8,'fsdp'=16] {'fsdp'}, use_global_device_ids=true, to_apply=%add.5 | all-reduce | flops 19584 | bytes 78336
  90.4 4.7 fusion.2
  96.1 6.3 copy.131
  102.4 4.9 all-to-all-start
  110.3 35.0 %all-gather.14.cloned.1.call-done = bf16[1152,2304]{1,0:T(8,128)(2,1)} async-done(((bf16[72,2304]{1,0:T(8,128)(2,1)}), bf16[1152,2304]{1,0:T(8,128)(2,1)}) %all-gather.14.cloned.1.call-update) | async-done | bytes 5308432 | tf_op jit(solution)/shard_map/all_gather | solution.py:160
  145.4 3.4 fusion.7
  152.4 1.9 copy-done.2
  154.3 1.8 fusion.28
  157.4 4.0 reduce.52
  163.0 4.3 all-to-all-start.1
  168.5 6.8 all-to-all-done.1
  175.3 1.6 reshape.720
  178.1 16.8 %all-gather.12.cloned.1.call-done = bf16[1152,1152]{1,0:T(8,128)(2,1)} async-done(((bf16[72,1152]{1,0:T(8,128)(2,1)}), bf16[1152,1152]{1,0:T(8,128)(2,1)}) %all-gather.12.cloned.1.call-update) | async-done | bytes 2654224 | tf_op jit(solution)/shard_map/all_gather | solution.py:156
  194.9 2.4 convolution_add_fusion.5
  197.4 47.9 %all-gather.16.cloned.1.call-done = bf16[1152,1152]{1,0:T(8,128)(2,1)} async-done(((bf16[72,1152]{1,0:T(8,128)(2,1)}), bf16[1152,1152]{1,0:T(8,128)(2,1)}) %all-gather.16.cloned.1.call-update) | async-done | bytes 2654224 | tf_op jit(solution)/shard_map/all_gather | solution.py:158
  245.3 2.3 fusion.11
  251.5 44.2 %all-gather.18.cloned.1.call-done = bf16[1152,1152]{1,0:T(8,128)(2,1)} async-done(((bf16[72,1152]{1,0:T(8,128)(2,1)}), bf16[1152,1152]{1,0:T(8,128)(2,1)}) %all-gather.18.cloned.1.call-update) | async-done | bytes 2654224 | tf_op jit(solution)/shard_map/all_gather | solution.py:162
  295.7 2.5 fusion.96
  298.4 81.0 %all-gather.20.cloned.1.call-done = bf16[1152,4608]{1,0:T(8,128)(2,1)} async-done(((bf16[72,4608]{1,0:T(8,128)(2,1)}), bf16[1152,4608]{1,0:T(8,128)(2,1)}) %all-gather.20.cloned.1.call-update) | async-done | bytes 10616848 | tf_op jit(solution)/shard_map/all_gather | solution.py:164
  379.4 7.2 convolution_add_fusion
  386.6 75.5 %all-gather.22.cloned.1.call-done = bf16[4608,1152]{1,0:T(8,128)(2,1)} async-done(((bf16[288,1152]{1,0:T(8,128)(2,1)}), bf16[4608,1152]{1,0:T(8,128)(2,1)}) %all-gather.22.cloned.1.call-update) | async-done | bytes 10616848 | tf_op jit(solution)/shard_map/all_gather | solution.py:166
  462.1 9.4 fusion.97
  471.5 4.0 fusion.44
  475.6 7.6 fusion.43
  484.1 1.8 convolution_convert_fusion.8
  485.9 1.8 copy.141
  493.1 2.1 copy.151
  496.4 3.4 pad_maximum_fusion
  499.9 4.2 fusion.89
  504.1 2.3 convolution_convert_fusion.6
  506.6 2.4 convolution_convert_fusion.5
  509.0 3.3 convolution_convert_fusion.4
  513.1 65.5 %all-reduce.32.cloned.1.call-done = bf16[1,120,2304]{2,0,1:T(2,128)(2,1)} async-done(((bf16[1,120,2304]{2,0,1:T(2,128)(2,1)}), bf16[1,120,2304]{2,0,1:T(2,128)(2,1)}) %all-reduce.32.cloned.1.call-update) | async-done | bytes 552976
  579.6 3.9 convolution_convert_fusion.3
  583.6 2.7 fusion.19
  587.2 6.8 reduce.53
  594.8 3.9 all-to-all-start.2
  598.8 7.4 all-to-all-done.2
  606.7 5.2 multiply_reduce_fusion
  611.9 4.8 multiply_convert_fusion
  620.7 2.5 copy.147
  623.2 4.1 reshape.723
  627.3 14.1 all_to_all.63
  641.4 5.1 reshape.724
  646.5 2.9 copy.158
  649.5 5.6 convolution_convert_fusion.2
  655.8 8.3 convolution_convert_fusion.1
  664.2 1.6 copy-done.6
  665.8 6.8 convolution_convert_fusion
  673.9 6.2 fusion.41
  684.7 47.3 %reduce-scatter.31.cloned.1.call-done = bf16[72,1152]{1,0:T(8,128)(2,1)} async-done(((bf16[1152,1152]{1,0:T(8,128)(2,1)}), bf16[72,1152]{1,0:T(8,128)(2,1)}) %reduce-scatter.31.cloned.1.call-update) | async-done | bytes 165904
  732.1 76.7 %reduce-scatter.33.cloned.1.call-done = bf16[72,1152]{1,0:T(8,128)(2,1)} async-done(((bf16[1152,1152]{1,0:T(8,128)(2,1)}), bf16[72,1152]{1,0:T(8,128)(2,1)}) %reduce-scatter.33.cloned.1.call-update) | async-done | bytes 165904
  808.7 88.4 %reduce-scatter.19.cloned.1.call-done = bf16[72,2304]{1,0:T(8,128)(2,1)} async-done(((bf16[1152,2304]{1,0:T(8,128)(2,1)}), bf16[72,2304]{1,0:T(8,128)(2,1)}) %reduce-scatter.19.cloned.1.call-update) | async-done | bytes 331792 | tf_op jit(solution)/shard_map/reduce_scatter | solution.py:105
  897.1 104.1 %reduce-scatter.27.cloned.1.call-done = bf16[72,3456]{1,0:T(8,128)(2,1)} async-done(((bf16[1152,3456]{1,0:T(8,128)(2,1)}), bf16[72,3456]{1,0:T(8,128)(2,1)}) %reduce-scatter.27.cloned.1.call-update) | async-done | bytes 497680
  1001.1 116.6 %reduce-scatter.21.cloned.1.call-done = bf16[72,4608]{1,0:T(8,128)(2,1)} async-done(((bf16[1152,4608]{1,0:T(8,128)(2,1)}), bf16[72,4608]{1,0:T(8,128)(2,1)}) %reduce-scatter.21.cloned.1.call-update) | async-done | bytes 663568 | tf_op jit(solution)/shard_map/reduce_scatter | solution.py:105
  1117.7 116.5 %reduce-scatter.23.cloned.1.call-done = bf16[288,1152]{1,0:T(8,128)(2,1)} async-done(((bf16[4608,1152]{1,0:T(8,128)(2,1)}), bf16[288,1152]{1,0:T(8,128)(2,1)}) %reduce-scatter.23.cloned.1.call-update) | async-done | bytes 663568 | tf_op jit(solution)/shard_map/reduce_scatter | solution.py:105
  1237.0 4.0 fusion.20
  1241.0 31.3 %all-gather.1 = bf16[8,15,1152]{2,1,0:T(8,128)(2,1)S(1)} all-gather(bf16[1,15,1152]{2,1,0:T(8,128)(2,1)S(1)} %fusion.20), channel_id=2, replica_groups=mesh['seq'=8,'fsdp'=16] {'seq'}, dimensions={0}, use_global_device_ids=true | all-gather | bytes 311040 | tf_op jit(solution)/shard_map/all_gather | solution.py:285
  1274.6 67.3 %all-reduce.25 = (bf16[6912]{0:T(1024)(128)(2,1)S(1)}, bf16[1152]{0:T(1024)(128)(2,1)S(1)}, bf16[1152]{0:T(1024)(128)(2,1)S(1)}, bf16[1152]{0:T(1024)(128)(2,1)S...) all-reduce(bf16[6912]{0:T(1024)(128)(2,1)S(1)} %convert_element_typ, ...), channel_id=5, replica_groups=mesh['seq'=8,'fsdp'=16] {'fsdp'}, use_global_device_ids=true, to_apply=%region_22.23.clone | all-reduce | flops 19584 | bytes 78336
  1344.0 33.9 %all-reduce.27 = (bf16[6912]{0:T(1024)(128)(2,1)S(1)}, bf16[432]{0:T(512)(128)(2,1)S(1)}, bf16[72]{0:T(256)(128)(2,1)S(1)}, bf16[72]{0:T(256)(128)(2,1)S(1)}, bf...) all-reduce(bf16[6912]{0:T(1024)(128)(2,1)S(1)} %dynamic-update-slic, ...), channel_id=1, replica_groups=mesh['seq'=8,'fsdp'=16] {'seq'}, use_global_device_ids=true, to_apply=%add.10 | all-reduce | flops 8136 | bytes 32544
  1383.3 36.9 %all-reduce.34.cloned.1.call-done = (bf16[72,3456]{1,0:T(8,128)(2,1)}, bf16[72,1152]{1,0:T(8,128)(2,1)}, bf16[72,1152]{1,0:T(8,128)(2,1)}, bf16[72,2304]{1,0:T(8...) async-done(((bf16[72,3456]{1,0:T(8,128)(2,1)}, bf16[72,1152]{1,0:T(8,128)(2,1)}, bf16[72,1152]{1,0:T(8,128)(2,1)}, ...) | async-done | bytes 2654224 | tf_op jit(solution)/shard_map/psum | solution.py:108
  1420.2 2.2 convert_element_type.367
  1422.4 1.7 convert_element_type.371
  1424.0 1.7 convert_element_type.374
  (337 shorter events, 61.5 us)
Async XLA Ops:
  7.2 138.2 %copy-start = (bf16[1,120,1152]{2,1,0:T(8,128)(2,1)S(1)}, bf16[1,120,1152]{2,1,0:T(8,128)(2,1)}, u32[]{:S(2)}) copy-start(bf16[1,120,1152]{2,1,0:T(8,128)(2,1)} %param.22) | copy-start | bytes 829444
  7.2 7.4 copy-start.77
  7.2 7.7 copy-start.78
  7.3 7.9 copy-start.79
  7.3 8.1 copy-start.80
  7.3 8.4 copy-start.81
  7.3 8.6 copy-start.82
  7.3 8.9 copy-start.83
  7.3 9.1 copy-start.73
  7.3 9.4 copy-start.74
  7.3 81.3 %copy-start.54 = (bf16[1,6912]{1,0:T(2,128)(2,1)S(1)}, bf16[1,6912]{1,0:T(2,128)(2,1)}, u32[]{:S(2)}) copy-start(bf16[1,6912]{1,0:T(2,128)(2,1)} %param.21) | copy-start | bytes 41476
  7.3 82.2 %copy-start.4 = (bf16[1,128,1152]{2,1,0:T(8,128)(2,1)S(1)}, bf16[1,128,1152]{2,1,0:T(8,128)(2,1)}, u32[]{:S(2)}) copy-start(bf16[1,128,1152]{2,1,0:T(8,128)(2,1)} %param.20) | copy-start | bytes 884740
  7.3 82.6 %all-gather.10.cloned.1.call-start = ((), (), s32[]{:S(2)}) async-start(), calls=%async_computation.12 | async-start | bytes 8460288 | tf_op jit(solution)/shard_map/all_gather | solution.py:153
  8.1 137.3 %all-gather.14.cloned.1.call-start = ((), (), s32[]{:S(2)}) async-start(), calls=%async_computation.14 | async-start | bytes 5640192 | tf_op jit(solution)/shard_map/all_gather | solution.py:160
  8.8 186.1 %all-gather.12.cloned.1.call-start = ((), (), s32[]{:S(2)}) async-start(), calls=%async_computation.13 | async-start | bytes 2820096 | tf_op jit(solution)/shard_map/all_gather | solution.py:156
  9.6 235.7 %all-gather.16.cloned.1.call-start = ((), (), s32[]{:S(2)}) async-start(), calls=%async_computation.15 | async-start | bytes 2820096 | tf_op jit(solution)/shard_map/all_gather | solution.py:158
  10.1 285.5 %all-gather.18.cloned.1.call-start = ((), (), s32[]{:S(2)}) async-start(), calls=%async_computation.16 | async-start | bytes 2820096 | tf_op jit(solution)/shard_map/all_gather | solution.py:162
  10.7 368.7 %all-gather.20.cloned.1.call-start = ((), (), s32[]{:S(2)}) async-start(), calls=%async_computation.17 | async-start | bytes 11280384 | tf_op jit(solution)/shard_map/all_gather | solution.py:164
  11.3 450.8 %all-gather.22.cloned.1.call-start = ((), (), s32[]{:S(2)}) async-start(), calls=%async_computation.18 | async-start | bytes 11280384 | tf_op jit(solution)/shard_map/all_gather | solution.py:166
  102.4 46.4 %all-to-all-start = ((bf16[1,128,3,1152]{1,2,0,3:T(4,128)(2,1)}), bf16[1,128,3,1152]{1,2,0,3:T(4,128)(2,1)S(1)}, u32[]{:S(2)}, u32[]{:S(2)}) async-start(bf16[1,128,3,1152]{1,2,0,3:T(4,128)(2,1)} %copy.131), calls=%async_computation | async-start | bytes 2359296 | tf_op jit(solution)/shard_map/all_to_all | solution.py:183
  163.0 12.3 all-to-all-start.1
  167.3 411.3 %all-reduce.32.cloned.1.call-start = ((), (), s32[]{:S(2)}) async-start(), calls=%async_computation.23 | async-start | bytes 2211840
  167.4 27.5 %copy-start.51 = (f32[1152]{0:T(1024)S(1)}, f32[1152]{0:T(1024)}, u32[]{:S(2)}) copy-start(f32[1152]{0:T(1024)} %convert_element_type.325) | copy-start | bytes 13828
  168.5 80.0 %copy-start.20 = (bf16[1,120,1152]{1,2,0:T(8,128)(2,1)}, bf16[1,120,1152]{1,2,0:T(8,128)(2,1)S(1)}, u32[]{:S(2)}) copy-start(bf16[1,120,1152]{1,2,0:T(8,128)(2,1)S(1)} %copy.140) | copy-start | bytes 829444
  177.9 19.3 %copy-start.39 = (f32[1152]{0:T(1024)S(1)}, f32[1152]{0:T(1024)}, u32[]{:S(2)}) copy-start(f32[1152]{0:T(1024)} %get-tuple-element.58) | copy-start | bytes 13828
  178.0 67.3 %copy-start.50 = (f32[1152]{0:T(1024)S(1)}, f32[1152]{0:T(1024)}, u32[]{:S(2)}) copy-start(f32[1152]{0:T(1024)} %convert_element_type.330) | copy-start | bytes 13828
  178.1 69.6 %copy-start.13 = (bf16[1,128,8,144]{1,3,2,0:T(8,128)(2,1)}, bf16[1,128,8,144]{1,3,2,0:T(8,128)(2,1)S(1)}, u32[]{:S(2)}) copy-start(bf16[1,128,8,144]{1,3,2,0:T(8,128)(2,1)S(1)} %copy.137) | copy-start | bytes 884740
  197.4 51.2 %copy-start.15 = (bf16[128,1152]{1,0:T(8,128)(2,1)}, bf16[128,1152]{1,0:T(8,128)(2,1)S(1)}, u32[]{:S(2)}) copy-start(bf16[128,1152]{1,0:T(8,128)(2,1)S(1)} %fusion.52) | copy-start | bytes 884740
  250.0 45.7 %copy-start.49 = (f32[1152]{0:T(1024)S(1)}, f32[1152]{0:T(1024)}, u32[]{:S(2)}) copy-start(f32[1152]{0:T(1024)} %convert_element_type.336) | copy-start | bytes 13828
  251.5 127.9 %copy-start.30 = (bf16[16,72,128]{2,1,0:T(8,128)(2,1)}, bf16[16,72,128]{2,1,0:T(8,128)(2,1)S(1)}, u32[]{:S(2)}) copy-start(bf16[16,72,128]{2,1,0:T(8,128)(2,1)S(1)} %convolution_convert_fusion.11) | copy-start | bytes 884740
  251.5 127.9 %copy-start.42 = (f32[4608]{0:T(1024)S(1)}, f32[4608]{0:T(1024)}, u32[]{:S(2)}) copy-start(f32[4608]{0:T(1024)} %convert_element_type.338) | copy-start | bytes 55300
  298.2 177.4 %copy-start.57 = (f32[128]{0:T(128)}, f32[128]{0:T(128)S(1)}, u32[]{:S(2)}) copy-start(f32[128]{0:T(128)S(1)} %broadcast_multiply_fusion) | copy-start | bytes 1540
  298.4 177.2 %copy-start.64 = (f32[128]{0:T(128)}, f32[128]{0:T(128)S(1)}, u32[]{:S(2)}) copy-start(f32[128]{0:T(128)S(1)} %fusion.79) | copy-start | bytes 1540
  298.4 190.9 %copy-start.41 = (f32[16,128]{1,0:T(8,128)}, f32[16,128]{1,0:T(8,128)S(1)}, u32[]{:S(2)}) copy-start(f32[16,128]{1,0:T(8,128)S(1)} %log_add_fusion.1) | copy-start | bytes 24580
  379.4 82.7 %copy-start.23 = (bf16[1,128,1152]{2,1,0:T(8,128)(2,1)S(1)}, bf16[1,128,1152]{2,1,0:T(8,128)(2,1)}, u32[]{:S(2)}) copy-start(bf16[1,128,1152]{2,1,0:T(8,128)(2,1)} %param.39) | copy-start | bytes 884740
  379.4 82.7 %copy-start.43 = (f32[1152]{0:T(1024)S(1)}, f32[1152]{0:T(1024)}, u32[]{:S(2)}) copy-start(f32[1152]{0:T(1024)} %get-tuple-element.53) | copy-start | bytes 13828
  462.1 9.4 copy-start.3
  475.6 7.7 copy-start.26
  475.6 7.6 copy-start.24
  475.6 8.5 copy-start.9
  499.8 184.9 %reduce-scatter.29.cloned.1.call-start = ((), (), s32[]{:S(2)}) async-start(), calls=%async_computation.25 | async-start | bytes 2820096
  506.5 225.6 %reduce-scatter.31.cloned.1.call-start = ((), (), s32[]{:S(2)}) async-start(), calls=%async_computation.26 | async-start | bytes 2820096
  508.9 299.8 %reduce-scatter.33.cloned.1.call-start = ((), (), s32[]{:S(2)}) async-start(), calls=%async_computation.27 | async-start | bytes 2820096
  512.4 384.7 %reduce-scatter.19.cloned.1.call-start = ((), (), s32[]{:S(2)}) async-start(), calls=%async_computation.19 | async-start | bytes 5640192 | tf_op jit(solution)/shard_map/reduce_scatter | solution.py:105
  583.6 15.2 %copy-start.46 = (f32[2,1024]{1,0:T(2,128)S(1)}, f32[2,1024]{1,0:T(2,128)}, u32[]{:S(2)}) copy-start(f32[2,1024]{1,0:T(2,128)} %copy-done.45) | copy-start | bytes 24580
  583.6 15.2 %copy-start.53 = (f32[2,1024]{1,0:T(2,128)S(1)}, f32[2,1024]{1,0:T(2,128)}, u32[]{:S(2)}) copy-start(f32[2,1024]{1,0:T(2,128)} %copy-done.52) | copy-start | bytes 24580
  587.2 19.5 %copy-start.32 = (bf16[1024,1,144]{0,2,1:T(8,128)(2,1)S(1)}, bf16[1024,1,144]{0,2,1:T(8,128)(2,1)}, u32[]{:S(2)}) copy-start(bf16[1024,1,144]{0,2,1:T(8,128)(2,1)} %copy-done.31) | copy-start | bytes 884740
  594.8 11.4 all-to-all-start.2
  598.7 402.5 %reduce-scatter.27.cloned.1.call-start = ((), (), s32[]{:S(2)}) async-start(), calls=%async_computation.24 | async-start | bytes 8460288
  606.7 12.3 slice-start
  641.4 8.1 copy-start.48
  641.4 8.1 copy-start.56
  655.1 462.6 %reduce-scatter.21.cloned.1.call-start = ((), (), s32[]{:S(2)}) async-start(), calls=%async_computation.20 | async-start | bytes 11280384 | tf_op jit(solution)/shard_map/reduce_scatter | solution.py:105
  664.1 570.1 %reduce-scatter.23.cloned.1.call-start = ((), (), s32[]{:S(2)}) async-start(), calls=%async_computation.21 | async-start | bytes 11280384 | tf_op jit(solution)/shard_map/reduce_scatter | solution.py:105
  672.5 670.1 %reduce-scatter.25.cloned.1.call-start = ((), (), s32[]{:S(2)}) async-start(), calls=%async_computation.22 | async-start | bytes 1990656
  684.3 552.5 %copy-start.59 = (bf16[16,72]{1,0:T(8,128)(2,1)S(1)}, bf16[16,72]{1,0:T(8,128)(2,1)}, u32[]{:S(2)}) copy-start(bf16[16,72]{1,0:T(8,128)(2,1)} %get-tuple-element.130) | copy-start | bytes 6916
  684.3 552.6 %copy-start.36 = (bf16[1,15,2304]{2,0,1:T(2,128)(2,1)S(1)}, bf16[1,15,2304]{2,0,1:T(2,128)(2,1)}, u32[]{:S(2)}) copy-start(bf16[1,15,2304]{2,0,1:T(2,128)(2,1)} %copy-done.35) | copy-start | bytes 207364
  684.4 735.8 %all-reduce.34.cloned.1.call-start = ((), (), s32[]{:S(2)}) async-start(), calls=%async_computation.28 | async-start | bytes 5308416 | tf_op jit(solution)/shard_map/psum | solution.py:108
  1237.0 37.6 %copy-start.61 = (bf16[1152]{0:T(1024)(128)(2,1)S(1)}, bf16[1152]{0:T(1024)(128)(2,1)}, u32[]{:S(2)}) copy-start(bf16[1152]{0:T(1024)(128)(2,1)} %get-tuple-element.94) | copy-start | bytes 6916
  1237.0 37.6 %copy-start.62 = (bf16[1152]{0:T(1024)(128)(2,1)S(1)}, bf16[1152]{0:T(1024)(128)(2,1)}, u32[]{:S(2)}) copy-start(bf16[1152]{0:T(1024)(128)(2,1)} %get-tuple-element.111) | copy-start | bytes 6916
  1237.0 37.6 %copy-start.63 = (bf16[1152]{0:T(1024)(128)(2,1)S(1)}, bf16[1152]{0:T(1024)(128)(2,1)}, u32[]{:S(2)}) copy-start(bf16[1152]{0:T(1024)(128)(2,1)} %get-tuple-element.96) | copy-start | bytes 6916
  1237.0 37.6 %copy-start.66 = (bf16[4608]{0:T(1024)(128)(2,1)S(1)}, bf16[4608]{0:T(1024)(128)(2,1)}, u32[]{:S(2)}) copy-start(bf16[4608]{0:T(1024)(128)(2,1)} %get-tuple-element.132) | copy-start | bytes 27652
  1420.2 7.2 copy-start.34
  1420.2 8.3 copy-start.33
  (42 other events, 151.0 us)
Sparse Core Ops, SparseCore 0:
  10.6 74.5 all-gather.9
  87.6 57.7 all-gather.13
  147.8 47.0 all-gather.11
  197.1 48.1 all-gather.15
  247.5 48.1 all-gather.17
  298.0 81.3 all-gather.19
  381.8 80.2 all-gather.21
  499.9 78.5 all-reduce.31
  583.3 72.7 reduce-scatter.28
  660.1 71.9 reduce-scatter.30
  736.8 71.8 reduce-scatter.32
  812.8 84.1 reduce-scatter.18
  901.4 99.6 reduce-scatter.26
  1005.9 111.7 reduce-scatter.20
  1122.5 111.7 reduce-scatter.22
  1236.6 49.9 reduce-scatter.24
  1289.9 130.2 all-reduce.33
where the time goes:
time: 1450 us; the launch traced here: 1440 us
  waiting for transfers between devices  971 us (67%)
  blocking collectives  218 us (15%)
  matrix products  114 us (8%)
  local copies, waits for them, and re-layouts  54.1 us (4%)
  other arithmetic  44 us (3%)
  between operations  21 us (1%)
    reduce_scatter x3, waiting for transfers between devices, reduce_bucket(): lax.psum_scatter(for_sending(gradients), 'fsdp', scatter_dimension=0, til...  321 us
    unnamed x23, waiting for transfers between devices  298 us
    unnamed x3, blocking collectives  173 us
    all_gather x1, waiting for transfers between devices, on_device(): lax.all_gather(up_weight, 'fsdp', axis=0, tiled=True)  81 us
    all_gather x1, waiting for transfers between devices, on_device(): lax.all_gather(down_weight, 'fsdp', axis=0, tiled=True)  75.5 us
    dot_general x14, matrix products, project(): return jnp.dot(former, latter, preferred_element_type=jnp.float32)  62.4 us
    all_gather x1, waiting for transfers between devices, on_device(): lax.all_gather(cross_query, 'fsdp', axis=0, tiled=True)  47.9 us
    all_gather x1, waiting for transfers between devices, on_device(): lax.all_gather(cross_proj, 'fsdp', axis=0, tiled=True)  44.2 us
  transfers between devices with their start and end apart: 20, of which 16 were waited for; matrix products, arithmetic and copies ran while one was open for 11% of the time, Pallas kernels for 0%

commit v1 on v0

--- a/solution.py
+++ b/solution.py
@@ -1,9 +1,14 @@
+import functools
+
 import jax
 import jax.numpy as jnp
 from jax import lax
+from jax.experimental import pallas as pl
+from jax.experimental.pallas import tpu as pltpu
 from jax.sharding import PartitionSpec as P
 
 HD = 72
+MESH = pl.DeviceIdType.MESH
 
 
 epsilon = 1e-06
@@ -99,14 +104,410 @@
     return stacked.reshape(gathered.shape[0], 3, -1).astype(jnp.bfloat16)
 
 
-def reduce_bucket(gradients):
-    owner_part = jax.tree.map(
-        lambda part: part.astype(jnp.float32),
-        lax.psum_scatter(for_sending(gradients), "fsdp", scatter_dimension=0, tiled=True),
-    )
-    return jax.tree.map(
-        lambda part: part.astype(jnp.float32), lax.psum(for_sending(owner_part), "seq")
-    )
+def place():
+    seq, fsdp = lax.axis_index("seq"), lax.axis_index("fsdp")
+    y, x_lo = seq // 2, seq % 2
+    z, rest = fsdp // 4, fsdp % 4
+    x_hi, core = rest // 2, rest % 2
+    return x_hi * 2 + x_lo, y, z, core
+
+
+def device(x, y, z, core):
+    return (y * 2 + x % 2, z * 4 + (x // 2) * 2 + core)
+
+
+def step(value, by):
+    return (value + by + 4) % 4
+
+
+class Copies:
+    def __init__(self, send, recv):
+        self.send, self.recv, self.index, self.started = send, recv, {}, []
+
+    def number(self, key):
+        return self.index.setdefault(key, len(self.index))
+
+    def push(self, key, src, dst, target):
+        at = self.number(key)
+        copy = pltpu.make_async_remote_copy(
+            src_ref=src,
+            dst_ref=dst,
+            send_sem=self.send.at[at],
+            recv_sem=self.recv.at[at],
+            device_id=target,
+            device_id_type=MESH,
+        )
+        copy.start()
+        self.started.append(copy)
+
+    def arrived(self, key, dst, source):
+        at = self.number(key)
+        pltpu.make_async_remote_copy(
+            src_ref=dst,
+            dst_ref=dst,
+            send_sem=self.send.at[at],
+            recv_sem=self.recv.at[at],
+            device_id=source,
+            device_id_type=MESH,
+        ).wait_recv()
+
+    def finish(self):
+        for copy in self.started:
+            copy.wait_send()
+
+
+def greet(others):
+    barrier = pltpu.get_barrier_semaphore()
+    for other in others:
+        pl.semaphore_signal(barrier, inc=1, device_id=other, device_id_type=MESH)
+    pl.semaphore_wait(barrier, len(others))
+
+
+def gather_kernel(up, qkv, cq, small, ckv, pair, o_up, o_qkv, o_cq, o_small, o_ckv, o_pair, local, send, recv):
+    x, y, z, c = place()
+    xh, xl = x // 2, x % 2
+    here = (x, y, z, c)
+    sibling = device(x, y, z, 1 - c)
+    far = device(step(x, 2), y, z, c)
+    along_x = [device(step(x, d), y, z, c) for d in (1, 2, 3)]
+    along_y = [device(x, step(y, d), z, c) for d in (1, 2, 3)]
+    along_z = [device(x, y, step(z, d), c) for d in (1, 2, 3)]
+    greet([sibling] + along_x + along_y + along_z)
+    copies = Copies(send, recv)
+    width = up.shape[1] // 4
+    quarter = lambda q: pl.ds(pl.multiple_of(q * width, 128), width)
+    half = lambda ref, h: pl.ds(pl.multiple_of(h * (ref.shape[-1] // 2), 128), ref.shape[-1] // 2)
+    whole = ((qkv, o_qkv, "qkv"), (cq, o_cq, "cq"), (small, o_small, "small"))
+    halved = ((ckv, o_ckv, "ckv"), (pair, o_pair, "pair"))
+
+    stays = []
+    for source, out, _ in whole:
+        stays.append((source, out.at[z, xh, c]))
+    for source, out, _ in halved:
+        stays.append((source.at[:, half(source, xl)], out.at[z, xh, c, :, half(source, xl)]))
+    stays.append((up.at[:, quarter(y)], o_up.at[z, xh, c, :, quarter(y)]))
+    stays = [pltpu.make_async_copy(a, b, local.at[i]) for i, (a, b) in enumerate(stays)]
+    for copy in stays:
+        copy.start()
+
+    for source, out, name in whole:
+        copies.push((name, "far"), source, out.at[z, xh, c], far)
+        for d, target in zip((1, 2, 3), along_z):
+            copies.push((name, "z", 0, d), source, out.at[z, xh, c], target)
+        copies.push((name, "core", 0), source, out.at[z, xh, c], sibling)
+    mine = up.at[:, quarter(y)]
+    there = o_up.at[z, xh, c, :, quarter(y)]
+    copies.push(("up", "far"), mine, there, far)
+    for source, out, name in halved:
+        for d, target in zip((1, 2, 3), along_z):
+            copies.push(
+                (name, "z", d),
+                source.at[:, half(source, xl)],
+                out.at[z, xh, c, :, half(source, xl)],
+                target,
+            )
+    for d, target in zip((1, 2, 3), along_z):
+        copies.push(("up", "z", 0, d), mine, there, target)
+    for d, target in zip((1, 2, 3), along_y):
+        copies.push(("up", "y", 0, 0, d), mine, there, target)
+    for source, out, name in halved:
+        for d, target in zip((1, 2, 3), along_x):
+            copies.push(
+                (name, "x", 0, d),
+                source.at[:, half(source, xl)],
+                out.at[z, xh, c, :, half(source, xl)],
+                target,
+            )
+    for _, out, name in whole:
+        block = out.at[z, 1 - xh, c]
+        copies.arrived((name, "far"), block, far)
+        for d, target in zip((1, 2, 3), along_z):
+            copies.push((name, "z", 1, d), block, block, target)
+        copies.push((name, "core", 1), block, block, sibling)
+    block = o_up.at[z, 1 - xh, c, :, quarter(y)]
+    copies.arrived(("up", "far"), block, far)
+    for d, target in zip((1, 2, 3), along_z):
+        copies.push(("up", "z", 1, d), block, block, target)
+    for d, target in zip((1, 2, 3), along_y):
+        copies.push(("up", "y", 0, 1, d), block, block, target)
+    for dz in (1, 2, 3):
+        from_z = step(z, -dz)
+        for _, out, name in halved:
+            block = out.at[from_z, xh, c, :, half(out, xl)]
+            copies.arrived((name, "z", dz), block, device(x, y, from_z, c))
+            for d, target in zip((1, 2, 3), along_x):
+                copies.push((name, "x", dz, d), block, block, target)
+        for flip in (0, 1):
+            block = o_up.at[from_z, (xh + flip) % 2, c, :, quarter(y)]
+            copies.arrived(("up", "z", flip, dz), block, device(x, y, from_z, c))
+            for d, target in zip((1, 2, 3), along_y):
+                copies.push(("up", "y", dz, flip, d), block, block, target)
+    for copy in stays:
+        copy.wait()
+    for _, out, name in halved:
+        block = out.at[:, xh, c, :, half(out, xl)]
+        copies.push((name, "core", 0), block, block, sibling)
+    block = o_up.at[:, :, c, :, quarter(y)]
+    copies.push(("up", "core", 0), block, block, sibling)
+    for dz in (1, 2, 3):
+        from_z = step(z, -dz)
+        for _, out, name in whole:
+            for flip in (0, 1):
+                block = out.at[from_z, (xh + flip) % 2, c]
+                copies.arrived((name, "z", flip, dz), block, device(x, y, from_z, c))
+            block = out.at[from_z, :, c]
+            copies.push((name, "core", 1 + dz), block, block, sibling)
+    for d in (1, 2, 3):
+        from_x, from_y = step(x, -d), step(y, -d)
+        for _, out, name in halved:
+            for dz in (0, 1, 2, 3):
+                block = out.at[step(z, -dz), from_x // 2, c, :, half(out, from_x % 2)]
+                copies.arrived((name, "x", dz, d), block, device(from_x, y, z, c))
+            block = out.at[:, from_x // 2, c, :, half(out, from_x % 2)]
+            copies.push((name, "core", d), block, block, sibling)
+        for dz in (0, 1, 2, 3):
+            for flip in (0, 1):
+                block = o_up.at[step(z, -dz), (xh + flip) % 2, c, :, quarter(from_y)]
+                copies.arrived(("up", "y", dz, flip, d), block, device(x, from_y, z, c))
+        block = o_up.at[:, :, c, :, quarter(from_y)]
+        copies.push(("up", "core", d), block, block, sibling)
+    for _, out, name in whole:
+        copies.arrived((name, "core", 0), out.at[z, xh, 1 - c], sibling)
+        copies.arrived((name, "core", 1), out.at[z, 1 - xh, 1 - c], sibling)
+        for dz in (1, 2, 3):
+            copies.arrived((name, "core", 1 + dz), out.at[step(z, -dz), :, 1 - c], sibling)
+    for d in (0, 1, 2, 3):
+        from_x, from_y = step(x, -d), step(y, -d)
+        for _, out, name in halved:
+            block = out.at[:, from_x // 2, 1 - c, :, half(out, from_x % 2)]
+            copies.arrived((name, "core", d), block, sibling)
+        block = o_up.at[:, :, 1 - c, :, quarter(from_y)]
+        copies.arrived(("up", "core", d), block, sibling)
+    copies.finish()
+
+
+def gather_weights(*shards):
+    count = 128
+    outs = pl.pallas_call(
+        gather_kernel,
+        out_shape=tuple(
+            jax.ShapeDtypeStruct((4, 2, 2) + shard.shape, shard.dtype) for shard in shards
+        ),
+        in_specs=[pl.BlockSpec(memory_space=pl.ANY)] * len(shards),
+        out_specs=tuple(pl.BlockSpec(memory_space=pl.ANY) for _ in shards),
+        scratch_shapes=[
+            pltpu.SemaphoreType.DMA((8,)),
+            pltpu.SemaphoreType.DMA((count,)),
+            pltpu.SemaphoreType.DMA((count,)),
+        ],
+        compiler_params=pltpu.CompilerParams(collective_id=0, has_side_effects=True),
+    )(*shards)
+    return tuple(out.reshape((-1,) + out.shape[4:]) for out in outs)
+
+
+def add_up(parts, out):
+    blocks, _, columns = out.shape
+    tile = next(t for t in (384, 640, 256, 128) if columns % t == 0)
+
+    @pl.loop(0, blocks * (columns // tile))
+    def _(i):
+        block = i // (columns // tile)
+        cols = pl.ds(pl.multiple_of((i % (columns // tile)) * tile, 128), tile)
+        total = parts[0][block, :, cols].astype(jnp.float32)
+        for part in parts[1:]:
+            total = total + part[block, :, cols].astype(jnp.float32)
+        out[block, :, cols] = total.astype(out.dtype)
+
+
+def scatter_kernel(
+    up, qkv, cq, mix, down, mod, cap,
+    o_up, o_att, o_mix, o_down, o_mod, o_cap,
+    u1, u1s, u2, u2s, u3, u3s,
+    a1, a1s, a2, a2s, a3, a3s,
+    m1, m1s, m2, m2s, m3, m3s,
+    d1, d1s, d2, d2s, t1,
+    local, send, recv,
+):
+    x, y, z, c = place()
+    xh, xl = x // 2, x % 2
+    seq = y * 2 + xl
+    peers = [((seq + e) % 8, z * 4 + xh * 2 + c) for e in range(1, 8)]
+    along_x = [device(step(x, d), y, z, c) for d in (1, 2, 3)]
+    along_y = [device(x, step(y, d), z, c) for d in (1, 2, 3)]
+    along_z = [device(x, y, step(z, d), c) for d in (1, 2, 3)]
+    far_x = [device((1 - xh) * 2 + e, y, z, c) for e in (0, 1)]
+    greet(peers + far_x + along_z)
+    copies = Copies(send, recv)
+    width = up.shape[-1] // 4
+    columns = lambda q, w: pl.ds(pl.multiple_of(q * w, 128), w)
+    side = mix.shape[-1] // 2
+    piece = side // 4
+    waits = []
+
+    def keep(src, dst):
+        copy = pltpu.make_async_copy(src, dst, local.at[len(waits)])
+        copy.start()
+        waits.append(copy)
+
+    for d in (1, 2, 3):
+        to_x, to_y, to_z = step(x, d), step(y, d), step(z, d)
+        copies.push(("u1", d), up.at[:, :, :, columns(to_y, width)], u1.at[d], along_y[d - 1])
+        copies.push(("a1", d), qkv.at[to_z], a1.at[d, :, :, pl.ds(0, 3 * width)], along_z[d - 1])
+        copies.push(("c1", d), cq.at[to_z], a1.at[d, :, :, pl.ds(3 * width, width)], along_z[d - 1])
+        copies.push(
+            ("m1", d), mix.at[:, to_x // 2, :, columns(to_x % 2, side)], m1.at[d], along_x[d - 1]
+        )
+    for d in (1, 2, 3):
+        copies.push(("d1", d), down.at[step(y, d)], d1.at[d], along_y[d - 1])
+    for e in range(1, 8):
+        copies.push(("t1", e), mod, t1.at[e], peers[e - 1])
+        copies.push(("cap", e), cap, o_cap.at[seq], peers[e - 1])
+    keep(up.at[:, :, :, columns(y, width)], u1.at[0])
+    keep(qkv.at[z], a1.at[0, :, :, pl.ds(0, 3 * width)])
+    keep(cq.at[z], a1.at[0, :, :, pl.ds(3 * width, width)])
+    keep(mix.at[:, xh, :, columns(xl, side)], m1.at[0])
+    keep(down.at[y], d1.at[0])
+    keep(mod, t1.at[0])
+    keep(cap, o_cap.at[seq])
+    for copy in waits:
+        copy.wait()
+
+    for d in (1, 2, 3):
+        copies.arrived(("d1", d), d1.at[d], along_y[3 - d])
+    add_up([d1.at[pl.ds(i, 1)] for i in range(4)], d1s)
+    copies.push(("d2",), d1s, d2, device(xh * 2 + 1 - xl, y, z, c))
+    for d in (1, 2, 3):
+        copies.arrived(("u1", d), u1.at[d], along_y[3 - d])
+    for zz in range(4):
+        add_up([u1.at[i, zz] for i in range(4)], u1s.at[zz])
+    for d in (1, 2, 3):
+        copies.push(("u2", d), u1s.at[step(z, d)], u2.at[d], along_z[d - 1])
+    for d in (1, 2, 3):
+        copies.arrived(("a1", d), a1.at[d, :, :, pl.ds(0, 3 * width)], along_z[3 - d])
+        copies.arrived(("c1", d), a1.at[d, :, :, pl.ds(3 * width, width)], along_z[3 - d])
+    add_up([a1.at[i] for i in range(4)], a1s)
+    for d in (1, 2, 3):
+        copies.push(("a2", d), a1s.at[:, :, columns(step(y, d), width)], a2.at[d], along_y[d - 1])
+    for d in (1, 2, 3):
+        copies.arrived(("m1", d), m1.at[d], along_x[3 - d])
+    add_up([m1.at[i] for i in range(4)], m1s)
+    for d in (1, 2, 3):
+        copies.push(("m2", d), m1s.at[:, :, columns(step(y, d), piece)], m2.at[d], along_y[d - 1])
+
+    copies.arrived(("d2",), d2, device(xh * 2 + 1 - xl, y, z, c))
+    add_up([d1s, d2], d2s)
+    keep(d2s.at[0], o_down.at[y])
+    for d in (1, 2, 3):
+        copies.push(("d3", d), d2s.at[0], o_down.at[y], along_y[d - 1])
+    for d in (1, 2, 3):
+        copies.arrived(("u2", d), u2.at[d], along_z[3 - d])
+    add_up([u1s.at[z]] + [u2.at[d] for d in (1, 2, 3)], u2s)
+    for d in (1, 2, 3):
+        copies.push(("u3", d), u2s.at[step(x, d) // 2], u3.at[d], along_x[d - 1])
+    for d in (1, 2, 3):
+        copies.arrived(("a2", d), a2.at[d], along_y[3 - d])
+    add_up([a1s.at[:, :, columns(y, width)]] + [a2.at[d] for d in (1, 2, 3)], a2s)
+    for d in (1, 2, 3):
+        copies.push(("a3", d), a2s.at[step(x, d) // 2], a3.at[d], along_x[d - 1])
+    for d in (1, 2, 3):
+        copies.arrived(("m2", d), m2.at[d], along_y[3 - d])
+    add_up([m1s.at[:, :, columns(y, piece)]] + [m2.at[d] for d in (1, 2, 3)], m2s)
+    for d in (1, 2, 3):
+        copies.push(("m3", d), m2s.at[step(z, d)], m3.at[d], along_z[d - 1])
+
+    for d in (1, 2, 3):
+        copies.arrived(("u3", d), u3.at[d], along_x[3 - d])
+    add_up([u2s.at[pl.ds(xh, 1)]] + [u3.at[pl.ds(d, 1)] for d in (1, 2, 3)], u3s)
+    keep(u3s.at[0], o_up.at[:, columns(y, width)])
+    for d in (1, 2, 3):
+        copies.push(("u4", d), u3s.at[0], o_up.at[:, columns(y, width)], along_y[d - 1])
+    for d in (1, 2, 3):
+        copies.arrived(("a3", d), a3.at[d], along_x[3 - d])
+    add_up([a2s.at[pl.ds(xh, 1)]] + [a3.at[pl.ds(d, 1)] for d in (1, 2, 3)], a3s)
+    keep(a3s.at[0], o_att.at[:, columns(y, width)])
+    for d in (1, 2, 3):
+        copies.push(("a4", d), a3s.at[0], o_att.at[:, columns(y, width)], along_y[d - 1])
+    for d in (1, 2, 3):
+        copies.arrived(("m3", d), m3.at[d], along_z[3 - d])
+    add_up([m2s.at[pl.ds(z, 1)]] + [m3.at[pl.ds(d, 1)] for d in (1, 2, 3)], m3s)
+    spot = lambda s: columns((s % 2) * 4 + s // 2, piece)
+    keep(m3s.at[0], o_mix.at[:, spot(seq)])
+    for e in range(1, 8):
+        copies.push(("m4", e), m3s.at[0], o_mix.at[:, spot(seq)], peers[e - 1])
+    total = t1[0].astype(jnp.float32)
+    for e in range(1, 8):
+        copies.arrived(("t1", e), t1.at[e], peers[7 - e])
+        total = total + t1[e].astype(jnp.float32)
+    o_mod[...] = total
+    for d in (1, 2, 3):
+        from_y = step(y, -d)
+        copies.arrived(("d3", d), o_down.at[from_y], along_y[3 - d])
+        copies.arrived(("u4", d), o_up.at[:, columns(from_y, width)], along_y[3 - d])
+        copies.arrived(("a4", d), o_att.at[:, columns(from_y, width)], along_y[3 - d])
+    for e in range(1, 8):
+        source = (seq + 8 - e) % 8
+        copies.arrived(("cap", e), o_cap.at[source], peers[7 - e])
+        copies.arrived(("m4", e), o_mix.at[:, spot(source)], peers[7 - e])
+    for copy in waits[7:]:
+        copy.wait()
+    copies.finish()
+
+
+def scatter_grads(up, qkv, cq, mix, down, mod, cap):
+    width, side = up.shape[-1] // 4, mix.shape[-1] // 2
+    piece = side // 4
+    vmem = lambda *shape: pltpu.VMEM(shape, jnp.bfloat16)
+    count = 64
+    anywhere = pl.BlockSpec(memory_space=pl.ANY)
+    return pl.pallas_call(
+        scatter_kernel,
+        out_shape=(
+            jax.ShapeDtypeStruct((HD, 4 * width), jnp.bfloat16),
+            jax.ShapeDtypeStruct((HD, 4 * width), jnp.bfloat16),
+            jax.ShapeDtypeStruct((HD, 2 * side), jnp.bfloat16),
+            jax.ShapeDtypeStruct((4, HD, width), jnp.bfloat16),
+            jax.ShapeDtypeStruct(mod.shape, jnp.float32),
+            jax.ShapeDtypeStruct((8,) + cap.shape, jnp.bfloat16),
+        ),
+        in_specs=[anywhere] * 7,
+        out_specs=(anywhere,) * 4 + (pl.BlockSpec(memory_space=pltpu.VMEM), anywhere),
+        scratch_shapes=[
+            vmem(4, 4, 2, HD, width), vmem(4, 2, HD, width), vmem(4, 2, HD, width),
+            vmem(2, HD, width), vmem(4, HD, width), vmem(1, HD, width),
+            vmem(4, 2, HD, 4 * width), vmem(2, HD, 4 * width), vmem(4, 2, HD, width),
+            vmem(2, HD, width), vmem(4, HD, width), vmem(1, HD, width),
+            vmem(4, 4, HD, side), vmem(4, HD, side), vmem(4, 4, HD, piece),
+            vmem(4, HD, piece), vmem(4, HD, piece), vmem(1, HD, piece),
+            vmem(4, HD, width), vmem(1, HD, width), vmem(1, HD, width), vmem(1, HD, width),
+            vmem(8, *mod.shape),
+            pltpu.SemaphoreType.DMA((16,)),
+            pltpu.SemaphoreType.DMA((count,)),
+            pltpu.SemaphoreType.DMA((count,)),
+        ],
+        compiler_params=pltpu.CompilerParams(
+            collective_id=1, has_side_effects=True, vmem_limit_bytes=48 * 1024 * 1024
+        ),
+    )(up, qkv, cq, mix, down, mod, cap)
+
+
+def sibling_pairs():
+    return [(i, i + 1 - 2 * (i % 2)) for i in range(16)]
+
+
+def by_core(matrix):
+    core = lax.axis_index("fsdp") % 2
+    split = matrix.reshape((8, 2, -1) + matrix.shape[1:])
+    pick = lambda which: lax.dynamic_index_in_dim(split, which, 1, keepdims=False).reshape(
+        (-1,) + matrix.shape[1:]
+    )
+    return pick(core), pick(1 - core)
+
+
+def pair_grad(former, latter):
+    own, other = by_core(former.T)
+    theirs = project(other, latter).astype(jnp.bfloat16)
+    received = lax.ppermute(theirs, "fsdp", sibling_pairs())
+    return (project(own, latter) + received.astype(jnp.float32)).astype(jnp.bfloat16)
 
 
 def on_device(
@@ -131,41 +532,36 @@
     down_bias,
     cotangent,
 ):
-    (
-        full_table,
-        full_qkv,
-        full_qbias,
-        full_vbias,
-        full_proj,
-        full_pbias,
-        full_cquery,
-        full_cqbias,
-        full_ckv,
-        full_cvbias,
-        full_cproj,
-        full_cpbias,
-        full_up,
-        full_ubias,
-        full_down,
-        full_dbias,
-    ) = (
-        lax.all_gather(shift_table, "fsdp", axis=0, tiled=True),
-        lax.all_gather(qkv_weight, "fsdp", axis=0, tiled=True),
-        lax.all_gather(query_bias, "fsdp", axis=0, tiled=True),
-        lax.all_gather(value_bias, "fsdp", axis=0, tiled=True),
-        lax.all_gather(proj_weight, "fsdp", axis=0, tiled=True),
-        lax.all_gather(proj_bias, "fsdp", axis=0, tiled=True),
-        lax.all_gather(cross_query, "fsdp", axis=0, tiled=True),
-        lax.all_gather(cross_qbias, "fsdp", axis=0, tiled=True),
-        lax.all_gather(cross_kv, "fsdp", axis=0, tiled=True),
-        lax.all_gather(cross_vbias, "fsdp", axis=0, tiled=True),
-        lax.all_gather(cross_proj, "fsdp", axis=0, tiled=True),
-        lax.all_gather(cross_pbias, "fsdp", axis=0, tiled=True),
-        lax.all_gather(up_weight, "fsdp", axis=0, tiled=True),
-        lax.all_gather(up_bias, "fsdp", axis=0, tiled=True),
-        lax.all_gather(down_weight, "fsdp", axis=0, tiled=True),
-        lax.all_gather(down_bias, "fsdp", axis=0, tiled=True),
-    )
+    full_down = lax.all_gather(down_weight, "fsdp", axis=0, tiled=True)
+    small = jnp.concatenate(
+        [
+            shift_table.reshape(HD, 6),
+            query_bias.reshape(HD, 1),
+            value_bias.reshape(HD, 1),
+            proj_bias.reshape(HD, 1),
+            cross_qbias.reshape(HD, 1),
+            cross_vbias.reshape(HD, 1),
+            cross_pbias.reshape(HD, 1),
+            down_bias.reshape(HD, 1),
+            up_bias.reshape(HD, 4),
+        ],
+        axis=1,
+    )
+    small = jnp.pad(small, ((0, 0), (0, 128 - small.shape[1])))
+    full_up, full_qkv, full_cquery, full_small, full_ckv, full_pair = gather_weights(
+        up_weight,
+        qkv_weight,
+        cross_query,
+        small,
+        cross_kv,
+        jnp.concatenate([proj_weight, cross_proj], axis=1),
+    )
+    full_proj, full_cproj = jnp.split(full_pair, 2, axis=1)
+    full_table = full_small[:, :6].reshape(-1)
+    full_qbias, full_vbias, full_pbias, full_cqbias, full_cvbias, full_cpbias, full_dbias = (
+        full_small[:, 6 + i] for i in range(7)
+    )
+    full_ubias = full_small[:, 13:17].reshape(-1)
     latent_count, local_len, model_width = latents.shape
     inputs = latents.astype(jnp.float32)
     modulation = (full_table.astype(jnp.float32) + timestep.astype(jnp.float32)).reshape(
@@ -213,21 +609,23 @@
     down_bgrad = token_sum(grad_three)
     grad_act = project(grad_three, full_down.T)
     grad_hidden = gelu_pull(grad_act)[0].astype(jnp.bfloat16)
-    up_grad = weight_grad(normed_two, grad_hidden)
+    up_grad = pair_grad(normed_two[0], grad_hidden[0])
     up_bgrad = token_sum(grad_hidden)
     grad_pre_two = project(grad_hidden, full_up.T)
     grad_mid_two, grad_shift_two, grad_scale_two = pull_two(grad_pre_two)
     grad_after_two = grad_out + grad_mid_two
-    mlp_parts = reduce_bucket((up_grad, up_bgrad, down_grad, down_bgrad))
+    down_part = lax.psum_scatter(
+        down_grad.astype(jnp.bfloat16), "fsdp", scatter_dimension=0, tiled=True
+    )
     grad_branch_two = grad_after_two.astype(jnp.bfloat16)
-    cproj_grad = weight_grad(crossed, grad_branch_two)
+    cproj_grad = pair_grad(crossed[0], grad_branch_two[0])
     cproj_bgrad = token_sum(grad_branch_two)
     grad_crossed = project(grad_branch_two, full_cproj.T).astype(jnp.bfloat16)
     grad_cq, grad_ck, grad_cv = jax.vmap(attend_backward)(
         by_heads(cross_rows), text_keys, text_values, cross_logsum, by_heads(grad_crossed)
     )
     grad_cross_rows = grad_cq.reshape(latent_count, local_len, model_width).astype(jnp.bfloat16)
-    cquery_grad = weight_grad(middle, grad_cross_rows)
+    cquery_grad = pair_grad(middle[0], grad_cross_rows[0])
     cquery_bgrad = token_sum(grad_cross_rows)
     grad_after_one = grad_after_two + project(grad_cross_rows, full_cquery.T)
     text_partial = jnp.concatenate(
@@ -237,16 +635,27 @@
         ],
         axis=-1,
     )
+    text_piece = text_partial.shape[1] // 8
+    text_pieces = lax.all_to_all(
+        text_partial[0].astype(jnp.bfloat16).reshape(8, text_piece, -1), "seq", 0, 0
+    )
+    text_grad = jnp.sum(text_pieces.astype(jnp.float32), axis=0).astype(jnp.bfloat16)
+    caption_part = lax.dynamic_slice_in_dim(
+        caption[0], lax.axis_index("seq") * text_piece, text_piece, 0
+    )
+    ckv_grad = pair_grad(caption_part, text_grad)
+    cvalue_bgrad = jnp.sum(text_grad[:, model_width:].astype(jnp.float32), axis=0)
+    caption_piece = project(text_grad, full_ckv.T)
     grad_gate_one = jnp.sum(grad_after_one * branch_one, axis=1, keepdims=True)
     grad_branch_one = (gate_one * grad_after_one).astype(jnp.bfloat16)
-    proj_grad = weight_grad(tok_major, grad_branch_one)
+    proj_grad = pair_grad(tok_major[0], grad_branch_one[0])
     proj_bgrad = token_sum(grad_branch_one)
     grad_tok = project(grad_branch_one, full_proj.T).astype(jnp.bfloat16)
     grad_heads = lax.all_to_all(grad_tok, "seq", split_axis=2, concat_axis=1, tiled=True)
     grad_packed_heads = lax.map(self_backward, (head_major, logsum, grad_heads))
     grad_packed = lax.all_to_all(grad_packed_heads, "seq", split_axis=1, concat_axis=3, tiled=True)
     grad_flat = grad_packed.reshape(latent_count, local_len, 3 * model_width)
-    qkv_grad = weight_grad(normed_one, grad_flat)
+    qkv_grad = pair_grad(normed_one[0], grad_flat[0])
     qbias_grad = token_sum(grad_packed[:, :, 0])
     vbias_grad = token_sum(grad_packed[:, :, 2])
     grad_pre_one = project(grad_flat, full_qkv.T)
@@ -264,68 +673,66 @@
         axis=1,
     )
     grad_mod = grad_mod.reshape(latent_count, 6 * model_width)
-    table_part = jnp.sum(grad_mod, axis=0)
-    text_sum, mod_sum = (
-        lax.psum_scatter(
-            text_partial.astype(jnp.bfloat16), "seq", scatter_dimension=1, tiled=True
-        ).astype(jnp.float32),
-        lax.psum_scatter(
-            grad_mod.astype(jnp.bfloat16), "seq", scatter_dimension=1, tiled=True
-        ).astype(jnp.float32),
-    )
-    text_grad = text_sum.astype(jnp.bfloat16)
-    text_piece = text_grad.shape[1]
-    caption_part = lax.dynamic_slice_in_dim(
-        caption, lax.axis_index("seq") * text_piece, text_piece, 1
-    )
-    ckv_grad = weight_grad(caption_part, text_grad)
-    cvalue_bgrad = token_sum(text_grad[..., model_width:])
-    caption_piece = project(text_grad, full_ckv.T)
-    caption_grad, timestep_grad = (
-        lax.all_gather(caption_piece.astype(jnp.bfloat16), "seq", axis=1, tiled=True).astype(
-            caption_piece.dtype
-        ),
-        lax.all_gather(mod_sum.astype(jnp.bfloat16), "seq", axis=1, tiled=True).astype(
-            mod_sum.dtype
-        ),
-    )
-    rest = reduce_bucket(
-        (
-            table_part,
-            qkv_grad,
-            qbias_grad,
-            vbias_grad,
+    small_grad = jnp.concatenate(
+        [
+            grad_mod.reshape(-1, 6),
+            qbias_grad.reshape(-1, 1),
+            vbias_grad.reshape(-1, 1),
+            proj_bgrad.reshape(-1, 1),
+            cquery_bgrad.reshape(-1, 1),
+            cvalue_bgrad.reshape(-1, 1),
+            cproj_bgrad.reshape(-1, 1),
+            down_bgrad.reshape(-1, 1),
+            up_bgrad.reshape(-1, 4),
+        ],
+        axis=1,
+    )
+    small_own, small_other = by_core(small_grad)
+    small_sum = small_own + lax.ppermute(
+        small_other.astype(jnp.bfloat16), "fsdp", sibling_pairs()
+    ).astype(jnp.float32)
+    mix = jnp.concatenate(
+        [
             proj_grad,
-            proj_bgrad,
-            cquery_grad,
-            cquery_bgrad,
             ckv_grad,
-            cvalue_bgrad,
             cproj_grad,
-            cproj_bgrad,
-        )
-    )
+            jnp.pad(small_sum.astype(jnp.bfloat16), ((0, 0), (0, 512 - small_sum.shape[1]))),
+        ],
+        axis=1,
+    )
+    blocks = lambda grad: grad.reshape(4, 2, HD, -1)
+    sum_up, sum_att, sum_mix, sum_down, sum_mod, caption_all = scatter_grads(
+        blocks(up_grad),
+        blocks(qkv_grad),
+        blocks(cquery_grad),
+        blocks(mix),
+        down_part.reshape(4, HD, model_width),
+        jnp.pad(grad_mod.astype(jnp.bfloat16).reshape(-1, 128), ((0, 10), (0, 0))),
+        jnp.pad(caption_piece.astype(jnp.bfloat16), ((0, 1), (0, 0))),
+    )
+    wide = lambda part: part.astype(jnp.float32)
+    sum_small = wide(sum_mix[:, 4 * model_width : 4 * model_width + 17])
     return (
         block_out,
         grad_latents,
-        timestep_grad,
-        caption_grad,
-        rest[0],
-        rest[1],
-        rest[2],
-        rest[3],
-        rest[4],
-        rest[5],
-        rest[6],
-        rest[7],
-        rest[8],
-        rest[9],
-        rest[10],
-        rest[11],
-        mlp_parts[0],
-        mlp_parts[1],
-        mlp_parts[2],
-        mlp_parts[3],
+        sum_mod[:54].reshape(1, -1),
+        wide(caption_all[:, :text_piece].reshape(1, -1, model_width)),
+        sum_small[:, :6].reshape(-1),
+        wide(sum_att[:, : 3 * model_width]),
+        sum_small[:, 6],
+        sum_small[:, 7],
+        wide(sum_mix[:, :model_width]),
+        sum_small[:, 8],
+        wide(sum_att[:, 3 * model_width :]),
+        sum_small[:, 9],
+        wide(sum_mix[:, model_width : 3 * model_width]),
+        sum_small[:, 10],
+        wide(sum_mix[:, 3 * model_width : 4 * model_width]),
+        sum_small[:, 11],
+        wide(sum_up),
+        sum_small[:, 13:17].reshape(-1),
+        wide(sum_down.reshape(4 * HD, model_width)),
+        sum_small[:, 12],
     )
 
 

time: 1450 us -> 624 us (0.43)
  waiting for transfers between devices: 971 us -> 31.5 us
  Pallas kernels: 0 us -> 308 us
  blocking collectives: 218 us -> 0 us
  local copies, waits for them, and re-layouts: 54.1 us -> 81.8 us
    reduce_scatter x3 -> x1, waiting for transfers between devices: 321 us -> 0.01 us  [on_device(): lax.psum_scatter(down_grad.astype(jnp.bfloat16), 'fsdp', scatter_dimensio...]
    pallas_call x0 -> x2, Pallas kernels: none -> 308 us  [the longest x1 172 us: gather_weights(): pl.pallas_call(gather_kernel, out_shape=tuple((jax.ShapeDtypeStruct((4, 2...]
    all_gather x7 -> x1, waiting for transfers between devices: 300 us -> 0.02 us  [on_device(): full_down = lax.all_gather(down_weight, 'fsdp', axis=0, tiled=True)]
    unnamed x23 -> x2, waiting for transfers between devices: 298 us -> 0.7 us
    unnamed x3 -> x0, blocking collectives: 173 us -> none
    psum x1 -> x0, waiting for transfers between devices: 36.9 us -> none  [reduce_bucket(): lax.psum(for_sending(owner_part), 'seq')]
    all_gather x1 -> x0, blocking collectives: 31.3 us -> none  [on_device(): lax.all_gather(caption_piece.astype(jnp.bfloat16), 'seq', axis=1, tiled=T...]
    dot_general x14 -> x26, matrix products: 62.4 us -> 91 us  [project(): return jnp.dot(former, latter, preferred_element_type=jnp.float32)]
  transfers between devices with their start and end apart: 20 -> 14, of which waited for: 16 -> 5; matrix products, arithmetic and copies ran while one was open for 11% -> 36% of each run, Pallas kernels for 0% -> 28%
where the time goes in v1:
time: 624 us; the launch traced here: 616 us
  Pallas kernels  308 us (49%)
  matrix products  118 us (19%)
  local copies, waits for them, and re-layouts  81.8 us (13%)
  other arithmetic  37.5 us (6%)
  waiting for transfers between devices  31.5 us (5%)
  starting transfers between devices  22.9 us (4%)
  between operations  15.8 us (3%)
    pallas_call x1, Pallas kernels, gather_weights(): pl.pallas_call(gather_kernel, out_shape=tuple((jax.ShapeDtypeStruct((4, 2...  172 us
    pallas_call x1, Pallas kernels, scatter_grads(): pl.pallas_call(scatter_kernel, out_shape=(jax.ShapeDtypeStruct((HD, 4 * w...  136 us
    dot_general x26, matrix products, project(): return jnp.dot(former, latter, preferred_element_type=jnp.float32)  91 us
    unnamed x170, local copies, waits for them, and re-layouts  20.9 us
    all_to_all x1, waiting for transfers between devices, on_device(): lax.all_to_all(packed, 'seq', split_axis=3, concat_axis=1, tiled=True)  12.8 us
  transfers between devices with their start and end apart: 14, of which 5 were waited for; matrix products, arithmetic and copies ran while one was open for 36% of the time, Pallas kernels for 28%

profile of v1, /device:TPU:0, one launch (start us, length us, event | category | flops | bytes accessed | tf_op | source)
XLA Modules:
  0.0 615.8 jit_solution(14020545927656063733)
XLA Ops:
  15.7 1.7 pad_maximum_fusion.2.pair
  17.4 172.2 %shard_map.347 = (bf16[4,2,2,72,4608]{4,3,2,1,0:T(8,128)(2,1)}, bf16[4,2,2,72,3456]{4,3,2,1,0:T(8,128)(2,1)}, bf16[4,2,2,72,1152]{4,3,2,1,0:T(8,128)(2,1)}, bf16...) custom-call(bf16[72,4608]{1,0:T(8,128)(2,1)} %up.1, ...), custom_call_target="tpu_custom_call" | custom-call | tf_op jit(solution)/shard_map/pallas_call | solution.py:291
  191.2 2.1 slice_reduce_fusion.2
  193.9 4.7 fusion.4
  199.7 6.3 %copy.220 = bf16[1,128,3,1152]{1,2,0,3:T(4,128)(2,1)} copy(bf16[1,128,3,1152]{1,3,2,0:T(8,128)(2,1)S(1)} %bitcast.336) | data formatting | bytes 1769472 | tf_op jit(solution)/shard_map/reshape | solution.py:578
  206.0 3.8 all-to-all-start
  209.8 3.5 fusion.9
  215.0 12.8 %all-to-all-done = bf16[1,128,3,1152]{1,2,0,3:T(4,128)(2,1)S(1)} async-done(((bf16[1,128,3,1152]{1,2,0,3:T(4,128)(2,1)}), bf16[1,128,3,1152]{1,2,0,3:T(4,128)(2,1)S(1)}, u32[]{:S(2)}, u32[]{:S(2)}) %all-to-all-start) | async-done | bytes 884768 | tf_op jit(solution)/shard_map/all_to_all | solution.py:579
  231.4 1.9 copy-done.3
  233.3 1.8 fusion.33
  236.5 4.0 reduce.74
  240.5 1.5 reshape.907
  242.0 4.1 all-to-all-start.1
  248.7 5.3 all-to-all-done.1
  254.0 2.9 reshape.908
  257.6 2.5 fusion.57
  263.8 2.5 fusion.98
  266.5 5.8 convolution_add_fusion
  272.4 1.5 copy-done.6
  273.8 5.8 convolution_convert_fusion
  279.7 8.7 %convert_reduce_fusion = (f32[4608]{0:T(1024)S(1)}, bf16[128,4608]{1,0:T(8,128)(2,1)S(1)}) fusion(f32[128,4608]{1,0:T(8,128)} %copy-done.6, bf16[4608,1152]{1,0:T(8,128)(2,1)} %all-gather.2.cloned.1.call-done, bf16[1,128,1152]{2,1,0:T(8,128)(2,1)} %param.39, f32[1152]{0:T(1024)S(1)} %get-tuple-element.94), kind=kOutput, calls=%fused_computation.52 | convolution fusion | flops 1372368384 | bytes 14473728 | tf_op jit(solution)/shard_map/dot_general | solution.py:36
  288.5 9.1 %fusion.99 = (f32[1152]{0:T(1024)S(1)}, f32[128,1152]{1,0:T(8,128)S(1)}) fusion(bf16[128,4608]{1,0:T(8,128)(2,1)S(1)} %get-tuple-element.151, bf16[1152,4608]{1,0:T(8,128)(2,1)} %bitcast.306), kind=kOutput, calls=%fused_computation.228 | convolution fusion | flops 1359100800 | bytes 12390912 | tf_op jit(solution)/shard_map/dot_general | solution.py:36
  299.8 3.0 convert_reduce_fusion.5
  304.1 1.8 copy.240
  307.9 3.4 convolution_convert_fusion.8
  313.7 2.2 copy.244
  315.9 2.4 concatenate.76
  318.3 1.6 multiply_reduce_fusion.2
  321.3 1.8 convert_reduce_fusion.8
  326.3 1.8 concatenate.75
  328.1 2.7 fusion.21
  331.5 6.8 %reduce.75 = bf16[1152,128]{1,0:T(8,128)(2,1)S(1)} reduce(bf16[1152,1,128]{2,1,0:T(2,128)(2,1)S(1)} %bitcast.350, bf16[]{:T(256)} %broadcast.327), dimensions={1}, to_apply=%bitcast.234.reduce_sub_computation | reduce | bytes 589826
  339.0 3.4 all-to-all-start.2
  343.9 1.6 convolution_convert_fusion.4
  345.5 1.7 constant_dynamic-slice_fusion.9
  347.2 1.9 pad_maximum_fusion.1
  349.1 4.7 all-to-all-done.2
  353.8 4.2 all-to-all-start.4
  358.5 5.1 fusion.28
  363.6 4.7 multiply_reduce_fusion
  368.4 2.5 multiply_convert_fusion
  370.9 1.4 fusion.32
  373.3 2.5 copy.237
  375.8 4.8 reshape.911
  380.7 5.6 all-to-all-start.3
  386.2 3.9 convolution_convert_fusion.1
  392.0 2.4 convolution_convert_fusion.3
  395.0 3.0 all-to-all-done.3
  397.9 3.1 reshape.912
  402.4 6.0 fusion.48
  414.6 3.1 convolution_convert_fusion.2
  419.8 5.0 collective-permute-done.6
  425.6 1.6 convolution_convert_fusion.6
  427.4 4.0 convolution_convert_fusion.9
  434.1 1.5 constant_dynamic-slice_fusion
  435.6 1.8 copy.255
  438.4 1.8 add_convert_fusion.3
  440.3 1.8 add_convert_fusion.4
  442.1 1.8 add_convert_fusion.5
  444.0 2.6 add_convert_fusion.2
  446.6 3.2 fusion.2
  449.9 5.3 add_convert_fusion.1
  455.2 6.4 %add_convert_fusion = bf16[576,4608]{1,0:T(8,128)(2,1)} fusion(bf16[576,4608]{1,0:T(8,128)(2,1)} %collective-permute-done, bf16[576,128]{1,0:T(8,128)(2,1)S(1)} %bitcast.366, bf16[128,4608]{1,0:T(8,128)(2,1)S(1)} %copy-done.11), kind=kOutput, calls=%fused_computation.3 | convolution fusion | flops 687439872 | bytes 11943936 | tf_op jit(solution)/shard_map/dot_general | solution.py:36
  462.7 136.2 %shard_map.348 = (bf16[72,4608]{1,0:T(8,128)(2,1)S(1)}, bf16[72,4608]{1,0:T(8,128)(2,1)S(1)}, bf16[72,5120]{1,0:T(8,128)(2,1)S(1)}, bf16[4,72,1152]{2,1,0:T(8,12...) custom-call(bf16[4,2,72,4608]{3,2,1,0:T(8,128)(2,1)} %bitcast.307, ...), custom_call_target="tpu_custom_call" | custom-call | tf_op jit(solution)/shard_map/pallas_call | solution.py:462
  (307 shorter events, 69.6 us)
Async XLA Ops:
  7.2 202.6 %copy-start = (bf16[1,120,1152]{2,1,0:T(8,128)(2,1)S(1)}, bf16[1,120,1152]{2,1,0:T(8,128)(2,1)}, u32[]{:S(2)}) copy-start(bf16[1,120,1152]{2,1,0:T(8,128)(2,1)} %param.22) | copy-start | bytes 829444
  7.2 183.8 %copy-start.62 = (bf16[1,6912]{1,0:T(2,128)(2,1)S(1)}, bf16[1,6912]{1,0:T(2,128)(2,1)}, u32[]{:S(2)}) copy-start(bf16[1,6912]{1,0:T(2,128)(2,1)} %param.21) | copy-start | bytes 41476
  7.2 272.5 %all-gather.2.cloned.1.call-start = ((), (), s32[]{:S(2)}) async-start(), calls=%async_computation.6 | async-start | bytes 11280384 | tf_op jit(solution)/shard_map/all_gather | solution.py:535
  17.4 175.9 %copy-start.5 = (bf16[1,128,1152]{2,1,0:T(8,128)(2,1)S(1)}, bf16[1,128,1152]{2,1,0:T(8,128)(2,1)}, u32[]{:S(2)}) copy-start(bf16[1,128,1152]{2,1,0:T(8,128)(2,1)} %param.20) | copy-start | bytes 884740
  193.4 5.3 copy-start.55
  193.5 5.2 copy-start.68
  193.7 4.9 copy-start.70
  193.8 4.9 copy-start.63
  206.0 21.8 %all-to-all-start = ((bf16[1,128,3,1152]{1,2,0,3:T(4,128)(2,1)}), bf16[1,128,3,1152]{1,2,0,3:T(4,128)(2,1)S(1)}, u32[]{:S(2)}, u32[]{:S(2)}) async-start(bf16[1,128,3,1152]{1,2,0,3:T(4,128)(2,1)} %copy.220), calls=%async_computation | async-start | bytes 2359296 | tf_op jit(solution)/shard_map/all_to_all | solution.py:579
  209.8 4.2 copy-start.4
  230.0 3.3 copy-start.3
  235.1 13.0 %copy-start.41 = (bf16[1,120,1152]{2,1,0:T(8,128)(2,1)S(1)}, bf16[1,120,1152]{2,1,0:T(8,128)(2,1)}, u32[]{:S(2)}) copy-start(bf16[1,120,1152]{2,1,0:T(8,128)(2,1)} %get-tuple-element.118) | copy-start | bytes 829444
  242.0 11.9 %all-to-all-start.1 = ((bf16[8,2,9216]{2,1,0:T(2,128)(2,1)}), bf16[8,2,9216]{2,1,0:T(2,128)(2,1)}, u32[]{:S(2)}, u32[]{:S(2)}) async-start(bf16[8,2,9216]{2,1,0:T(2,128)(2,1)} %reshape.907), calls=%async_computation.1 | async-start | bytes 589824 | tf_op jit(solution)/shard_map/all_to_all | solution.py:581
  246.1 215.5 %reduce-scatter.2.cloned.1.call-start = ((), (), s32[]{:S(2)}) async-start(), calls=%async_computation.7 | async-start | bytes 11280384 | tf_op jit(solution)/shard_map/reduce_scatter | solution.py:617
  248.1 13.8 %copy-start.25 = (bf16[1,120,1152]{1,2,0:T(8,128)(2,1)}, bf16[1,120,1152]{1,2,0:T(8,128)(2,1)S(1)}, u32[]{:S(2)}) copy-start(bf16[1,120,1152]{1,2,0:T(8,128)(2,1)S(1)} %copy.229) | copy-start | bytes 829444
  248.4 14.2 %copy-start.36 = (bf16[1,120,1152]{1,2,0:T(8,128)(2,1)}, bf16[1,120,1152]{1,2,0:T(8,128)(2,1)S(1)}, u32[]{:S(2)}) copy-start(bf16[1,120,1152]{1,2,0:T(8,128)(2,1)S(1)} %copy.227) | copy-start | bytes 829444
  260.2 3.6 copy-start.12
  266.5 7.3 %copy-start.29 = (bf16[1,128,1152]{2,1,0:T(8,128)(2,1)S(1)}, bf16[1,128,1152]{2,1,0:T(8,128)(2,1)}, u32[]{:S(2)}) copy-start(bf16[1,128,1152]{2,1,0:T(8,128)(2,1)} %param.39) | copy-start | bytes 884740
  288.5 97.8 %copy-start.10 = (bf16[128,4608]{1,0:T(8,128)(2,1)}, bf16[128,4608]{1,0:T(8,128)(2,1)S(1)}, u32[]{:S(2)}) copy-start(bf16[128,4608]{1,0:T(8,128)(2,1)S(1)} %get-tuple-element.151) | copy-start | bytes 3538948
  288.5 11.3 %copy-start.7 = (f32[128,4608]{1,0:T(8,128)S(1)}, f32[128,4608]{1,0:T(8,128)}, u32[]{:S(2)}) copy-start(f32[128,4608]{1,0:T(8,128)} %copy-done.6) | copy-start | bytes 7077892
  288.5 11.3 %copy-start.30 = (bf16[1,128,1152]{2,1,0:T(8,128)(2,1)S(1)}, bf16[1,128,1152]{2,1,0:T(8,128)(2,1)}, u32[]{:S(2)}) copy-start(bf16[1,128,1152]{2,1,0:T(8,128)(2,1)} %param.39) | copy-start | bytes 884740
  288.5 11.3 %copy-start.72 = (bf16[4608,1152]{1,0:T(8,128)(2,1)S(1)}, bf16[4608,1152]{1,0:T(8,128)(2,1)}, u32[]{:S(2)}) copy-start(bf16[4608,1152]{1,0:T(8,128)(2,1)} %all-gather.2.cloned.1.call-done) | copy-start | bytes 31850500
  307.2 6.4 %copy-start.22 = (bf16[1,128,1152]{2,1,0:T(8,128)(2,1)}, bf16[1,128,1152]{2,1,0:T(8,128)(2,1)S(1)}, u32[]{:S(2)}) copy-start(bf16[1,128,1152]{2,1,0:T(8,128)(2,1)S(1)} %get-tuple-element.101) | copy-start | bytes 884740
  320.1 3.6 copy-start.28
  323.1 7.7 %copy-start.20 = (bf16[1,128,1152]{2,1,0:T(8,128)(2,1)}, bf16[1,128,1152]{2,1,0:T(8,128)(2,1)S(1)}, u32[]{:S(2)}) copy-start(bf16[1,128,1152]{2,1,0:T(8,128)(2,1)S(1)} %get-tuple-element.103) | copy-start | bytes 884740
  330.8 13.2 %copy-start.23 = (bf16[1,128,1152]{2,1,0:T(8,128)(2,1)S(1)}, bf16[1,128,1152]{2,1,0:T(8,128)(2,1)}, u32[]{:S(2)}) copy-start(bf16[1,128,1152]{2,1,0:T(8,128)(2,1)} %copy-done.22) | copy-start | bytes 884740
  339.0 14.7 %all-to-all-start.2 = ((bf16[8,2,9216]{2,1,0:T(2,128)(2,1)}), bf16[8,2,9216]{2,1,0:T(2,128)(2,1)S(1)}, u32[]{:S(2)}, u32[]{:S(2)}) async-start(bf16[8,2,9216]{2,1,0:T(2,128)(2,1)} %reshape.909), calls=%async_computation.2 | async-start | bytes 589824 | tf_op jit(solution)/shard_map/all_to_all | solution.py:654
  345.5 81.7 %collective-permute-start.5 = (bf16[576,1152]{1,0:T(8,128)(2,1)}, bf16[576,1152]{1,0:T(8,128)(2,1)}, u32[]{:S(2)}, u32[]{:S(2)}) collective-permute-start(bf16[576,1152]{1,0:T(8,128)(2,1)} %convolution_convert_fusion.4), channel_id=1, source_target_pairs={{0,1},{1,0},{2,3},{3,2},{4,5},{5,4},{6,7},{7,6},{8,9},{9,8},{10,11... | collective-permute-start | bytes 3981320 | tf_op jit(solution)/shard_map/ppermute | solution.py:509
  353.8 26.9 %all-to-all-start.4 = ((bf16[8,15,2304]{2,1,0:T(8,128)(2,1)}), bf16[8,15,2304]{2,1,0:T(8,128)(2,1)}, u32[]{:S(2)}, u32[]{:S(2)}) async-start(bf16[8,15,2304]{2,1,0:T(8,128)(2,1)} %pad_maximum_fusion.1), calls=%async_computation.4 | async-start | bytes 1179648 | tf_op jit(solution)/shard_map/all_to_all | solution.py:639
  358.5 5.1 copy-start.39
  358.5 9.8 %slice-start = ((s8[8388608]{0:T(1024)(128)(4,1)}), s8[4194304]{0:T(1024)(128)(4,1)S(1)}, s32[]{:S(2)}) async-start(s8[8388608]{0:T(1024)(128)(4,1)} %bitcast.301), calls=%async_computation.8 | async-start | bytes 8388608
  363.6 4.7 slice-start.1
  380.7 17.3 %all-to-all-start.3 = ((bf16[8,2,27648]{2,1,0:T(2,128)(2,1)}), bf16[8,2,27648]{2,1,0:T(2,128)(2,1)S(1)}, u32[]{:S(2)}, u32[]{:S(2)}) async-start(bf16[8,2,27648]{2,1,0:T(2,128)(2,1)} %reshape.911), calls=%async_computation.3 | async-start | bytes 1769472 | tf_op jit(solution)/shard_map/all_to_all | solution.py:656
  390.1 65.1 %collective-permute-start = (bf16[576,4608]{1,0:T(8,128)(2,1)}, bf16[576,4608]{1,0:T(8,128)(2,1)}, u32[]{:S(2)}, u32[]{:S(2)}) collective-permute-start(bf16[576,4608]{1,0:T(8,128)(2,1)} %convolution_convert_fusion.1), channel_id=1, source_target_pairs={{0,1},{1,0},{2,3},{3,2},{4,5},{5,4},{6,7},{7,6},{8,9},{9,8},{10,11... | collective-permute-start | bytes 15925256 | tf_op jit(solution)/shard_map/ppermute | solution.py:509
  391.3 9.7 %copy-start.34 = (bf16[15,2304]{1,0:T(8,128)(2,1)}, bf16[15,2304]{1,0:T(8,128)(2,1)S(1)}, u32[]{:S(2)}) copy-start(bf16[15,2304]{1,0:T(8,128)(2,1)S(1)} %reduce_sum.276) | copy-start | bytes 207364
  394.5 7.8 %copy-start.50 = (f32[1152]{0:T(1024)S(1)}, f32[1152]{0:T(1024)}, u32[]{:S(2)}) copy-start(f32[1152]{0:T(1024)} %copy-done.49) | copy-start | bytes 13828
  394.5 7.8 %copy-start.69 = (f32[128]{0:T(128)S(1)}, f32[128]{0:T(128)}, u32[]{:S(2)}) copy-start(f32[128]{0:T(128)} %copy-done.68) | copy-start | bytes 1540
  394.5 49.5 %collective-permute-start.4 = (bf16[576,2304]{1,0:T(8,128)(2,1)}, bf16[576,2304]{1,0:T(8,128)(2,1)}, u32[]{:S(2)}, u32[]{:S(2)}) collective-permute-start(bf16[576,2304]{1,0:T(8,128)(2,1)} %convolution_convert_fusion.3), channel_id=1, source_target_pairs={{0,1},{1,0},{2,3},{3,2},{4,5},{5,4},{6,7},{7,6},{8,9},{9,8},{10,11... | collective-permute-start | bytes 7962632 | tf_op jit(solution)/shard_map/ppermute | solution.py:509
  402.3 6.1 copy-start.71
  402.3 6.1 copy-start.64
  402.3 7.1 %copy-start.13 = (f32[128,1152]{1,0:T(8,128)S(1)}, f32[128,1152]{1,0:T(8,128)}, u32[]{:S(2)}) copy-start(f32[128,1152]{1,0:T(8,128)} %copy-done.12) | copy-start | bytes 1769476
  402.3 7.1 %copy-start.33 = (f32[1,128,1152]{2,1,0:T(8,128)S(1)}, f32[1,128,1152]{2,1,0:T(8,128)}, u32[]{:S(2)}) copy-start(f32[1,128,1152]{2,1,0:T(8,128)} %get-tuple-element.141) | copy-start | bytes 1769476
  402.4 7.0 %copy-start.56 = (f32[1152]{0:T(1024)S(1)}, f32[1152]{0:T(1024)}, u32[]{:S(2)}) copy-start(f32[1152]{0:T(1024)} %copy-done.55) | copy-start | bytes 13828
  408.4 3.9 copy-start.65
  408.4 3.9 copy-start.66
  408.4 3.9 copy-start.67
  409.4 4.4 copy-start.37
  414.6 4.7 copy-start.21
  414.6 4.7 copy-start.44
  414.6 10.8 %copy-start.54 = (bf16[8,72,15]{1,0,2:T(8,128)(2,1)S(1)}, bf16[8,72,15]{1,0,2:T(8,128)(2,1)}, u32[]{:S(2)}) copy-start(bf16[8,72,15]{1,0,2:T(8,128)(2,1)} %get-tuple-element.86) | copy-start | bytes 51844
  414.6 10.9 %copy-start.15 = (bf16[16,72,128]{2,1,0:T(8,128)(2,1)S(1)}, bf16[16,72,128]{2,1,0:T(8,128)(2,1)}, u32[]{:S(2)}) copy-start(bf16[16,72,128]{2,1,0:T(8,128)(2,1)} %copy-done.14) | copy-start | bytes 884740
  417.7 9.6 %copy-start.35 = (bf16[15,2304]{1,0:T(8,128)(2,1)S(1)}, bf16[15,2304]{1,0:T(8,128)(2,1)}, u32[]{:S(2)}) copy-start(bf16[15,2304]{1,0:T(8,128)(2,1)} %copy-done.34) | copy-start | bytes 207364
  417.7 32.2 %collective-permute-start.1 = (bf16[576,3456]{1,0:T(8,128)(2,1)}, bf16[576,3456]{1,0:T(8,128)(2,1)}, u32[]{:S(2)}, u32[]{:S(2)}) collective-permute-start(bf16[576,3456]{1,0:T(8,128)(2,1)} %convolution_convert_fusion.2), channel_id=1, source_target_pairs={{0,1},{1,0},{2,3},{3,2},{4,5},{5,4},{6,7},{7,6},{8,9},{9,8},{10,11... | collective-permute-start | bytes 11943944 | tf_op jit(solution)/shard_map/ppermute | solution.py:509
  418.7 6.1 collective-permute-start.6
  424.8 15.5 %collective-permute-start.3 = (bf16[576,1152]{1,0:T(8,128)(2,1)S(1)}, bf16[576,1152]{1,0:T(8,128)(2,1)}, u32[]{:S(2)}, u32[]{:S(2)}) collective-permute-start(bf16[576,1152]{1,0:T(8,128)(2,1)S(1)} %convolution_convert_fusion.5), channel_id=1, source_target_pairs={{0,1},{1,0},{2,3},{3,2},{4,5},{5,4},{6,7},{7,6},{8,9},{9,8},{10,11... | collective-permute-start | bytes 3981320 | tf_op jit(solution)/shard_map/ppermute | solution.py:509
  427.1 4.3 copy-start.48
  427.1 11.2 %copy-start.24 = (bf16[1,128,1152]{2,1,0:T(8,128)(2,1)S(1)}, bf16[1,128,1152]{2,1,0:T(8,128)(2,1)}, u32[]{:S(2)}) copy-start(bf16[1,128,1152]{2,1,0:T(8,128)(2,1)} %copy-done.22) | copy-start | bytes 884740
  427.1 11.3 %copy-start.43 = (bf16[8,1,72,128]{3,2,1,0:T(8,128)(2,1)S(1)}, bf16[8,1,72,128]{3,2,1,0:T(8,128)(2,1)}, u32[]{:S(2)}) copy-start(bf16[8,1,72,128]{3,2,1,0:T(8,128)(2,1)} %get-tuple-element.122) | copy-start | bytes 442372
  427.1 15.0 %collective-permute-start.2 = (bf16[576,1152]{1,0:T(8,128)(2,1)}, bf16[576,1152]{1,0:T(8,128)(2,1)}, u32[]{:S(2)}, u32[]{:S(2)}) collective-permute-start(bf16[576,1152]{1,0:T(8,128)(2,1)} %convolution_convert_fusion.6), channel_id=1, source_target_pairs={{0,1},{1,0},{2,3},{3,2},{4,5},{5,4},{6,7},{7,6},{8,9},{9,8},{10,11... | collective-permute-start | bytes 3981320 | tf_op jit(solution)/shard_map/ppermute | solution.py:509
  431.3 8.9 %copy-start.42 = (bf16[8,1,72,128]{3,2,1,0:T(8,128)(2,1)S(1)}, bf16[8,1,72,128]{3,2,1,0:T(8,128)(2,1)}, u32[]{:S(2)}) copy-start(bf16[8,1,72,128]{3,2,1,0:T(8,128)(2,1)} %get-tuple-element.153) | copy-start | bytes 442372
  438.4 3.7 copy-start.45
  449.9 5.3 copy-start.11
  449.9 5.3 copy-start.40
  605.4 3.3 copy-start.1
  (25 other events, 55.2 us)
Sparse Core Ops, SparseCore 0:
  10.5 133.1 all-gather.1
  279.8 117.6 reduce-scatter.1

commit v2 on v0

v2 whole, which is shorter than its diff:
```python
import functools

import jax
import jax.numpy as jnp
from jax import lax
from jax.experimental import pallas as pl
from jax.experimental.pallas import tpu as pltpu
from jax.sharding import PartitionSpec as P

HD = 72
MESH = pl.DeviceIdType.MESH


epsilon = 1e-06


def for_sending(array):

    def short(part):
        return part.astype(jnp.bfloat16) if part.dtype == jnp.float32 else part

    return jax.tree.map(short, array)


def normalize(values):
    centre = values - jnp.mean(values, axis=-1, keepdims=True)
    spread = jnp.mean(centre * centre, axis=-1, keepdims=True)
    return centre * lax.rsqrt(spread + epsilon)


def modulate(values, shift, scale):
    return normalize(values) * (1.0 + scale) + shift


def project(former, latter):
    return jnp.dot(former, latter, preferred_element_type=jnp.float32)


def weight_grad(former, latter):
    return jnp.einsum("bli,blo->io", former, latter, preferred_element_type=jnp.float32)


def token_sum(values):
    return jnp.sum(values.astype(jnp.float32), axis=(0, 1))


def by_heads(matrix):
    return matrix.reshape(matrix.shape[:-1] + (matrix.shape[-1] // HD, HD))


def attend_forward(queries, key_rows, values):
    factor = HD ** (-0.5)
    scores = (
        jnp.einsum("qhd,khd->hqk", queries, key_rows, preferred_element_type=jnp.float32) * factor
    )
    largest = jnp.max(scores, axis=-1, keepdims=True)
    exponent = jnp.exp(scores - largest)
    partition = jnp.sum(exponent, axis=-1, keepdims=True)
    weights = (exponent / partition).astype(jnp.bfloat16)
    output = jnp.einsum("hqk,khd->qhd", weights, values, preferred_element_type=jnp.float32)
    return (output.astype(jnp.bfloat16), largest + jnp.log(partition))


def attend_backward(queries, key_rows, values, logsum, grad_out):
    factor = HD ** (-0.5)
    scores = (
        jnp.einsum("qhd,khd->hqk", queries, key_rows, preferred_element_type=jnp.float32) * factor
    )
    weights = jnp.exp(scores - logsum)
    grad_weights = jnp.einsum("qhd,khd->hqk", grad_out, values, preferred_element_type=jnp.float32)
    inner = jnp.sum(weights * grad_weights, axis=-1, keepdims=True)
    grad_scores = (weights * (grad_weights - inner)).astype(jnp.bfloat16)
    grad_q = (
        jnp.einsum("hqk,khd->qhd", grad_scores, key_rows, preferred_element_type=jnp.float32)
        * factor
    )
    grad_k = (
        jnp.einsum("hqk,qhd->khd", grad_scores, queries, preferred_element_type=jnp.float32)
        * factor
    )
    grad_v = jnp.einsum(
        "hqk,qhd->khd", weights.astype(jnp.bfloat16), grad_out, preferred_element_type=jnp.float32
    )
    return (grad_q, grad_k, grad_v)


def place():
    seq, fsdp = lax.axis_index("seq"), lax.axis_index("fsdp")
    y, x_lo = seq // 2, seq % 2
    z, rest = fsdp // 4, fsdp % 4
    x_hi, core = rest // 2, rest % 2
    return x_hi * 2 + x_lo, y, z, core


def device(x, y, z, core):
    return (y * 2 + x % 2, z * 4 + (x // 2) * 2 + core)


def step(value, by):
    return (value + by + 4) % 4


class Copies:
    def __init__(self, send, recv):
        self.send, self.recv, self.index, self.started = send, recv, {}, []

    def number(self, key):
        return self.index.setdefault(key, len(self.index))

    def push(self, key, src, dst, target):
        at = self.number(key)
        copy = pltpu.make_async_remote_copy(
            src_ref=src,
            dst_ref=dst,
            send_sem=self.send.at[at],
            recv_sem=self.recv.at[at],
            device_id=target,
            device_id_type=MESH,
        )
        copy.start()
        self.started.append(copy)

    def arrived(self, key, dst, source):
        at = self.number(key)
        pltpu.make_async_remote_copy(
            src_ref=dst,
            dst_ref=dst,
            send_sem=self.send.at[at],
            recv_sem=self.recv.at[at],
            device_id=source,
            device_id_type=MESH,
        ).wait_recv()

    def finish(self):
        for copy in self.started:
            copy.wait_send()


def greet(others):
    barrier = pltpu.get_barrier_semaphore()
    for other in others:
        pl.semaphore_signal(barrier, inc=1, device_id=other, device_id_type=MESH)
    pl.semaphore_wait(barrier, len(others))


class Piece:
    def __init__(self, source, out, axis, dim, start, size):
        self.source, self.out, self.axis = source, out, axis
        self.dim, self.start, self.size = dim, start, size

    def cut(self, part):
        parts = {"x": 2, "y": 4, "z": 1}[self.axis]
        size = self.size // parts
        unit = 128 if self.dim == 1 else 16
        start = self.start if parts == 1 else pl.multiple_of(self.start + part * size, unit)
        window = pl.ds(start, size)
        return (slice(None), window) if self.dim == 1 else (window, slice(None))


class Gather:
    def __init__(self, pieces, copies, local):
        self.pieces, self.copies, self.local = pieces, copies, local
        self.x, self.y, self.z, self.c = x, y, z, c = place()
        self.xh, self.xl = x // 2, x % 2
        self.sibling = device(x, y, z, 1 - c)
        self.far = device(step(x, 2), y, z, c)
        self.lines = {
            "x": [device(step(x, d), y, z, c) for d in (1, 2, 3)],
            "y": [device(x, step(y, d), z, c) for d in (1, 2, 3)],
            "z": [device(x, y, step(z, d), c) for d in (1, 2, 3)],
        }
        self.part = {"x": self.xl, "y": y, "z": 0}

    def others(self):
        return [self.sibling] + self.lines["x"] + self.lines["y"] + self.lines["z"]

    def block(self, p, dz, flip, part, core=None):
        core = self.c if core is None else core
        return p.out.at[(step(self.z, -dz), (self.xh + flip) % 2, core) + p.cut(part)]

    def both(self, key, src, dst, axis):
        self.copies.push(key + (1,), src, dst, self.lines[axis][0])
        self.copies.push(key + (3,), src, dst, self.lines[axis][2])

    def first(self):
        self.stays = []
        for n, p in enumerate(self.pieces):
            mine = p.source.at[p.cut(self.part[p.axis])]
            there = self.block(p, 0, 0, self.part[p.axis])
            copy = pltpu.make_async_copy(mine, there, self.local.at[n])
            copy.start()
            self.stays.append(copy)
            if p.axis != "x":
                self.copies.push((n, "far"), mine, there, self.far)
            if p.axis != "z":
                for d in (1, 2, 3):
                    self.copies.push((n, "mid", 0, d), mine, there, self.lines["z"][d - 1])
        for n, p in enumerate(self.pieces):
            mine = p.source.at[p.cut(self.part[p.axis])]
            self.both((n, "end", 0, 0), mine, self.block(p, 0, 0, self.part[p.axis]), p.axis)

    def second(self):
        for n, p in enumerate(self.pieces):
            if p.axis == "x":
                continue
            block = self.block(p, 0, 1, self.part[p.axis])
            self.copies.arrived((n, "far"), block, self.far)
            if p.axis == "y":
                for d in (1, 2, 3):
                    self.copies.push((n, "mid", 1, d), block, block, self.lines["z"][d - 1])
            self.both((n, "end", 0, 1), block, block, p.axis)

    def third(self):
        for dz in (1, 3, 2):
            for n, p in enumerate(self.pieces):
                if p.axis == "z":
                    continue
                for flip in (0, 1) if p.axis == "y" else (0,):
                    block = self.block(p, dz, flip, self.part[p.axis])
                    self.copies.arrived((n, "mid", flip, dz), block, self.lines["z"][3 - dz])
                    self.both((n, "end", dz, flip), block, block, p.axis)

    def blocks(self, p):
        if p.axis == "z":
            return ((0, 0), (0, 1))
        return tuple((dz, f) for dz in (0, 1, 3, 2) for f in ((0, 1) if p.axis == "y" else (0,)))

    def ended(self, n, p, dz, flip, d):
        if p.axis == "z":
            block = self.block(p, d, flip, 0)
        elif p.axis == "y":
            block = self.block(p, dz, flip, step(self.y, -d))
        else:
            from_x = step(self.x, -d)
            block = p.out.at[(step(self.z, -dz), from_x // 2, self.c) + p.cut(from_x % 2)]
        self.copies.arrived((n, "end", dz, flip, d), block, self.lines[p.axis][3 - d])
        return block

    def group(self, p, d, core):
        if p.axis == "z":
            return p.out.at[(step(self.z, -d), slice(None), core) + p.cut(0)]
        if p.axis == "y":
            return p.out.at[(slice(None), slice(None), core) + p.cut(step(self.y, -d))]
        from_x = step(self.x, -d)
        return p.out.at[(slice(None), from_x // 2, core) + p.cut(from_x % 2)]

    def share(self, n, p, d):
        block = self.group(p, d, self.c)
        self.copies.push((n, "core", d), block, block, self.sibling)

    def fourth(self):
        for copy in self.stays:
            copy.wait()
        for n, p in enumerate(self.pieces):
            self.share(n, p, 0)
        for at in range(8):
            for n, p in enumerate(self.pieces):
                if at >= len(self.blocks(p)):
                    continue
                dz, flip = self.blocks(p)[at]
                line = self.lines[p.axis]
                for d in (1, 3):
                    block = self.ended(n, p, dz, flip, d)
                    if (at % 2 == 0) == (d == 1):
                        on = line[0] if d == 1 else line[2]
                        self.copies.push((n, "end", dz, flip, 2), block, block, on)
                if at == len(self.blocks(p)) - 1:
                    self.share(n, p, 1)
                    self.share(n, p, 3)

    def last(self):
        for n, p in enumerate(self.pieces):
            for dz, flip in self.blocks(p):
                self.ended(n, p, dz, flip, 2)
            self.share(n, p, 2)
        for d in (0, 1, 3, 2):
            for n, p in enumerate(self.pieces):
                block = self.group(p, d, 1 - self.c)
                self.copies.arrived((n, "core", d), block, self.sibling)


def early_kernel(qkv, small, o_qkv, o_small, local, send, recv):
    pieces = [
        Piece(small, o_small, "z", 0, 0, small.shape[0]),
        Piece(qkv, o_qkv, "z", 1, 18 * 128, 9 * 128),
        Piece(qkv, o_qkv, "x", 1, 8 * 128, 10 * 128),
        Piece(qkv, o_qkv, "y", 1, 0, 8 * 128),
    ]
    copies = Copies(send, recv)
    work = Gather(pieces, copies, local)
    greet(work.others())
    work.first()
    work.second()
    work.third()
    work.fourth()
    work.last()
    copies.finish()


def head_slices(rows):
    for j in range(rows.shape[1] // (16 * HD)):
        for h in range(16):
            at = j * 16 * HD + h * HD
            yield h // 2, 2 * j + h % 2, at


def exchange(copies, name, seq, peers, sent, got, local):
    for e in range(1, 8):
        copies.push((name, e), sent.at[(seq + e) % 8], got.at[seq], peers[e - 1])
    copy = pltpu.make_async_copy(sent.at[seq], got.at[seq], local)
    copy.start()
    return copy


def exchanged(copies, name, seq, peers, got, copy):
    copy.wait()
    for e in range(1, 8):
        copies.arrived((name, e), got.at[(seq + 8 - e) % 8], peers[7 - e])


def seq_peers():
    x, y, z, c = place()
    seq = y * 2 + x % 2
    return seq, [((seq + e) % 8, z * 4 + (x // 2) * 2 + c) for e in range(1, 8)]


def unique(x, y, z, c, extra):
    _, peers = seq_peers()
    far = [device((1 - x // 2) * 2 + e, y, z, c) for e in (0, 1)]
    return peers + far + [device(x, y, step(z, d), c) for d in (1, 2, 3)] + extra


CHUNK = 256


def attend(heads, h, out):
    tokens = 8 * 128
    keys = heads[:, 2 + h].reshape(tokens, HD)
    values = heads[:, 4 + h].reshape(tokens, HD)

    @pl.loop(0, tokens // CHUNK)
    def _(i):
        queries = heads[pl.ds(i * 2, 2), h].reshape(CHUNK, HD)
        scores = lax.dot_general(
            queries, keys, (((1,), (1,)), ((), ())), preferred_element_type=jnp.float32
        ) * (HD**-0.5)
        exponent = jnp.exp(scores - jnp.max(scores, axis=1, keepdims=True))
        weights = exponent * (1.0 / jnp.sum(exponent, axis=1, keepdims=True))
        got = jnp.dot(weights.astype(jnp.bfloat16), values, preferred_element_type=jnp.float32)
        out[pl.ds(i * 2, 2), h] = got.astype(jnp.bfloat16).reshape(2, 128, HD)


def attend_back(heads, grads, h, out, key_sum, value_sum):
    tokens = 8 * 128
    keys = heads[:, 2 + h].reshape(tokens, HD)
    values = heads[:, 4 + h].reshape(tokens, HD)
    key_sum[...] = jnp.zeros_like(key_sum)
    value_sum[...] = jnp.zeros_like(value_sum)
    across = (((1,), (1,)), ((), ()))

    @pl.loop(0, tokens // CHUNK)
    def _(i):
        queries = heads[pl.ds(i * 2, 2), h].reshape(CHUNK, HD)
        grad = grads[pl.ds(i * 2, 2), h].reshape(CHUNK, HD)
        scores = lax.dot_general(
            keys, queries, across, preferred_element_type=jnp.float32
        ) * (HD**-0.5)
        exponent = jnp.exp(scores - jnp.max(scores, axis=0, keepdims=True))
        weights = exponent * (1.0 / jnp.sum(exponent, axis=0, keepdims=True))
        grad_weights = lax.dot_general(values, grad, across, preferred_element_type=jnp.float32)
        inner = jnp.sum(weights * grad_weights, axis=0, keepdims=True)
        grad_scores = (weights * (grad_weights - inner)).astype(jnp.bfloat16)
        value_sum[...] += jnp.dot(
            weights.astype(jnp.bfloat16), grad, preferred_element_type=jnp.float32
        )
        key_sum[...] += jnp.dot(grad_scores, queries, preferred_element_type=jnp.float32)
        grad_q = lax.dot_general(
            grad_scores, keys, (((0,), (0,)), ((), ())), preferred_element_type=jnp.float32
        ) * (HD**-0.5)
        out[pl.ds(i * 2, 2), h] = grad_q.astype(jnp.bfloat16).reshape(2, 128, HD)

    out[:, 2 + h] = (key_sum[...] * (HD**-0.5)).astype(jnp.bfloat16).reshape(8, 128, HD)
    out[:, 4 + h] = value_sum[...].astype(jnp.bfloat16).reshape(8, 128, HD)


def late_kernel(
    up, cq, ckv, pair, down, packed,
    o_up, o_cq, o_ckv, o_pair, o_down, o_heads, o_rows,
    sent, heads, mixed, joined, local, send, recv,
):
    height = down.shape[0]
    pieces = [
        Piece(cq, o_cq, "z", 1, 0, cq.shape[1]),
        Piece(ckv, o_ckv, "z", 1, 0, ckv.shape[1]),
        Piece(pair, o_pair, "x", 1, 0, pair.shape[1]),
        Piece(up, o_up, "y", 1, 0, up.shape[1]),
        Piece(down, o_down, "x", 0, 128, height - 128),
        Piece(down, o_down, "y", 0, 0, 128),
    ]
    copies = Copies(send, recv)
    work = Gather(pieces, copies, local)
    seq, peers = seq_peers()
    greet(unique(work.x, work.y, work.z, work.c, [work.sibling]))
    for to, what, at in head_slices(packed):
        sent[to, what] = packed[:, at : at + HD]
    own = exchange(copies, "in", seq, peers, sent, heads, local.at[6])
    work.first()
    exchanged(copies, "in", seq, peers, heads, own)
    keep = pltpu.make_async_copy(heads, o_heads, local.at[7])
    keep.start()
    attend(heads, 0, mixed)
    work.second()
    attend(heads, 1, mixed)
    own = exchange(copies, "out", seq, peers, mixed, joined, local.at[8])
    work.third()
    work.fourth()
    exchanged(copies, "out", seq, peers, joined, own)
    for at, what, to in head_slices(o_rows):
        o_rows[:, to : to + HD] = joined[at, what]
    work.last()
    keep.wait()
    copies.finish()


def whole(out):
    return out.reshape((-1,) + out.shape[4:])


def full_shapes(shards):
    return tuple(jax.ShapeDtypeStruct((4, 2, 2) + s.shape, s.dtype) for s in shards)


def semaphores(*counts):
    return [pltpu.SemaphoreType.DMA((n,)) for n in counts]


ANYWHERE = pl.BlockSpec(memory_space=pl.ANY)
ON_CHIP = pl.BlockSpec(memory_space=pltpu.VMEM)


def parameters(collective):
    return pltpu.CompilerParams(
        collective_id=collective, has_side_effects=True, vmem_limit_bytes=48 * 1024 * 1024
    )


def gather_early(*shards):
    outs = pl.pallas_call(
        early_kernel,
        out_shape=full_shapes(shards),
        in_specs=[ANYWHERE] * 2,
        out_specs=(ANYWHERE,) * 2,
        scratch_shapes=semaphores(4, 128, 128),
        compiler_params=parameters(0),
    )(*shards)
    return tuple(whole(out) for out in outs)


def gather_late(shards, packed):
    bf16 = lambda *shape: jax.ShapeDtypeStruct(shape, jnp.bfloat16)
    vmem = lambda *shape: pltpu.VMEM(shape, jnp.bfloat16)
    outs = pl.pallas_call(
        late_kernel,
        out_shape=full_shapes(shards) + (bf16(8, 6, 128, HD), bf16(128, 16 * HD)),
        in_specs=[ANYWHERE] * 5 + [ON_CHIP],
        out_specs=(ANYWHERE,) * 6 + (ON_CHIP,),
        scratch_shapes=[
            vmem(8, 6, 128, HD), vmem(8, 6, 128, HD), vmem(8, 2, 128, HD), vmem(8, 2, 128, HD),
        ]
        + semaphores(9, 256, 256),
        compiler_params=parameters(1),
    )(*shards, packed)
    return tuple(whole(out) for out in outs[:5]) + outs[5:]


def add_up(parts, out):
    blocks, _, columns = out.shape
    tile = next(t for t in (384, 512, 256, 128) if columns % t == 0)

    @pl.loop(0, blocks * (columns // tile))
    def _(i):
        block = i // (columns // tile)
        cols = pl.ds(pl.multiple_of((i % (columns // tile)) * tile, 128), tile)
        total = parts[0][block, :, cols].astype(jnp.float32)
        for part in parts[1:]:
            total = total + part[block, :, cols].astype(jnp.float32)
        out[block, :, cols] = total.astype(out.dtype)


def columns(part, width, start=0):
    return pl.ds(pl.multiple_of(start + part * width, 128), width)


class Scatter:
    def __init__(self, by_y, by_x, by_z, outs, scratch, copies, keep):
        self.by_y, self.by_x, self.by_z = by_y, by_x, by_z
        self.o_up, self.o_mix, self.o_att = outs
        self.scratch, self.copies, self.keep = scratch, copies, keep
        self.x, self.y, self.z, self.c = x, y, z, c = place()
        self.xh, self.xl = x // 2, x % 2
        self.seq, self.peers = seq_peers()
        self.along_x = [device(step(x, d), y, z, c) for d in (1, 2, 3)]
        self.along_y = [device(x, step(y, d), z, c) for d in (1, 2, 3)]
        self.along_z = [device(x, y, step(z, d), c) for d in (1, 2, 3)]

    @staticmethod
    def buffers(by_y, by_x, by_z):
        vmem = lambda *shape: pltpu.VMEM(shape, jnp.bfloat16)
        wy, wx, wz = by_y // 4, by_x // 2, by_z
        return [
            vmem(4, 4, 2, HD, wy), vmem(4, 2, HD, wy), vmem(4, 2, HD, wy),
            vmem(2, HD, wy), vmem(4, HD, wy), vmem(1, HD, wy),
            vmem(4, 2, HD, wz), vmem(2, HD, wz), vmem(4, 2, HD, wz // 4),
            vmem(2, HD, wz // 4), vmem(4, HD, wz // 4), vmem(1, HD, wz // 4),
            vmem(4, 4, HD, wx), vmem(4, HD, wx), vmem(4, 4, HD, wx // 4),
            vmem(4, HD, wx // 4), vmem(4, HD, wx // 4), vmem(1, HD, wx // 4),
        ]

    def first(self):
        u1, a1, m1 = self.scratch[0], self.scratch[6], self.scratch[12]
        up, up_at, up_size = self.by_y
        mix, mix_at, mix_size = self.by_x
        for d in (1, 2, 3):
            to_x, to_y, to_z = step(self.x, d), step(self.y, d), step(self.z, d)
            cols = columns(to_y, up_size // 4, up_at)
            self.copies.push(("u1", d), up.at[:, :, :, cols], u1.at[d], self.along_y[d - 1])
            cols = columns(to_x % 2, mix_size // 2, mix_at)
            self.copies.push(
                ("m1", d), mix.at[:, to_x // 2, :, cols], m1.at[d], self.along_x[d - 1]
            )
            at = 0
            for n, (source, start, size) in enumerate(self.by_z):
                self.copies.push(
                    ("a1", n, d),
                    source.at[to_z, :, :, pl.ds(start, size)],
                    a1.at[d, :, :, pl.ds(at, size)],
                    self.along_z[d - 1],
                )
                at += size
        self.keep(up.at[:, :, :, columns(self.y, up_size // 4, up_at)], u1.at[0])
        self.keep(mix.at[:, self.xh, :, columns(self.xl, mix_size // 2, mix_at)], m1.at[0])
        at = 0
        for source, start, size in self.by_z:
            self.keep(
                source.at[self.z, :, :, pl.ds(start, size)], a1.at[0, :, :, pl.ds(at, size)]
            )
            at += size

    def second(self):
        u1, u1s, u2 = self.scratch[:3]
        a1, a1s, a2 = self.scratch[6:9]
        m1, m1s, m2 = self.scratch[12:15]
        for d in (1, 2, 3):
            at = 0
            for n, (_, _, size) in enumerate(self.by_z):
                got = a1.at[d, :, :, pl.ds(at, size)]
                self.copies.arrived(("a1", n, d), got, self.along_z[3 - d])
                at += size
        add_up([a1.at[i] for i in range(4)], a1s)
        for d in (1, 2, 3):
            cols = columns(step(self.y, d), a2.shape[-1])
            self.copies.push(("a2", d), a1s.at[:, :, cols], a2.at[d], self.along_y[d - 1])
        for d in (1, 2, 3):
            self.copies.arrived(("m1", d), m1.at[d], self.along_x[3 - d])
        add_up([m1.at[i] for i in range(4)], m1s)
        for d in (1, 2, 3):
            cols = columns(step(self.y, d), m2.shape[-1])
            self.copies.push(("m2", d), m1s.at[:, :, cols], m2.at[d], self.along_y[d - 1])
        for d in (1, 2, 3):
            self.copies.arrived(("u1", d), u1.at[d], self.along_y[3 - d])
        for zz in range(4):
            add_up([u1.at[i, zz] for i in range(4)], u1s.at[zz])
        for d in (1, 2, 3):
            self.copies.push(
                ("u2", d), u1s.at[step(self.z, d)], u2.at[d], self.along_z[d - 1]
            )

    def third(self):
        u1s, u2, u2s, u3 = self.scratch[1:5]
        a1s, a2, a2s, a3 = self.scratch[7:11]
        m1s, m2, m2s, m3 = self.scratch[13:17]
        for d in (1, 2, 3):
            self.copies.arrived(("a2", d), a2.at[d], self.along_y[3 - d])
        add_up(
            [a1s.at[:, :, columns(self.y, a2.shape[-1])]] + [a2.at[d] for d in (1, 2, 3)], a2s
        )
        for d in (1, 2, 3):
            to = step(self.x, d) // 2
            self.copies.push(("a3", d), a2s.at[to], a3.at[d], self.along_x[d - 1])
        for d in (1, 2, 3):
            self.copies.arrived(("m2", d), m2.at[d], self.along_y[3 - d])
        add_up(
            [m1s.at[:, :, columns(self.y, m2.shape[-1])]] + [m2.at[d] for d in (1, 2, 3)], m2s
        )
        for d in (1, 2, 3):
            self.copies.push(("m3", d), m2s.at[step(self.z, d)], m3.at[d], self.along_z[d - 1])
        for d in (1, 2, 3):
            self.copies.arrived(("u2", d), u2.at[d], self.along_z[3 - d])
        add_up([u1s.at[self.z]] + [u2.at[d] for d in (1, 2, 3)], u2s)
        for d in (1, 2, 3):
            to = step(self.x, d) // 2
            self.copies.push(("u3", d), u2s.at[to], u3.at[d], self.along_x[d - 1])

    def fourth(self):
        u2s, u3, u3s = self.scratch[3:6]
        a2s, a3, a3s = self.scratch[9:12]
        m2s, m3, m3s = self.scratch[15:18]
        for name, line, sums, got, total, out, mine in (
            ("a", self.along_x, a2s, a3, a3s, self.o_att, self.xh),
            ("u", self.along_x, u2s, u3, u3s, self.o_up, self.xh),
            ("m", self.along_z, m2s, m3, m3s, self.o_mix, self.z),
        ):
            for d in (1, 2, 3):
                self.copies.arrived((name + "3", d), got.at[d], line[3 - d])
            add_up([sums.at[pl.ds(mine, 1)]] + [got.at[pl.ds(d, 1)] for d in (1, 2, 3)], total)
            if name == "m":
                spot = out.at[:, self.spot(self.seq)]
                for e in range(1, 8):
                    self.copies.push(("m4", e), total.at[0], spot, self.peers[e - 1])
            else:
                spot = out.at[:, columns(self.y, total.shape[-1])]
                for d in (1, 2, 3):
                    self.copies.push((name + "4", d), total.at[0], spot, self.along_y[d - 1])
            self.keep(total.at[0], spot)

    def spot(self, seq):
        return columns((seq % 2) * 4 + seq // 2, self.scratch[17].shape[-1])

    def last(self):
        for d in (1, 2, 3):
            from_y = step(self.y, -d)
            for name, out in (("u4", self.o_up), ("a4", self.o_att)):
                got = out.at[:, columns(from_y, out.shape[-1] // 4)]
                self.copies.arrived((name, d), got, self.along_y[3 - d])
        for e in range(1, 8):
            got = self.o_mix.at[:, self.spot((self.seq + 8 - e) % 8)]
            self.copies.arrived(("m4", e), got, self.peers[7 - e])


class Stays:
    def __init__(self, local):
        self.local, self.copies, self.done = local, [], 0

    def __call__(self, src, dst):
        copy = pltpu.make_async_copy(src, dst, self.local.at[len(self.copies)])
        copy.start()
        self.copies.append(copy)

    def wait(self):
        for copy in self.copies[self.done :]:
            copy.wait()
        self.done = len(self.copies)


def back_kernel(
    up, mix, heads, grad_rows, o_up, o_mix, o_att, o_flat,
    sent, grads, mixed, joined, key_sum, value_sum, *rest,
):
    scratch, (local, send, recv) = rest[:18], rest[18:]
    copies, keep = Copies(send, recv), Stays(local)
    half = mix.shape[-1] // 2
    work = Scatter(
        (up, 0, up.shape[-1]), (mix, 0, half), [(mix, half, half)],
        (o_up, o_mix, o_att), scratch, copies, keep,
    )
    seq, peers = seq_peers()
    greet(unique(work.x, work.y, work.z, work.c, []))
    for to, what, at in head_slices(grad_rows):
        sent[to, what] = grad_rows[:, at : at + HD]
    own = exchange(copies, "in", seq, peers, sent, grads, local.at[16])
    work.first()
    exchanged(copies, "in", seq, peers, grads, own)
    for h in (0, 1):
        attend_back(heads, grads, h, mixed, key_sum, value_sum)
    own = exchange(copies, "out", seq, peers, mixed, joined, local.at[17])
    keep.wait()
    work.second()
    work.third()
    exchanged(copies, "out", seq, peers, joined, own)
    for at, what, to in head_slices(o_flat):
        o_flat[:, to : to + HD] = joined[at, what]
    work.fourth()
    work.last()
    keep.wait()
    copies.finish()


def scatter_back(up, mix, heads, grad_rows):
    half = mix.shape[-1] // 2
    bf16 = lambda *shape: jax.ShapeDtypeStruct(shape, jnp.bfloat16)
    vmem = lambda *shape: pltpu.VMEM(shape, jnp.bfloat16)
    return pl.pallas_call(
        back_kernel,
        out_shape=(
            bf16(HD, up.shape[-1]), bf16(HD, half), bf16(HD, half), bf16(128, 48 * HD),
        ),
        in_specs=[ANYWHERE] * 2 + [ON_CHIP] * 2,
        out_specs=(ANYWHERE,) * 3 + (ON_CHIP,),
        scratch_shapes=[
            vmem(8, 2, 128, HD), vmem(8, 2, 128, HD), vmem(8, 6, 128, HD), vmem(8, 6, 128, HD),
            pltpu.VMEM((1024, HD), jnp.float32), pltpu.VMEM((1024, HD), jnp.float32),
        ]
        + Scatter.buffers(up.shape[-1], half, half)
        + semaphores(18, 64, 64),
        compiler_params=parameters(2),
    )(up, mix, heads, grad_rows)


def rest_kernel(
    qkv, small, down, mod, cap, o_up, o_mix, o_att, o_down, o_mod, o_cap,
    d1, d1s, d2, d2s, t1, *rest,
):
    scratch, (local, send, recv) = rest[:18], rest[18:]
    copies, keep = Copies(send, recv), Stays(local)
    work = Scatter(
        (qkv, 0, 1024), (qkv, 1024, 1024), [(qkv, 2048, 1408), (small, 0, 128)],
        (o_up, o_mix, o_att), scratch, copies, keep,
    )
    seq, peers, along_y = work.seq, work.peers, work.along_y
    greet(unique(work.x, work.y, work.z, work.c, []))
    for d in (1, 2, 3):
        copies.push(("d1", d), down.at[step(work.y, d)], d1.at[d], along_y[d - 1])
    work.first()
    for e in range(1, 8):
        copies.push(("t1", e), mod, t1.at[e], peers[e - 1])
        copies.push(("cap", e), cap, o_cap.at[seq], peers[e - 1])
    keep(down.at[work.y], d1.at[0])
    keep(mod, t1.at[0])
    keep(cap, o_cap.at[seq])
    keep.wait()
    beside = device(work.xh * 2 + 1 - work.xl, work.y, work.z, work.c)
    for d in (1, 2, 3):
        copies.arrived(("d1", d), d1.at[d], along_y[3 - d])
    add_up([d1.at[pl.ds(i, 1)] for i in range(4)], d1s)
    copies.push(("d2",), d1s, d2, beside)
    work.second()
    copies.arrived(("d2",), d2, beside)
    add_up([d1s, d2], d2s)
    keep(d2s.at[0], o_down.at[work.y])
    for d in (1, 2, 3):
        copies.push(("d3", d), d2s.at[0], o_down.at[work.y], along_y[d - 1])
    work.third()
    total = t1[0].astype(jnp.float32)
    for e in range(1, 8):
        copies.arrived(("t1", e), t1.at[e], peers[7 - e])
        total = total + t1[e].astype(jnp.float32)
    o_mod[...] = total
    work.fourth()
    work.last()
    for d in (1, 2, 3):
        copies.arrived(("d3", d), o_down.at[step(work.y, -d)], along_y[3 - d])
    for e in range(1, 8):
        copies.arrived(("cap", e), o_cap.at[(seq + 8 - e) % 8], peers[7 - e])
    keep.wait()
    copies.finish()


def scatter_rest(qkv, small, down, mod, cap):
    width = down.shape[-1]
    bf16 = lambda *shape: jax.ShapeDtypeStruct(shape, jnp.bfloat16)
    vmem = lambda *shape: pltpu.VMEM(shape, jnp.bfloat16)
    return pl.pallas_call(
        rest_kernel,
        out_shape=(
            bf16(HD, 1024), bf16(HD, 1024), bf16(HD, 1536), bf16(4, HD, width),
            jax.ShapeDtypeStruct(mod.shape, jnp.float32), bf16(8, *cap.shape),
        ),
        in_specs=[ANYWHERE] * 5,
        out_specs=(ANYWHERE,) * 4 + (ON_CHIP, ANYWHERE),
        scratch_shapes=[
            vmem(4, HD, width), vmem(1, HD, width), vmem(1, HD, width), vmem(1, HD, width),
            vmem(8, *mod.shape),
        ]
        + Scatter.buffers(1024, 1024, 1536)
        + semaphores(18, 80, 80),
        compiler_params=parameters(3),
    )(qkv, small, down, mod, cap)


def sibling_pairs():
    return [(i, i + 1 - 2 * (i % 2)) for i in range(16)]


def by_core(matrix):
    core = lax.axis_index("fsdp") % 2
    split = matrix.reshape((8, 2, -1) + matrix.shape[1:])
    pick = lambda which: lax.dynamic_index_in_dim(split, which, 1, keepdims=False).reshape(
        (-1,) + matrix.shape[1:]
    )
    return pick(core), pick(1 - core)


def pair_grad(former, latter):
    own, other = by_core(former.T)
    theirs = project(other, latter).astype(jnp.bfloat16)
    received = lax.ppermute(theirs, "fsdp", sibling_pairs())
    return (project(own, latter) + received.astype(jnp.float32)).astype(jnp.bfloat16)


def on_device(
    latents,
    timestep,
    caption,
    shift_table,
    qkv_weight,
    query_bias,
    value_bias,
    proj_weight,
    proj_bias,
    cross_query,
    cross_qbias,
    cross_kv,
    cross_vbias,
    cross_proj,
    cross_pbias,
    up_weight,
    up_bias,
    down_weight,
    down_bias,
    cotangent,
):
    group = lax.axis_index("fsdp")
    small = jnp.zeros((32 * HD * 16,), jnp.bfloat16)
    at = 0
    for vector in (
        shift_table, query_bias, value_bias, proj_bias, cross_qbias, cross_vbias, cross_pbias,
        down_bias, up_bias,
    ):
        small = lax.dynamic_update_slice(small, vector, (at + group * vector.shape[0],))
        at += 16 * vector.shape[0]
    full_qkv, each_small = gather_early(qkv_weight, small.reshape(32, -1))
    full_small = jnp.sum(each_small.reshape(16, 32, -1).astype(jnp.float32), axis=0)
    full_table = full_small[:6]
    full_qbias, full_vbias, full_pbias, full_cqbias, full_cvbias, full_cpbias, full_dbias = (
        full_small[6 + i] for i in range(7)
    )
    full_ubias = full_small[13:17].reshape(-1)
    latent_count, local_len, model_width = latents.shape
    inputs = latents.astype(jnp.float32)
    modulation = (full_table + timestep.astype(jnp.float32).reshape(6, model_width)).reshape(
        latent_count, 6, 1, model_width
    )
    shift_one, scale_one, gate_one = (modulation[:, 0], modulation[:, 1], modulation[:, 2])
    shift_two, scale_two, gate_two = (modulation[:, 3], modulation[:, 4], modulation[:, 5])
    pre_one, pull_one = jax.vjp(modulate, inputs, shift_one, scale_one)
    normed_one = pre_one.astype(jnp.bfloat16)
    qkv_bias = jnp.concatenate([full_qbias, jnp.zeros_like(full_qbias), full_vbias]).astype(
        jnp.float32
    )
    packed = (project(normed_one, full_qkv) + qkv_bias).astype(jnp.bfloat16)
    full_up, full_cquery, full_ckv, full_pair, full_down, heads, rows = gather_late(
        (
            up_weight,
            cross_query,
            cross_kv,
            jnp.concatenate([proj_weight, cross_proj], axis=1),
            down_weight,
        ),
        packed[0],
    )
    full_proj, full_cproj = jnp.split(full_pair, 2, axis=1)
    tok_major = rows[None]
    branch_one = project(tok_major, full_proj) + full_pbias.astype(jnp.float32)
    after_one = inputs + gate_one * branch_one
    middle = after_one.astype(jnp.bfloat16)
    cross_rows = (project(middle, full_cquery) + full_cqbias.astype(jnp.float32)).astype(
        jnp.bfloat16
    )
    kv_bias = jnp.concatenate([jnp.zeros_like(full_cvbias), full_cvbias]).astype(jnp.float32)
    text_kv = (project(caption, full_ckv) + kv_bias).astype(jnp.bfloat16)
    text_keys = by_heads(text_kv[..., :model_width])
    text_values = by_heads(text_kv[..., model_width:])
    cross_heads, cross_logsum = jax.vmap(attend_forward)(
        by_heads(cross_rows), text_keys, text_values
    )
    crossed = cross_heads.reshape(latent_count, local_len, model_width)
    branch_two = project(crossed, full_cproj) + full_cpbias.astype(jnp.float32)
    after_two = after_one + branch_two
    pre_two, pull_two = jax.vjp(modulate, after_two, shift_two, scale_two)
    normed_two = pre_two.astype(jnp.bfloat16)
    hidden = project(normed_two, full_up) + full_ubias.astype(jnp.float32)
    activated, gelu_pull = jax.vjp(jax.nn.gelu, hidden)
    act_rows = activated.astype(jnp.bfloat16)
    branch_three = project(act_rows, full_down) + full_dbias.astype(jnp.float32)
    block_out = (after_two + gate_two * branch_three).astype(jnp.bfloat16)
    grad_out = cotangent.astype(jnp.float32)
    grad_gate_two = jnp.sum(grad_out * branch_three, axis=1, keepdims=True)
    grad_three = (gate_two * grad_out).astype(jnp.bfloat16)
    down_grad = weight_grad(act_rows, grad_three)
    down_bgrad = token_sum(grad_three)
    grad_act = project(grad_three, full_down.T)
    grad_hidden = gelu_pull(grad_act)[0].astype(jnp.bfloat16)
    up_grad = pair_grad(normed_two[0], grad_hidden[0])
    up_bgrad = token_sum(grad_hidden)
    grad_pre_two = project(grad_hidden, full_up.T)
    grad_mid_two, grad_shift_two, grad_scale_two = pull_two(grad_pre_two)
    grad_after_two = grad_out + grad_mid_two
    down_part = lax.psum_scatter(
        down_grad.astype(jnp.bfloat16), "fsdp", scatter_dimension=0, tiled=True
    )
    grad_branch_two = grad_after_two.astype(jnp.bfloat16)
    cproj_grad = pair_grad(crossed[0], grad_branch_two[0])
    cproj_bgrad = token_sum(grad_branch_two)
    grad_crossed = project(grad_branch_two, full_cproj.T).astype(jnp.bfloat16)
    grad_cq, grad_ck, grad_cv = jax.vmap(attend_backward)(
        by_heads(cross_rows), text_keys, text_values, cross_logsum, by_heads(grad_crossed)
    )
    grad_cross_rows = grad_cq.reshape(latent_count, local_len, model_width).astype(jnp.bfloat16)
    cquery_grad = pair_grad(middle[0], grad_cross_rows[0])
    cquery_bgrad = token_sum(grad_cross_rows)
    grad_after_one = grad_after_two + project(grad_cross_rows, full_cquery.T)
    text_partial = jnp.concatenate(
        [
            grad_ck.reshape(grad_ck.shape[:2] + (model_width,)),
            grad_cv.reshape(grad_cv.shape[:2] + (model_width,)),
        ],
        axis=-1,
    )
    text_piece = text_partial.shape[1] // 8
    text_pieces = lax.all_to_all(
        text_partial[0].astype(jnp.bfloat16).reshape(8, text_piece, -1), "seq", 0, 0
    )
    text_grad = jnp.sum(text_pieces.astype(jnp.float32), axis=0).astype(jnp.bfloat16)
    caption_part = lax.dynamic_slice_in_dim(
        caption[0], lax.axis_index("seq") * text_piece, text_piece, 0
    )
    ckv_grad = pair_grad(caption_part, text_grad)
    cvalue_bgrad = jnp.sum(text_grad[:, model_width:].astype(jnp.float32), axis=0)
    caption_piece = project(text_grad, full_ckv.T)
    grad_gate_one = jnp.sum(grad_after_one * branch_one, axis=1, keepdims=True)
    grad_branch_one = (gate_one * grad_after_one).astype(jnp.bfloat16)
    proj_grad = pair_grad(tok_major[0], grad_branch_one[0])
    proj_bgrad = token_sum(grad_branch_one)
    grad_tok = project(grad_branch_one, full_proj.T).astype(jnp.bfloat16)
    blocks = lambda grad: grad.reshape(4, 2, HD, -1)
    mix = jnp.concatenate(
        [proj_grad, cproj_grad, cquery_grad, ckv_grad, jnp.zeros((8 * HD, 384), jnp.bfloat16)],
        axis=1,
    )
    sum_up, sum_mix, sum_att, flat = scatter_back(
        blocks(up_grad), blocks(mix), heads, grad_tok[0]
    )
    sum_mix = jnp.concatenate([sum_mix, sum_att], axis=1)
    grad_flat = flat[None]
    qkv_grad = pair_grad(normed_one[0], grad_flat[0])
    qbias_grad = token_sum(grad_flat[..., :model_width])
    vbias_grad = token_sum(grad_flat[..., 2 * model_width :])
    grad_pre_one = project(grad_flat, full_qkv.T)
    grad_norm_one, grad_shift_one, grad_scale_one = pull_one(grad_pre_one)
    grad_latents = grad_after_one + grad_norm_one
    grad_mod = jnp.concatenate(
        [
            grad_shift_one,
            grad_scale_one,
            grad_gate_one,
            grad_shift_two,
            grad_scale_two,
            grad_gate_two,
        ],
        axis=1,
    )
    grad_mod = grad_mod.reshape(latent_count, 6 * model_width)
    small_grad = jnp.concatenate(
        [
            grad_mod.reshape(-1, 6),
            qbias_grad.reshape(-1, 1),
            vbias_grad.reshape(-1, 1),
            proj_bgrad.reshape(-1, 1),
            cquery_bgrad.reshape(-1, 1),
            cvalue_bgrad.reshape(-1, 1),
            cproj_bgrad.reshape(-1, 1),
            down_bgrad.reshape(-1, 1),
            up_bgrad.reshape(-1, 4),
        ],
        axis=1,
    )
    small_own, small_other = by_core(small_grad)
    small_sum = small_own + lax.ppermute(
        small_other.astype(jnp.bfloat16), "fsdp", sibling_pairs()
    ).astype(jnp.float32)
    sum_q, sum_k, sum_v, sum_down, sum_mod, caption_all = scatter_rest(
        blocks(qkv_grad),
        jnp.pad(blocks(small_sum.astype(jnp.bfloat16)), ((0, 0), (0, 0), (0, 0), (0, 111))),
        down_part.reshape(4, HD, model_width),
        jnp.pad(grad_mod.astype(jnp.bfloat16).reshape(-1, 128), ((0, 10), (0, 0))),
        jnp.pad(caption_piece.astype(jnp.bfloat16), ((0, 1), (0, 0))),
    )
    wide = lambda part: part.astype(jnp.float32)
    sum_small = wide(sum_v[:, 1408 : 1408 + 17])
    return (
        block_out,
        grad_latents,
        sum_mod[:54].reshape(1, -1),
        wide(caption_all[:, :text_piece].reshape(1, -1, model_width)),
        sum_small[:, :6].reshape(-1),
        jnp.concatenate([wide(sum_q), wide(sum_k), wide(sum_v[:, :1408])], axis=1),
        sum_small[:, 6],
        sum_small[:, 7],
        wide(sum_mix[:, :model_width]),
        sum_small[:, 8],
        wide(sum_mix[:, 2 * model_width : 3 * model_width]),
        sum_small[:, 9],
        wide(sum_mix[:, 3 * model_width : 5 * model_width]),
        sum_small[:, 10],
        wide(sum_mix[:, model_width : 2 * model_width]),
        sum_small[:, 11],
        wide(sum_up),
        sum_small[:, 13:17].reshape(-1),
        wide(sum_down.reshape(4 * HD, model_width)),
        sum_small[:, 12],
    )


def solution(mesh):
    placed = (
        P("fsdp", "seq", None),
        P("fsdp", None),
        P("fsdp", None, None),
        P("fsdp"),
        P("fsdp", None),
        P("fsdp"),
        P("fsdp"),
        P("fsdp", None),
        P("fsdp"),
        P("fsdp", None),
        P("fsdp"),
        P("fsdp", None),
        P("fsdp"),
        P("fsdp", None),
        P("fsdp"),
        P("fsdp", None),
        P("fsdp"),
        P("fsdp", None),
        P("fsdp"),
        P("fsdp", "seq", None),
    )
    return jax.shard_map(
        on_device,
        mesh=mesh,
        in_specs=placed,
        out_specs=(
            P("fsdp", "seq", None),
            P("fsdp", "seq", None),
            P("fsdp", None),
            P("fsdp", None, None),
            P("fsdp"),
            P("fsdp", None),
            P("fsdp"),
            P("fsdp"),
            P("fsdp", None),
            P("fsdp"),
            P("fsdp", None),
            P("fsdp"),
            P("fsdp", None),
            P("fsdp"),
            P("fsdp", None),
            P("fsdp"),
            P("fsdp", None),
            P("fsdp"),
            P("fsdp", None),
            P("fsdp"),
        ),
        check_vma=False,
    )
```

time: 1450 us -> 566 us (0.39)
  waiting for transfers between devices: 971 us -> 15.2 us
  Pallas kernels: 0 us -> 337 us
  blocking collectives: 218 us -> 0 us
  other arithmetic: 44 us -> 14.5 us
    pallas_call x0 -> x4, Pallas kernels: none -> 337 us  [the longest x1 128 us: scatter_back(): pl.pallas_call(back_kernel, out_shape=(bf16(HD, up.shape[-1]), bf16(HD, h...]
    reduce_scatter x3 -> x1, waiting for transfers between devices: 321 us -> 0.01 us  [on_device(): lax.psum_scatter(down_grad.astype(jnp.bfloat16), 'fsdp', scatter_dimensio...]
    all_gather x7 -> x0, waiting for transfers between devices: 300 us -> none  [the longest x1 81 us: on_device(): lax.all_gather(up_weight, 'fsdp', axis=0, tiled=True)]
    unnamed x23 -> x1, waiting for transfers between devices: 298 us -> 0.02 us
    unnamed x3 -> x0, blocking collectives: 173 us -> none
    dot_general x14 -> x26, matrix products: 62.4 us -> 102 us  [project(): return jnp.dot(former, latter, preferred_element_type=jnp.float32)]
    psum x1 -> x0, waiting for transfers between devices: 36.9 us -> none  [reduce_bucket(): lax.psum(for_sending(owner_part), 'seq')]
    all_gather x1 -> x0, blocking collectives: 31.3 us -> none  [on_device(): lax.all_gather(caption_piece.astype(jnp.bfloat16), 'seq', axis=1, tiled=T...]
  transfers between devices with their start and end apart: 20 -> 9, of which waited for: 16 -> 1; matrix products, arithmetic and copies ran while one was open for 11% -> 23% of each run, Pallas kernels for 0% -> 23%
where the time goes in v2:
time: 566 us; the launch traced here: 558 us
  Pallas kernels  337 us (60%)
  matrix products  117 us (21%)
  local copies, waits for them, and re-layouts  51.4 us (9%)
  between operations  15.8 us (3%)
  waiting for transfers between devices  15.2 us (3%)
  other arithmetic  14.5 us (3%)
  starting transfers between devices  6.97 us (1%)
    pallas_call x1, Pallas kernels, scatter_back(): pl.pallas_call(back_kernel, out_shape=(bf16(HD, up.shape[-1]), bf16(HD, h...  128 us
    pallas_call x1, Pallas kernels, gather_late(): pl.pallas_call(late_kernel, out_shape=full_shapes(shards) + (bf16(8, 6, 1...  116 us
    dot_general x26, matrix products, project(): return jnp.dot(former, latter, preferred_element_type=jnp.float32)  102 us
    pallas_call x1, Pallas kernels, scatter_rest(): pl.pallas_call(rest_kernel, out_shape=(bf16(HD, 1024), bf16(HD, 1024), bf...  51 us
    pallas_call x1, Pallas kernels, gather_early(): pl.pallas_call(early_kernel, out_shape=full_shapes(shards), in_specs=[ANY...  41.5 us
    all_to_all x1, waiting for transfers between devices, on_device(): lax.all_to_all(text_partial[0].astype(jnp.bfloat16).reshape(8, text_piece...  15.2 us
  transfers between devices with their start and end apart: 9, of which 1 were waited for; matrix products, arithmetic and copies ran while one was open for 23% of the time, Pallas kernels for 23%

profile of v2, /device:TPU:0, one launch (start us, length us, event | category | flops | bytes accessed | tf_op | source)
XLA Modules:
  0.0 558.2 jit_solution(17776083484217098596)
XLA Ops:
  7.3 0.9 dynamic_update_slice.27
  15.0 1.0 copy-done.8
  16.1 41.5 %shard_map.347 = (bf16[4,2,2,72,3456]{4,3,2,1,0:T(8,128)(2,1)}, bf16[4,2,2,32,1152]{4,3,2,1,0:T(8,128)(2,1)S(1)}) custom-call(bf16[72,3456]{1,0:T(8,128)(2,1)S(1)} %copy-done.8, bf16[32,1152]{1,0:T(8,128)(2,1)S(1)} %reshape.614.small), custom_call_target="tpu_custom_call" | custom-call | tf_op jit(solution)/shard_map/pallas_call | solution.py:448
  60.3 4.8 fusion.packed
  65.2 116.0 %shard_map.348 = (bf16[4,2,2,72,4608]{4,3,2,1,0:T(8,128)(2,1)}, bf16[4,2,2,72,1152]{4,3,2,1,0:T(8,128)(2,1)}, bf16[4,2,2,72,2304]{4,3,2,1,0:T(8,128)(2,1)}, bf16...) custom-call(bf16[72,4608]{1,0:T(8,128)(2,1)S(1)} %copy-done.3, ...), custom_call_target="tpu_custom_call" | custom-call | tf_op jit(solution)/shard_map/pallas_call | solution.py:462
  181.2 3.3 fusion.47
  185.2 0.9 copy.123
  186.1 3.4 fusion.2
  189.6 0.9 copy.124
  190.5 0.9 copy.122
  191.4 1.5 fusion.85
  193.1 1.3 convolution_convert_fusion.11
  194.5 2.6 fusion.86
  198.1 6.0 %convolution_add_fusion = f32[128,4608]{1,0:T(8,128)S(1)} fusion(bf16[1152,4608]{1,0:T(8,128)(2,1)} %bitcast.238, f32[4608]{0:T(1024)S(1)} %add.329, f32[1,128,1152]{2,1,0:T(8,128)} %copy-done.14, f32[1152]{0:T(1024)S(1)} %get-tuple-element.83, f32[1152]{0:T(1024)S(1)} %get-tuple-element.84, f32[128]{0:T(128)S(1)} %fusion.77, f32[128]{0:T(128)S(1)} %broadcast_multiply_fusion), kind=kOutput, calls=%fused_computation.5 | convolution fusion | flops 1360281600 | bytes 13594624 | tf_op jit(solution)/shard_map/dot_general | solution.py:36
  204.2 1.5 copy-done.12
  205.6 6.1 %convolution_convert_fusion = bf16[4608,1152]{1,0:T(8,128)(2,1)} fusion(bf16[1,128,1152]{2,1,0:T(8,128)(2,1)S(1)} %copy-done.24, f32[1152]{0:T(1024)S(1)} %get-tuple-element.82, f32[128,4608]{1,0:T(8,128)S(1)} %convolution_add_fusion), kind=kOutput, calls=%fused_computation | convolution fusion | flops 1370013696 | bytes 13275648 | tf_op jit(solution)/shard_map/bli,blo->io/dot_general | solution.py:40
  211.7 10.3 %convert_reduce_fusion = (f32[4608]{0:T(1024)}, bf16[128,4608]{1,0:T(8,128)(2,1)}) fusion(f32[128,4608]{1,0:T(8,128)} %copy-done.12, bf16[4608,1152]{1,0:T(8,128)(2,1)} %bitcast.285, bf16[1,128,1152]{2,1,0:T(8,128)(2,1)} %param.39, f32[1152]{0:T(1024)S(1)} %get-tuple-element.82), kind=kOutput, calls=%fused_computation.40 | convolution fusion | flops 1372368384 | bytes 14473728 | tf_op jit(solution)/shard_map/dot_general | solution.py:36
  222.0 9.8 %fusion.87 = (f32[1152]{0:T(1024)}, f32[128,1152]{1,0:T(8,128)S(1)}) fusion(bf16[128,4608]{1,0:T(8,128)(2,1)} %get-tuple-element.132, bf16[1152,4608]{1,0:T(8,128)(2,1)} %bitcast.239), kind=kOutput, calls=%fused_computation.208 | convolution fusion | flops 1359100800 | bytes 12390912 | tf_op jit(solution)/shard_map/dot_general | solution.py:36
  231.8 1.6 fusion.41
  233.4 1.9 copy.126
  236.2 1.9 constant_dynamic-slice_fusion.8
  238.1 5.4 convolution_convert_fusion.1
  244.3 8.5 %convert_reduce_fusion.3 = (f32[1152]{0:T(1024)}, f32[1152]{0:T(1024)}, bf16[1,128,1152]{2,1,0:T(8,128)(2,1)}, f32[128]{0:T(128)S(1)}, f32[1,128,1152]{2,1,0:T(8,128)S(1)}) fusion(bf16[1,128,1152]{2,1,0:T(8,128)(2,1)S(1)} %copy-done.25, f32[1152]{0:T(1024)S(1)} %get-tuple-element.82, f32[1,128,1152]{2,1,0:T(8,128)S(1)} %copy-done.16, ...), kind=kOutput, calls=%fused_computation.98 | convolution fusion | flops 1366914688 | bytes 15360512 | tf_op jit(solution)/shard_map/dot_general | solution.py:36
  253.6 1.6 convolution_convert_fusion.8
  255.2 1.8 copy.125
  257.1 1.6 multiply_reduce_fusion
  259.7 1.2 fusion.25
  260.8 2.1 copy.129
  262.9 2.4 concatenate.58
  265.4 2.1 fusion.24
  267.5 2.2 copy.130
  269.7 1.7 concatenate.59
  271.4 1.8 pad_maximum_fusion
  273.2 4.2 all-to-all-start
  278.2 2.1 convert_reduce_fusion.5
  280.3 15.2 %all-to-all-done = bf16[8,15,2304]{2,1,0:T(8,128)(2,1)} async-done(((bf16[8,15,2304]{2,1,0:T(8,128)(2,1)}), bf16[8,15,2304]{2,1,0:T(8,128)(2,1)}, u32[]{:S(2)}, u32[]{:S(2)}) %all-to-all-start) | async-done | bytes 552992 | tf_op jit(solution)/shard_map/all_to_all | solution.py:920
  295.4 1.2 reduce_sum.262
  296.6 2.4 convolution_convert_fusion.3
  299.1 3.0 convert_reduce_fusion.6
  302.1 1.6 convolution_convert_fusion.6
  305.1 1.8 constant_dynamic-slice_fusion.3
  306.9 1.6 convolution_convert_fusion.5
  308.5 1.6 convolution_convert_fusion.4
  314.7 1.4 concatenate.71
  316.1 1.9 copy.140
  318.1 2.7 convolution_convert_fusion.7.grad_rows
  320.8 1.8 fusion.19
  322.7 1.9 fusion.20
  324.6 1.9 fusion.21
  326.5 2.8 fusion.3
  329.5 9.0 %add_convert_fusion = bf16[576,4608]{1,0:T(8,128)(2,1)} fusion(bf16[576,4608]{1,0:T(8,128)(2,1)} %collective-permute-done, bf16[576,128]{1,0:T(8,128)(2,1)S(1)} %bitcast.272, bf16[128,4608]{1,0:T(8,128)(2,1)S(1)} %copy-done.19), kind=kOutput, calls=%fused_computation.1 | convolution fusion | flops 687439872 | bytes 11943936 | tf_op jit(solution)/shard_map/dot_general | solution.py:36
  338.5 128.3 %shard_map.349 = (bf16[72,4608]{1,0:T(8,128)(2,1)S(1)}, bf16[72,3072]{1,0:T(8,128)(2,1)S(1)}, bf16[72,3072]{1,0:T(8,128)(2,1)S(1)}, bf16[128,3456]{1,0:T(8,128)(2,1)S(1)}) custom-call(bf16[4,2,72,4608]{3,2,1,0:T(8,128)(2,1)} %bitcast.240, bf16[4,2,72,6144]{3,2,1,0:T(8,128)(2,1)} %bitcast.244, bf16[8,6,128,72]{3,2,1,0:T(8,128)(2,1)S(1)} %get-tuple-element.47.heads, ...), custom_call_target="tpu_custom_call" | custom-call | tf_op jit(solution)/shard_map/pallas_call | solution.py:692
  466.9 2.6 fusion.38
  470.0 1.2 fusion.42
  471.2 1.2 copy.131
  473.1 3.1 convolution_convert_fusion.2
  476.2 4.0 convolution_convert_fusion.9
  484.0 1.0 slice_convert_fusion.2
  486.0 1.2 convert_element_type.336
  487.4 5.2 add_convert_fusion.1
  492.7 1.1 copy-done.7
  493.7 51.0 %shard_map.350 = (bf16[72,1024]{1,0:T(8,128)(2,1)S(1)}, bf16[72,1024]{1,0:T(8,128)(2,1)S(1)}, bf16[72,1536]{1,0:T(8,128)(2,1)S(1)}, bf16[4,72,1152]{2,1,0:T(8,12...) custom-call(bf16[4,2,72,3456]{3,2,1,0:T(8,128)(2,1)} %bitcast.241, ...), custom_call_target="tpu_custom_call" | custom-call | tf_op jit(solution)/shard_map/pallas_call | solution.py:762
  545.7 1.2 bitcast_convert_fusion
  549.9 1.0 maximum_convert_fusion
  (258 shorter events, 31.7 us)
Async XLA Ops:
  7.2 178.9 %copy-start = (bf16[1,120,1152]{2,1,0:T(8,128)(2,1)S(1)}, bf16[1,120,1152]{2,1,0:T(8,128)(2,1)}, u32[]{:S(2)}) copy-start(bf16[1,120,1152]{2,1,0:T(8,128)(2,1)} %param.22) | copy-start | bytes 829444
  7.2 52.1 %copy-start.11 = (bf16[1,128,1152]{2,1,0:T(8,128)(2,1)S(1)}, bf16[1,128,1152]{2,1,0:T(8,128)(2,1)}, u32[]{:S(2)}) copy-start(bf16[1,128,1152]{2,1,0:T(8,128)(2,1)} %param.20) | copy-start | bytes 884740
  7.2 485.4 %reduce-scatter.2.cloned.1.call-start = ((), (), s32[]{:S(2)}) async-start(), calls=%async_computation.2 | async-start | bytes 11280384 | tf_op jit(solution)/shard_map/reduce_scatter | solution.py:898
  16.1 43.7 %copy-start.40 = (bf16[72,1152]{1,0:T(8,128)(2,1)S(1)}, bf16[72,1152]{1,0:T(8,128)(2,1)}, u32[]{:S(2)}) copy-start(bf16[72,1152]{1,0:T(8,128)(2,1)} %param.33) | copy-start | bytes 497668
  16.1 43.7 %copy-start.41 = (bf16[72,1152]{1,0:T(8,128)(2,1)S(1)}, bf16[72,1152]{1,0:T(8,128)(2,1)}, u32[]{:S(2)}) copy-start(bf16[72,1152]{1,0:T(8,128)(2,1)} %param.27) | copy-start | bytes 497668
  59.3 5.8 %copy-start.43 = (f32[1152]{0:T(1024)}, f32[1152]{0:T(1024)S(1)}, u32[]{:S(2)}) copy-start(f32[1152]{0:T(1024)S(1)} %get-tuple-element.85) | copy-start | bytes 13828
  59.3 135.1 %copy-start.45 = (f32[1152]{0:T(1024)}, f32[1152]{0:T(1024)S(1)}, u32[]{:S(2)}) copy-start(f32[1152]{0:T(1024)S(1)} %get-tuple-element.87) | copy-start | bytes 13828
  59.5 5.7 %copy-start.59 = (f32[128]{0:T(128)}, f32[128]{0:T(128)S(1)}, u32[]{:S(2)}) copy-start(f32[128]{0:T(128)S(1)} %broadcast_multiply_fusion.1) | copy-start | bytes 1540
  59.8 5.4 copy-start.54
  60.2 4.9 copy-start.3
  60.3 4.9 copy-start.4
  60.3 4.9 copy-start.9
  60.3 4.9 copy-start.10
  181.2 3.3 copy-start.17
  184.6 5.0 copy-start.32
  194.4 3.6 copy-start.34
  198.1 7.5 %copy-start.24 = (bf16[1,128,1152]{2,1,0:T(8,128)(2,1)S(1)}, bf16[1,128,1152]{2,1,0:T(8,128)(2,1)}, u32[]{:S(2)}) copy-start(bf16[1,128,1152]{2,1,0:T(8,128)(2,1)} %param.39) | copy-start | bytes 884740
  222.0 9.8 %copy-start.15 = (f32[1,128,1152]{2,1,0:T(8,128)S(1)}, f32[1,128,1152]{2,1,0:T(8,128)}, u32[]{:S(2)}) copy-start(f32[1,128,1152]{2,1,0:T(8,128)} %copy-done.14) | copy-start | bytes 1769476
  238.1 6.2 %copy-start.13 = (f32[128,4608]{1,0:T(8,128)S(1)}, f32[128,4608]{1,0:T(8,128)}, u32[]{:S(2)}) copy-start(f32[128,4608]{1,0:T(8,128)} %copy-done.12) | copy-start | bytes 7077892
  238.1 6.2 %copy-start.16 = (f32[1,128,1152]{2,1,0:T(8,128)S(1)}, f32[1,128,1152]{2,1,0:T(8,128)}, u32[]{:S(2)}) copy-start(f32[1,128,1152]{2,1,0:T(8,128)} %copy-done.14) | copy-start | bytes 1769476
  238.1 6.2 %copy-start.25 = (bf16[1,128,1152]{2,1,0:T(8,128)(2,1)S(1)}, bf16[1,128,1152]{2,1,0:T(8,128)(2,1)}, u32[]{:S(2)}) copy-start(bf16[1,128,1152]{2,1,0:T(8,128)(2,1)} %param.39) | copy-start | bytes 884740
  238.1 6.2 %copy-start.31 = (f32[128,1152]{1,0:T(8,128)S(1)}, f32[128,1152]{1,0:T(8,128)}, u32[]{:S(2)}) copy-start(f32[128,1152]{1,0:T(8,128)} %copy-done.30) | copy-start | bytes 1769476
  238.1 6.2 %copy-start.63 = (f32[1152]{0:T(1024)S(1)}, f32[1152]{0:T(1024)}, u32[]{:S(2)}) copy-start(f32[1152]{0:T(1024)} %get-tuple-element.66) | copy-start | bytes 13828
  238.1 15.5 %slice-start.2 = ((s8[5308416]{0:T(1024)(128)(4,1)}), s8[4194304]{0:T(1024)(128)(4,1)S(1)}, s32[]{:S(2)}) async-start(s8[5308416]{0:T(1024)(128)(4,1)} %bitcast.260), calls=%async_computation.5 | async-start | bytes 8388608
  243.5 85.9 %collective-permute-start = (bf16[576,4608]{1,0:T(8,128)(2,1)}, bf16[576,4608]{1,0:T(8,128)(2,1)}, u32[]{:S(2)}, u32[]{:S(2)}) collective-permute-start(bf16[576,4608]{1,0:T(8,128)(2,1)} %convolution_convert_fusion.1), channel_id=1, source_target_pairs={{0,1},{1,0},{2,3},{3,2},{4,5},{5,4},{6,7},{7,6},{8,9},{9,8},{10,11... | collective-permute-start | bytes 15925256 | tf_op jit(solution)/shard_map/ppermute | solution.py:796
  244.3 9.3 %slice-start.3 = ((s8[5308416]{0:T(1024)(128)(4,1)}), s8[1114112]{0:T(1024)(128)(4,1)S(1)}, s32[]{:S(2)}) async-start(s8[5308416]{0:T(1024)(128)(4,1)} %bitcast.260), calls=%async_computation.6 | async-start | bytes 2228224
  267.5 10.7 %copy-start.22 = (bf16[16,128,120]{1,2,0:T(8,128)(2,1)S(1)}, bf16[16,128,120]{1,2,0:T(8,128)(2,1)}, u32[]{:S(2)}) copy-start(bf16[16,128,120]{1,2,0:T(8,128)(2,1)} %copy-done.21) | copy-start | bytes 1474564
  273.2 22.2 %all-to-all-start = ((bf16[8,15,2304]{2,1,0:T(8,128)(2,1)}), bf16[8,15,2304]{2,1,0:T(8,128)(2,1)}, u32[]{:S(2)}, u32[]{:S(2)}) async-start(bf16[8,15,2304]{2,1,0:T(8,128)(2,1)} %pad_maximum_fusion), calls=%async_computation | async-start | bytes 1179648 | tf_op jit(solution)/shard_map/all_to_all | solution.py:920
  277.4 21.6 %copy-start.46 = (f32[1152]{0:T(1024)S(1)}, f32[1152]{0:T(1024)}, u32[]{:S(2)}) copy-start(f32[1152]{0:T(1024)} %copy-done.45) | copy-start | bytes 13828
  277.4 21.6 %copy-start.65 = (f32[128]{0:T(128)S(1)}, f32[128]{0:T(128)}, u32[]{:S(2)}) copy-start(f32[128]{0:T(128)} %copy-done.64) | copy-start | bytes 1540
  299.0 3.0 copy-start.38
  299.0 27.4 %collective-permute-start.4 = (bf16[576,2304]{1,0:T(8,128)(2,1)}, bf16[576,2304]{1,0:T(8,128)(2,1)}, u32[]{:S(2)}, u32[]{:S(2)}) collective-permute-start(bf16[576,2304]{1,0:T(8,128)(2,1)} %convolution_convert_fusion.3), channel_id=1, source_target_pairs={{0,1},{1,0},{2,3},{3,2},{4,5},{5,4},{6,7},{7,6},{8,9},{9,8},{10,11... | collective-permute-start | bytes 7962632 | tf_op jit(solution)/shard_map/ppermute | solution.py:796
  299.1 5.1 copy-start.33
  303.7 17.1 %collective-permute-start.1 = (bf16[576,1152]{1,0:T(8,128)(2,1)}, bf16[576,1152]{1,0:T(8,128)(2,1)}, u32[]{:S(2)}, u32[]{:S(2)}) collective-permute-start(bf16[576,1152]{1,0:T(8,128)(2,1)} %convolution_convert_fusion.6), channel_id=1, source_target_pairs={{0,1},{1,0},{2,3},{3,2},{4,5},{5,4},{6,7},{7,6},{8,9},{9,8},{10,11... | collective-permute-start | bytes 3981320 | tf_op jit(solution)/shard_map/ppermute | solution.py:796
  304.1 6.7 %copy-start.62 = (f32[1152]{0:T(1024)S(1)}, f32[1152]{0:T(1024)}, u32[]{:S(2)}) copy-start(f32[1152]{0:T(1024)} %get-tuple-element.65) | copy-start | bytes 13828
  304.1 7.3 %copy-start.48 = (f32[1152]{0:T(1024)S(1)}, f32[1152]{0:T(1024)}, u32[]{:S(2)}) copy-start(f32[1152]{0:T(1024)} %get-tuple-element.58) | copy-start | bytes 13828
  304.1 7.9 %copy-start.52 = (f32[1152]{0:T(1024)S(1)}, f32[1152]{0:T(1024)}, u32[]{:S(2)}) copy-start(f32[1152]{0:T(1024)} %get-tuple-element.127) | copy-start | bytes 13828
  304.1 9.2 %copy-start.49 = (f32[1152]{0:T(1024)S(1)}, f32[1152]{0:T(1024)}, u32[]{:S(2)}) copy-start(f32[1152]{0:T(1024)} %get-tuple-element.88) | copy-start | bytes 13828
  304.2 9.9 %copy-start.61 = (f32[1152]{0:T(1024)S(1)}, f32[1152]{0:T(1024)}, u32[]{:S(2)}) copy-start(f32[1152]{0:T(1024)} %get-tuple-element.64) | copy-start | bytes 13828
  304.2 10.6 %copy-start.53 = (f32[4608]{0:T(1024)S(1)}, f32[4608]{0:T(1024)}, u32[]{:S(2)}) copy-start(f32[4608]{0:T(1024)} %get-tuple-element.131) | copy-start | bytes 55300
  308.5 14.2 %collective-permute-start.2 = (bf16[576,1152]{1,0:T(8,128)(2,1)}, bf16[576,1152]{1,0:T(8,128)(2,1)}, u32[]{:S(2)}, u32[]{:S(2)}) collective-permute-start(bf16[576,1152]{1,0:T(8,128)(2,1)} %convolution_convert_fusion.5), channel_id=1, source_target_pairs={{0,1},{1,0},{2,3},{3,2},{4,5},{5,4},{6,7},{7,6},{8,9},{9,8},{10,11... | collective-permute-start | bytes 3981320 | tf_op jit(solution)/shard_map/ppermute | solution.py:796
  310.1 10.7 %copy-start.37 = (bf16[8,1,72,128]{3,2,1,0:T(8,128)(2,1)S(1)}, bf16[8,1,72,128]{3,2,1,0:T(8,128)(2,1)}, u32[]{:S(2)}) copy-start(bf16[8,1,72,128]{3,2,1,0:T(8,128)(2,1)} %get-tuple-element.112) | copy-start | bytes 442372
  310.1 14.5 %collective-permute-start.3 = (bf16[576,1152]{1,0:T(8,128)(2,1)}, bf16[576,1152]{1,0:T(8,128)(2,1)}, u32[]{:S(2)}, u32[]{:S(2)}) collective-permute-start(bf16[576,1152]{1,0:T(8,128)(2,1)} %convolution_convert_fusion.4), channel_id=1, source_target_pairs={{0,1},{1,0},{2,3},{3,2},{4,5},{5,4},{6,7},{7,6},{8,9},{9,8},{10,11... | collective-permute-start | bytes 3981320 | tf_op jit(solution)/shard_map/ppermute | solution.py:796
  318.1 4.6 copy-start.39
  326.5 3.0 copy-start.19
  326.5 3.0 copy-start.35
  326.5 140.4 %slice-start = ((s8[7962624]{0:T(1024)(128)(4,1)}), s8[4194304]{0:T(1024)(128)(4,1)S(1)}, s32[]{:S(2)}) async-start(s8[7962624]{0:T(1024)(128)(4,1)} %bitcast.235), calls=%async_computation.3 | async-start | bytes 8388608
  329.4 9.1 %copy-start.20 = (bf16[576,6144]{1,0:T(8,128)(2,1)}, bf16[576,6144]{1,0:T(8,128)(2,1)S(1)}, u32[]{:S(2)}) copy-start(bf16[576,6144]{1,0:T(8,128)(2,1)S(1)} %broadcast_dynamic-update-slice_fusion) | copy-start | bytes 21233668
  329.5 137.4 %slice-start.1 = ((s8[7962624]{0:T(1024)(128)(4,1)}), s8[3768320]{0:T(1024)(128)(4,1)S(1)}, s32[]{:S(2)}) async-start(s8[7962624]{0:T(1024)(128)(4,1)} %bitcast.235), calls=%async_computation.4 | async-start | bytes 7536640
  338.5 128.4 %copy-start.60 = (f32[128]{0:T(128)S(1)}, f32[128]{0:T(128)}, u32[]{:S(2)}) copy-start(f32[128]{0:T(128)} %copy-done.59) | copy-start | bytes 1540
  466.8 2.7 copy-start.1
  466.9 3.0 copy-start.28
  466.9 3.0 copy-start.29
  466.9 3.0 copy-start.44
  476.1 4.3 copy-start.56
  476.2 4.3 copy-start.57
  476.2 4.3 copy-start.58
  476.2 11.2 %collective-permute-start.5 = (bf16[576,3456]{1,0:T(8,128)(2,1)}, bf16[576,3456]{1,0:T(8,128)(2,1)}, u32[]{:S(2)}, u32[]{:S(2)}) collective-permute-start(bf16[576,3456]{1,0:T(8,128)(2,1)} %convolution_convert_fusion.2), channel_id=1, source_target_pairs={{0,1},{1,0},{2,3},{3,2},{4,5},{5,4},{6,7},{7,6},{8,9},{9,8},{10,11... | collective-permute-start | bytes 11943944 | tf_op jit(solution)/shard_map/ppermute | solution.py:796
  480.2 2.9 copy-start.51
  480.2 2.9 copy-start.42
  480.2 3.8 copy-start.2
  481.1 5.0 copy-start.6
  483.2 4.0 collective-permute-start.6
  484.0 3.4 copy-start.36
  (17 other events, 28.9 us)
Sparse Core Ops, SparseCore 0:
  211.8 116.6 reduce-scatter.1

commit v3 on v2

--- a/solution.py
+++ b/solution.py
@@ -36,10 +36,6 @@
     return jnp.dot(former, latter, preferred_element_type=jnp.float32)
 
 
-def weight_grad(former, latter):
-    return jnp.einsum("bli,blo->io", former, latter, preferred_element_type=jnp.float32)
-
-
 def token_sum(values):
     return jnp.sum(values.astype(jnp.float32), axis=(0, 1))
 
@@ -59,29 +55,6 @@
     weights = (exponent / partition).astype(jnp.bfloat16)
     output = jnp.einsum("hqk,khd->qhd", weights, values, preferred_element_type=jnp.float32)
     return (output.astype(jnp.bfloat16), largest + jnp.log(partition))
-
-
-def attend_backward(queries, key_rows, values, logsum, grad_out):
-    factor = HD ** (-0.5)
-    scores = (
-        jnp.einsum("qhd,khd->hqk", queries, key_rows, preferred_element_type=jnp.float32) * factor
-    )
-    weights = jnp.exp(scores - logsum)
-    grad_weights = jnp.einsum("qhd,khd->hqk", grad_out, values, preferred_element_type=jnp.float32)
-    inner = jnp.sum(weights * grad_weights, axis=-1, keepdims=True)
-    grad_scores = (weights * (grad_weights - inner)).astype(jnp.bfloat16)
-    grad_q = (
-        jnp.einsum("hqk,khd->qhd", grad_scores, key_rows, preferred_element_type=jnp.float32)
-        * factor
-    )
-    grad_k = (
-        jnp.einsum("hqk,qhd->khd", grad_scores, queries, preferred_element_type=jnp.float32)
-        * factor
-    )
-    grad_v = jnp.einsum(
-        "hqk,qhd->khd", weights.astype(jnp.bfloat16), grad_out, preferred_element_type=jnp.float32
-    )
-    return (grad_q, grad_k, grad_v)
 
 
 def place():
@@ -297,11 +270,13 @@
     copies.finish()
 
 
+PAIR = 2 * HD
+
+
 def head_slices(rows):
-    for j in range(rows.shape[1] // (16 * HD)):
-        for h in range(16):
-            at = j * 16 * HD + h * HD
-            yield h // 2, 2 * j + h % 2, at
+    for j in range(rows.shape[1] // (8 * PAIR)):
+        for to in range(8):
+            yield to, pl.ds(j * PAIR, PAIR), pl.ds((j * 8 + to) * PAIR, PAIR)
 
 
 def exchange(copies, name, seq, peers, sent, got, local):
@@ -333,54 +308,92 @@
 CHUNK = 256
 
 
+def head(which, h):
+    return pl.ds(which * PAIR + h * HD, HD)
+
+
 def attend(heads, h, out):
     tokens = 8 * 128
-    keys = heads[:, 2 + h].reshape(tokens, HD)
-    values = heads[:, 4 + h].reshape(tokens, HD)
+    keys = heads[:, :, head(1, h)].reshape(tokens, HD)
+    values = heads[:, :, head(2, h)].reshape(tokens, HD)
 
     @pl.loop(0, tokens // CHUNK)
     def _(i):
-        queries = heads[pl.ds(i * 2, 2), h].reshape(CHUNK, HD)
+        queries = heads[pl.ds(i * 2, 2), :, head(0, h)].reshape(CHUNK, HD)
         scores = lax.dot_general(
             queries, keys, (((1,), (1,)), ((), ())), preferred_element_type=jnp.float32
         ) * (HD**-0.5)
         exponent = jnp.exp(scores - jnp.max(scores, axis=1, keepdims=True))
         weights = exponent * (1.0 / jnp.sum(exponent, axis=1, keepdims=True))
         got = jnp.dot(weights.astype(jnp.bfloat16), values, preferred_element_type=jnp.float32)
-        out[pl.ds(i * 2, 2), h] = got.astype(jnp.bfloat16).reshape(2, 128, HD)
+        out[pl.ds(i * 2, 2), :, head(0, h)] = got.astype(jnp.bfloat16).reshape(2, 128, HD)
+
+
+def head_back(queries, keys, values, grad, mask):
+    across = (((1,), (1,)), ((), ()))
+    scores = lax.dot_general(keys, queries, across, preferred_element_type=jnp.float32)
+    scores = scores * (HD**-0.5) if mask is None else scores * (HD**-0.5) + mask
+    exponent = jnp.exp(scores - jnp.max(scores, axis=0, keepdims=True))
+    weights = exponent * (1.0 / jnp.sum(exponent, axis=0, keepdims=True))
+    grad_weights = lax.dot_general(values, grad, across, preferred_element_type=jnp.float32)
+    inner = jnp.sum(weights * grad_weights, axis=0, keepdims=True)
+    grad_scores = (weights * (grad_weights - inner)).astype(jnp.bfloat16)
+    grad_q = lax.dot_general(
+        grad_scores, keys, (((0,), (0,)), ((), ())), preferred_element_type=jnp.float32
+    ) * (HD**-0.5)
+    return weights.astype(jnp.bfloat16), grad_scores, grad_q.astype(jnp.bfloat16)
 
 
 def attend_back(heads, grads, h, out, key_sum, value_sum):
     tokens = 8 * 128
-    keys = heads[:, 2 + h].reshape(tokens, HD)
-    values = heads[:, 4 + h].reshape(tokens, HD)
+    keys = heads[:, :, head(1, h)].reshape(tokens, HD)
+    values = heads[:, :, head(2, h)].reshape(tokens, HD)
     key_sum[...] = jnp.zeros_like(key_sum)
     value_sum[...] = jnp.zeros_like(value_sum)
-    across = (((1,), (1,)), ((), ()))
 
     @pl.loop(0, tokens // CHUNK)
     def _(i):
-        queries = heads[pl.ds(i * 2, 2), h].reshape(CHUNK, HD)
-        grad = grads[pl.ds(i * 2, 2), h].reshape(CHUNK, HD)
-        scores = lax.dot_general(
-            keys, queries, across, preferred_element_type=jnp.float32
-        ) * (HD**-0.5)
-        exponent = jnp.exp(scores - jnp.max(scores, axis=0, keepdims=True))
-        weights = exponent * (1.0 / jnp.sum(exponent, axis=0, keepdims=True))
-        grad_weights = lax.dot_general(values, grad, across, preferred_element_type=jnp.float32)
-        inner = jnp.sum(weights * grad_weights, axis=0, keepdims=True)
-        grad_scores = (weights * (grad_weights - inner)).astype(jnp.bfloat16)
-        value_sum[...] += jnp.dot(
-            weights.astype(jnp.bfloat16), grad, preferred_element_type=jnp.float32
+        queries = heads[pl.ds(i * 2, 2), :, head(0, h)].reshape(CHUNK, HD)
+        grad = grads[pl.ds(i * 2, 2), :, head(0, h)].reshape(CHUNK, HD)
+        weights, grad_scores, grad_q = head_back(queries, keys, values, grad, None)
+        value_sum[...] += project(weights, grad)
+        key_sum[...] += project(grad_scores, queries)
+        out[pl.ds(i * 2, 2), :, head(0, h)] = grad_q.reshape(2, 128, HD)
+
+    out[:, :, head(1, h)] = (key_sum[...] * (HD**-0.5)).astype(jnp.bfloat16).reshape(8, 128, HD)
+    out[:, :, head(2, h)] = value_sum[...].astype(jnp.bfloat16).reshape(8, 128, HD)
+
+
+def cross_kernel(queries, text, grad_out, weight, grad_queries, grad_text, *, real):
+    grad = lax.dot_general(
+        grad_out[...], weight[...], (((1,), (1,)), ((), ())), preferred_element_type=jnp.float32
+    ).astype(jnp.bfloat16)
+    rows = lax.broadcasted_iota(jnp.int32, (text.shape[0], queries.shape[0]), 0)
+    mask = jnp.where(rows < real, 0.0, -1e30)
+    width = queries.shape[1]
+    for h in range(width // HD):
+        mine, values = pl.ds(h * HD, HD), pl.ds(width + h * HD, HD)
+        slopes = grad[:, h * HD : (h + 1) * HD]
+        weights, grad_scores, grad_q = head_back(
+            queries[:, mine], text[:, mine], text[:, values], slopes, mask
         )
-        key_sum[...] += jnp.dot(grad_scores, queries, preferred_element_type=jnp.float32)
-        grad_q = lax.dot_general(
-            grad_scores, keys, (((0,), (0,)), ((), ())), preferred_element_type=jnp.float32
-        ) * (HD**-0.5)
-        out[pl.ds(i * 2, 2), h] = grad_q.astype(jnp.bfloat16).reshape(2, 128, HD)
-
-    out[:, 2 + h] = (key_sum[...] * (HD**-0.5)).astype(jnp.bfloat16).reshape(8, 128, HD)
-    out[:, 4 + h] = value_sum[...].astype(jnp.bfloat16).reshape(8, 128, HD)
+        grad_queries[:, mine] = grad_q
+        grad_key = project(grad_scores, queries[:, mine]) * (HD**-0.5)
+        grad_text[:, mine] = grad_key.astype(jnp.bfloat16)
+        grad_text[:, values] = project(weights, slopes).astype(jnp.bfloat16)
+
+
+def cross_back(queries, text, grad_out, weight):
+    real = text.shape[0]
+    text = jnp.pad(text, ((0, -real % 128), (0, 0)))
+    bf16 = lambda like: jax.ShapeDtypeStruct(like.shape, jnp.bfloat16)
+    return pl.pallas_call(
+        functools.partial(cross_kernel, real=real),
+        out_shape=(bf16(queries), bf16(text)),
+        in_specs=[ON_CHIP] * 4,
+        out_specs=(ON_CHIP,) * 2,
+        compiler_params=pltpu.CompilerParams(vmem_limit_bytes=48 * 1024 * 1024),
+    )(queries, text, grad_out, weight)
 
 
 def late_kernel(
@@ -402,7 +415,7 @@
     seq, peers = seq_peers()
     greet(unique(work.x, work.y, work.z, work.c, [work.sibling]))
     for to, what, at in head_slices(packed):
-        sent[to, what] = packed[:, at : at + HD]
+        sent[to, :, what] = packed[:, at]
     own = exchange(copies, "in", seq, peers, sent, heads, local.at[6])
     work.first()
     exchanged(copies, "in", seq, peers, heads, own)
@@ -416,7 +429,7 @@
     work.fourth()
     exchanged(copies, "out", seq, peers, joined, own)
     for at, what, to in head_slices(o_rows):
-        o_rows[:, to : to + HD] = joined[at, what]
+        o_rows[:, to] = joined[at, :, what]
     work.last()
     keep.wait()
     copies.finish()
@@ -461,11 +474,11 @@
     vmem = lambda *shape: pltpu.VMEM(shape, jnp.bfloat16)
     outs = pl.pallas_call(
         late_kernel,
-        out_shape=full_shapes(shards) + (bf16(8, 6, 128, HD), bf16(128, 16 * HD)),
+        out_shape=full_shapes(shards) + (bf16(8, 128, 3 * PAIR), bf16(128, 8 * PAIR)),
         in_specs=[ANYWHERE] * 5 + [ON_CHIP],
         out_specs=(ANYWHERE,) * 6 + (ON_CHIP,),
         scratch_shapes=[
-            vmem(8, 6, 128, HD), vmem(8, 6, 128, HD), vmem(8, 2, 128, HD), vmem(8, 2, 128, HD),
+            vmem(8, 128, 3 * PAIR), vmem(8, 128, 3 * PAIR), vmem(8, 128, PAIR), vmem(8, 128, PAIR),
         ]
         + semaphores(9, 256, 256),
         compiler_params=parameters(1),
@@ -510,8 +523,8 @@
         return [
             vmem(4, 4, 2, HD, wy), vmem(4, 2, HD, wy), vmem(4, 2, HD, wy),
             vmem(2, HD, wy), vmem(4, HD, wy), vmem(1, HD, wy),
-            vmem(4, 2, HD, wz), vmem(2, HD, wz), vmem(4, 2, HD, wz // 4),
-            vmem(2, HD, wz // 4), vmem(4, HD, wz // 4), vmem(1, HD, wz // 4),
+            vmem(4, 2, HD, wz), vmem(2, HD, wz), vmem(4, 1, HD, wz // 2),
+            vmem(1, HD, wz // 2), vmem(4, 1, HD, wz // 8), vmem(1, HD, wz // 8),
             vmem(4, 4, HD, wx), vmem(4, HD, wx), vmem(4, 4, HD, wx // 4),
             vmem(4, HD, wx // 4), vmem(4, HD, wx // 4), vmem(1, HD, wx // 4),
         ]
@@ -519,15 +532,19 @@
     def first(self):
         u1, a1, m1 = self.scratch[0], self.scratch[6], self.scratch[12]
         up, up_at, up_size = self.by_y
-        mix, mix_at, mix_size = self.by_x
         for d in (1, 2, 3):
             to_x, to_y, to_z = step(self.x, d), step(self.y, d), step(self.z, d)
             cols = columns(to_y, up_size // 4, up_at)
             self.copies.push(("u1", d), up.at[:, :, :, cols], u1.at[d], self.along_y[d - 1])
-            cols = columns(to_x % 2, mix_size // 2, mix_at)
-            self.copies.push(
-                ("m1", d), mix.at[:, to_x // 2, :, cols], m1.at[d], self.along_x[d - 1]
-            )
+            at = 0
+            for n, (source, start, size) in enumerate(self.by_x):
+                self.copies.push(
+                    ("m1", n, d),
+                    source.at[:, to_x // 2, :, columns(to_x % 2, size // 2, start)],
+                    m1.at[d, :, :, pl.ds(at, size // 2)],
+                    self.along_x[d - 1],
+                )
+                at += size // 2
             at = 0
             for n, (source, start, size) in enumerate(self.by_z):
                 self.copies.push(
@@ -538,7 +555,13 @@
                 )
                 at += size
         self.keep(up.at[:, :, :, columns(self.y, up_size // 4, up_at)], u1.at[0])
-        self.keep(mix.at[:, self.xh, :, columns(self.xl, mix_size // 2, mix_at)], m1.at[0])
+        at = 0
+        for source, start, size in self.by_x:
+            self.keep(
+                source.at[:, self.xh, :, columns(self.xl, size // 2, start)],
+                m1.at[0, :, :, pl.ds(at, size // 2)],
+            )
+            at += size // 2
         at = 0
         for source, start, size in self.by_z:
             self.keep(
@@ -558,10 +581,15 @@
                 at += size
         add_up([a1.at[i] for i in range(4)], a1s)
         for d in (1, 2, 3):
-            cols = columns(step(self.y, d), a2.shape[-1])
-            self.copies.push(("a2", d), a1s.at[:, :, cols], a2.at[d], self.along_y[d - 1])
-        for d in (1, 2, 3):
-            self.copies.arrived(("m1", d), m1.at[d], self.along_x[3 - d])
+            to = step(self.x, d)
+            part = a1s.at[pl.ds(to // 2, 1), :, columns(to % 2, a2.shape[-1])]
+            self.copies.push(("a2", d), part, a2.at[d], self.along_x[d - 1])
+        for d in (1, 2, 3):
+            at = 0
+            for n, (_, _, size) in enumerate(self.by_x):
+                got = m1.at[d, :, :, pl.ds(at, size // 2)]
+                self.copies.arrived(("m1", n, d), got, self.along_x[3 - d])
+                at += size // 2
         add_up([m1.at[i] for i in range(4)], m1s)
         for d in (1, 2, 3):
             cols = columns(step(self.y, d), m2.shape[-1])
@@ -580,13 +608,12 @@
         a1s, a2, a2s, a3 = self.scratch[7:11]
         m1s, m2, m2s, m3 = self.scratch[13:17]
         for d in (1, 2, 3):
-            self.copies.arrived(("a2", d), a2.at[d], self.along_y[3 - d])
-        add_up(
-            [a1s.at[:, :, columns(self.y, a2.shape[-1])]] + [a2.at[d] for d in (1, 2, 3)], a2s
-        )
-        for d in (1, 2, 3):
-            to = step(self.x, d) // 2
-            self.copies.push(("a3", d), a2s.at[to], a3.at[d], self.along_x[d - 1])
+            self.copies.arrived(("a2", d), a2.at[d], self.along_x[3 - d])
+        mine = a1s.at[pl.ds(self.xh, 1), :, columns(self.xl, a2.shape[-1])]
+        add_up([mine] + [a2.at[d] for d in (1, 2, 3)], a2s)
+        for d in (1, 2, 3):
+            part = a2s.at[:, :, columns(step(self.y, d), a3.shape[-1])]
+            self.copies.push(("a3", d), part, a3.at[d], self.along_y[d - 1])
         for d in (1, 2, 3):
             self.copies.arrived(("m2", d), m2.at[d], self.along_y[3 - d])
         add_up(
@@ -605,36 +632,41 @@
         u2s, u3, u3s = self.scratch[3:6]
         a2s, a3, a3s = self.scratch[9:12]
         m2s, m3, m3s = self.scratch[15:18]
-        for name, line, sums, got, total, out, mine in (
-            ("a", self.along_x, a2s, a3, a3s, self.o_att, self.xh),
-            ("u", self.along_x, u2s, u3, u3s, self.o_up, self.xh),
-            ("m", self.along_z, m2s, m3, m3s, self.o_mix, self.z),
+        own = a2s.at[:, :, columns(self.y, a3.shape[-1])]
+        for name, line, own, got, total, out in (
+            ("a", self.along_y, own, [a3.at[d] for d in (1, 2, 3)], a3s, self.o_att),
+            ("u", self.along_x, u2s.at[pl.ds(self.xh, 1)],
+             [u3.at[pl.ds(d, 1)] for d in (1, 2, 3)], u3s, self.o_up),
+            ("m", self.along_z, m2s.at[pl.ds(self.z, 1)],
+             [m3.at[pl.ds(d, 1)] for d in (1, 2, 3)], m3s, self.o_mix),
         ):
             for d in (1, 2, 3):
-                self.copies.arrived((name + "3", d), got.at[d], line[3 - d])
-            add_up([sums.at[pl.ds(mine, 1)]] + [got.at[pl.ds(d, 1)] for d in (1, 2, 3)], total)
-            if name == "m":
-                spot = out.at[:, self.spot(self.seq)]
-                for e in range(1, 8):
-                    self.copies.push(("m4", e), total.at[0], spot, self.peers[e - 1])
-            else:
+                dst = a3.at[d] if name == "a" else (u3 if name == "u" else m3).at[d]
+                self.copies.arrived((name + "3", d), dst, line[3 - d])
+            add_up([own] + got, total)
+            if name == "u":
                 spot = out.at[:, columns(self.y, total.shape[-1])]
                 for d in (1, 2, 3):
-                    self.copies.push((name + "4", d), total.at[0], spot, self.along_y[d - 1])
+                    self.copies.push(("u4", d), total.at[0], spot, self.along_y[d - 1])
+            else:
+                spot = out.at[:, self.spot(self.seq, total)]
+                for e in range(1, 8):
+                    self.copies.push((name + "4", e), total.at[0], spot, self.peers[e - 1])
             self.keep(total.at[0], spot)
 
-    def spot(self, seq):
-        return columns((seq % 2) * 4 + seq // 2, self.scratch[17].shape[-1])
+    def spot(self, seq, total):
+        return columns((seq % 2) * 4 + seq // 2, total.shape[-1])
 
     def last(self):
         for d in (1, 2, 3):
-            from_y = step(self.y, -d)
-            for name, out in (("u4", self.o_up), ("a4", self.o_att)):
-                got = out.at[:, columns(from_y, out.shape[-1] // 4)]
-                self.copies.arrived((name, d), got, self.along_y[3 - d])
-        for e in range(1, 8):
-            got = self.o_mix.at[:, self.spot((self.seq + 8 - e) % 8)]
-            self.copies.arrived(("m4", e), got, self.peers[7 - e])
+            got = self.o_up.at[:, columns(step(self.y, -d), self.o_up.shape[-1] // 4)]
+            self.copies.arrived(("u4", d), got, self.along_y[3 - d])
+        for name, total, out in (
+            ("a4", self.scratch[11], self.o_att), ("m4", self.scratch[17], self.o_mix),
+        ):
+            for e in range(1, 8):
+                got = out.at[:, self.spot((self.seq + 8 - e) % 8, total)]
+                self.copies.arrived((name, e), got, self.peers[7 - e])
 
 
 class Stays:
@@ -658,15 +690,14 @@
 ):
     scratch, (local, send, recv) = rest[:18], rest[18:]
     copies, keep = Copies(send, recv), Stays(local)
-    half = mix.shape[-1] // 2
     work = Scatter(
-        (up, 0, up.shape[-1]), (mix, 0, half), [(mix, half, half)],
+        (up, 0, 2560), [(up, 2560, 2048), (mix, 0, 1024)], [(mix, 1024, 5120)],
         (o_up, o_mix, o_att), scratch, copies, keep,
     )
     seq, peers = seq_peers()
     greet(unique(work.x, work.y, work.z, work.c, []))
     for to, what, at in head_slices(grad_rows):
-        sent[to, what] = grad_rows[:, at : at + HD]
+        sent[to, :, what] = grad_rows[:, at]
     own = exchange(copies, "in", seq, peers, sent, grads, local.at[16])
     work.first()
     exchanged(copies, "in", seq, peers, grads, own)
@@ -678,7 +709,7 @@
     work.third()
     exchanged(copies, "out", seq, peers, joined, own)
     for at, what, to in head_slices(o_flat):
-        o_flat[:, to : to + HD] = joined[at, what]
+        o_flat[:, to] = joined[at, :, what]
     work.fourth()
     work.last()
     keep.wait()
@@ -686,22 +717,21 @@
 
 
 def scatter_back(up, mix, heads, grad_rows):
-    half = mix.shape[-1] // 2
     bf16 = lambda *shape: jax.ShapeDtypeStruct(shape, jnp.bfloat16)
     vmem = lambda *shape: pltpu.VMEM(shape, jnp.bfloat16)
     return pl.pallas_call(
         back_kernel,
         out_shape=(
-            bf16(HD, up.shape[-1]), bf16(HD, half), bf16(HD, half), bf16(128, 48 * HD),
+            bf16(HD, 2560), bf16(HD, 3072), bf16(HD, 5120), bf16(128, 24 * PAIR),
         ),
         in_specs=[ANYWHERE] * 2 + [ON_CHIP] * 2,
         out_specs=(ANYWHERE,) * 3 + (ON_CHIP,),
         scratch_shapes=[
-            vmem(8, 2, 128, HD), vmem(8, 2, 128, HD), vmem(8, 6, 128, HD), vmem(8, 6, 128, HD),
+            vmem(8, 128, PAIR), vmem(8, 128, PAIR), vmem(8, 128, 3 * PAIR), vmem(8, 128, 3 * PAIR),
             pltpu.VMEM((1024, HD), jnp.float32), pltpu.VMEM((1024, HD), jnp.float32),
         ]
-        + Scatter.buffers(up.shape[-1], half, half)
-        + semaphores(18, 64, 64),
+        + Scatter.buffers(2560, 3072, 5120)
+        + semaphores(18, 80, 80),
         compiler_params=parameters(2),
     )(up, mix, heads, grad_rows)
 
@@ -713,7 +743,7 @@
     scratch, (local, send, recv) = rest[:18], rest[18:]
     copies, keep = Copies(send, recv), Stays(local)
     work = Scatter(
-        (qkv, 0, 1024), (qkv, 1024, 1024), [(qkv, 2048, 1408), (small, 0, 128)],
+        (qkv, 0, 1536), [(qkv, 1536, 1024)], [(qkv, 2560, 896), (small, 0, 128)],
         (o_up, o_mix, o_att), scratch, copies, keep,
     )
     seq, peers, along_y = work.seq, work.peers, work.along_y
@@ -762,7 +792,7 @@
     return pl.pallas_call(
         rest_kernel,
         out_shape=(
-            bf16(HD, 1024), bf16(HD, 1024), bf16(HD, 1536), bf16(4, HD, width),
+            bf16(HD, 1536), bf16(HD, 1024), bf16(HD, 1024), bf16(4, HD, width),
             jax.ShapeDtypeStruct(mod.shape, jnp.float32), bf16(8, *cap.shape),
         ),
         in_specs=[ANYWHERE] * 5,
@@ -771,10 +801,71 @@
             vmem(4, HD, width), vmem(1, HD, width), vmem(1, HD, width), vmem(1, HD, width),
             vmem(8, *mod.shape),
         ]
-        + Scatter.buffers(1024, 1024, 1536)
-        + semaphores(18, 80, 80),
+        + Scatter.buffers(1536, 1024, 1024)
+        + semaphores(18, 96, 96),
         compiler_params=parameters(3),
     )(qkv, small, down, mod, cap)
+
+
+GELU = 0.7978845608028654
+CUBE = 0.044715
+
+
+def mlp_kernel(
+    rows, other, own, grad, up, down, bias, out, grad_rows, bias_grad, up_other, up_own, down_grad
+):
+    @pl.when(pl.program_id(0) == 0)
+    def _():
+        out[...] = jnp.zeros_like(out)
+        grad_rows[...] = jnp.zeros_like(grad_rows)
+
+    across = (((1,), (1,)), ((), ()))
+    hidden = project(rows[...], up[...]) + bias[...]
+    square = hidden * hidden
+    bend = jnp.tanh(GELU * (hidden + CUBE * hidden * square))
+    active = (0.5 * hidden * (1.0 + bend)).astype(jnp.bfloat16)
+    slope = 0.5 * (1.0 + bend) + 0.5 * hidden * (1.0 - bend * bend) * (
+        GELU * (1.0 + 3.0 * CUBE * square)
+    )
+    out[...] += project(active, down[...])
+    grad_act = lax.dot_general(grad[...], down[...], across, preferred_element_type=jnp.float32)
+    grad_hidden = grad_act * slope
+    rounded = grad_hidden.astype(jnp.bfloat16)
+    bias_grad[...] = jnp.sum(rounded.astype(jnp.float32), axis=0, keepdims=True)
+    grad_rows[...] += lax.dot_general(rounded, up[...], across, preferred_element_type=jnp.float32)
+    up_other[...] = project(other[...], rounded).astype(jnp.bfloat16)
+    up_own[...] = project(own[...], rounded).astype(jnp.bfloat16)
+    down_grad[...] = lax.dot_general(
+        active, grad[...], (((0,), (0,)), ((), ())), preferred_element_type=jnp.float32
+    ).astype(jnp.bfloat16)
+
+
+def mlp(rows, grad, up, down, bias):
+    tokens, width = rows.shape
+    units, size = up.shape[1], 512
+    own, other = by_core(rows.T)
+    fixed = lambda *shape: pl.BlockSpec(shape, lambda j: (0, 0))
+    wide = lambda n: pl.BlockSpec((n, size), lambda j: (0, j))
+    tall = pl.BlockSpec((size, width), lambda j: (j, 0))
+    f32 = lambda *shape: jax.ShapeDtypeStruct(shape, jnp.float32)
+    bf16 = lambda *shape: jax.ShapeDtypeStruct(shape, jnp.bfloat16)
+    return pl.pallas_call(
+        mlp_kernel,
+        grid=(units // size,),
+        out_shape=(
+            f32(tokens, width), f32(tokens, width), f32(1, units),
+            bf16(width // 2, units), bf16(width // 2, units), bf16(units, width),
+        ),
+        in_specs=[
+            fixed(tokens, width), fixed(width // 2, tokens), fixed(width // 2, tokens),
+            fixed(tokens, width), wide(width), tall, wide(1),
+        ],
+        out_specs=(
+            fixed(tokens, width), fixed(tokens, width), wide(1),
+            wide(width // 2), wide(width // 2), tall,
+        ),
+        compiler_params=pltpu.CompilerParams(vmem_limit_bytes=48 * 1024 * 1024),
+    )(rows, other, own, grad, up, down, bias)
 
 
 def sibling_pairs():
@@ -870,7 +961,7 @@
     text_kv = (project(caption, full_ckv) + kv_bias).astype(jnp.bfloat16)
     text_keys = by_heads(text_kv[..., :model_width])
     text_values = by_heads(text_kv[..., model_width:])
-    cross_heads, cross_logsum = jax.vmap(attend_forward)(
+    cross_heads, _ = jax.vmap(attend_forward)(
         by_heads(cross_rows), text_keys, text_values
     )
     crossed = cross_heads.reshape(latent_count, local_len, model_width)
@@ -878,60 +969,53 @@
     after_two = after_one + branch_two
     pre_two, pull_two = jax.vjp(modulate, after_two, shift_two, scale_two)
     normed_two = pre_two.astype(jnp.bfloat16)
-    hidden = project(normed_two, full_up) + full_ubias.astype(jnp.float32)
-    activated, gelu_pull = jax.vjp(jax.nn.gelu, hidden)
-    act_rows = activated.astype(jnp.bfloat16)
-    branch_three = project(act_rows, full_down) + full_dbias.astype(jnp.float32)
+    grad_out = cotangent.astype(jnp.float32)
+    grad_three = (gate_two * grad_out).astype(jnp.bfloat16)
+    product, grad_pre_two, up_bgrad, up_other, up_own, down_grad = mlp(
+        normed_two[0], grad_three[0], full_up, full_down, full_ubias.reshape(1, -1)
+    )
+    up_received = lax.ppermute(up_other, "fsdp", sibling_pairs())
+    down_part = lax.psum_scatter(down_grad, "fsdp", scatter_dimension=0, tiled=True)
+    branch_three = product[None] + full_dbias.astype(jnp.float32)
     block_out = (after_two + gate_two * branch_three).astype(jnp.bfloat16)
-    grad_out = cotangent.astype(jnp.float32)
     grad_gate_two = jnp.sum(grad_out * branch_three, axis=1, keepdims=True)
-    grad_three = (gate_two * grad_out).astype(jnp.bfloat16)
-    down_grad = weight_grad(act_rows, grad_three)
     down_bgrad = token_sum(grad_three)
-    grad_act = project(grad_three, full_down.T)
-    grad_hidden = gelu_pull(grad_act)[0].astype(jnp.bfloat16)
-    up_grad = pair_grad(normed_two[0], grad_hidden[0])
-    up_bgrad = token_sum(grad_hidden)
-    grad_pre_two = project(grad_hidden, full_up.T)
+    up_grad = (up_own.astype(jnp.float32) + up_received.astype(jnp.float32)).astype(jnp.bfloat16)
+    grad_pre_two = grad_pre_two[None]
     grad_mid_two, grad_shift_two, grad_scale_two = pull_two(grad_pre_two)
     grad_after_two = grad_out + grad_mid_two
-    down_part = lax.psum_scatter(
-        down_grad.astype(jnp.bfloat16), "fsdp", scatter_dimension=0, tiled=True
-    )
     grad_branch_two = grad_after_two.astype(jnp.bfloat16)
     cproj_grad = pair_grad(crossed[0], grad_branch_two[0])
     cproj_bgrad = token_sum(grad_branch_two)
-    grad_crossed = project(grad_branch_two, full_cproj.T).astype(jnp.bfloat16)
-    grad_cq, grad_ck, grad_cv = jax.vmap(attend_backward)(
-        by_heads(cross_rows), text_keys, text_values, cross_logsum, by_heads(grad_crossed)
-    )
-    grad_cross_rows = grad_cq.reshape(latent_count, local_len, model_width).astype(jnp.bfloat16)
+    grad_cross, grad_text = cross_back(
+        cross_rows[0], text_kv[0], grad_branch_two[0], full_cproj
+    )
+    grad_cross_rows = grad_cross[None]
     cquery_grad = pair_grad(middle[0], grad_cross_rows[0])
     cquery_bgrad = token_sum(grad_cross_rows)
     grad_after_one = grad_after_two + project(grad_cross_rows, full_cquery.T)
-    text_partial = jnp.concatenate(
-        [
-            grad_ck.reshape(grad_ck.shape[:2] + (model_width,)),
-            grad_cv.reshape(grad_cv.shape[:2] + (model_width,)),
-        ],
-        axis=-1,
-    )
-    text_piece = text_partial.shape[1] // 8
+    text_piece = grad_text.shape[0] // 8
     text_pieces = lax.all_to_all(
-        text_partial[0].astype(jnp.bfloat16).reshape(8, text_piece, -1), "seq", 0, 0
-    )
-    text_grad = jnp.sum(text_pieces.astype(jnp.float32), axis=0).astype(jnp.bfloat16)
-    caption_part = lax.dynamic_slice_in_dim(
-        caption[0], lax.axis_index("seq") * text_piece, text_piece, 0
-    )
-    ckv_grad = pair_grad(caption_part, text_grad)
-    cvalue_bgrad = jnp.sum(text_grad[:, model_width:].astype(jnp.float32), axis=0)
-    caption_piece = project(text_grad, full_ckv.T)
+        grad_text.reshape(8, text_piece, grad_text.shape[1]), "seq", 0, 0
+    )
     grad_gate_one = jnp.sum(grad_after_one * branch_one, axis=1, keepdims=True)
     grad_branch_one = (gate_one * grad_after_one).astype(jnp.bfloat16)
     proj_grad = pair_grad(tok_major[0], grad_branch_one[0])
     proj_bgrad = token_sum(grad_branch_one)
     grad_tok = project(grad_branch_one, full_proj.T).astype(jnp.bfloat16)
+    text_pieces, grad_tok, up_grad, proj_grad, cquery_grad, cproj_grad = (
+        lax.optimization_barrier(
+            (text_pieces, grad_tok, up_grad, proj_grad, cquery_grad, cproj_grad)
+        )
+    )
+    text_grad = jnp.sum(text_pieces.astype(jnp.float32), axis=0).astype(jnp.bfloat16)
+    caption_part = lax.dynamic_slice_in_dim(
+        jnp.pad(caption[0], ((0, grad_text.shape[0] - caption.shape[1]), (0, 0))),
+        lax.axis_index("seq") * text_piece, text_piece, 0
+    )
+    ckv_grad = pair_grad(caption_part, text_grad)
+    cvalue_bgrad = jnp.sum(text_grad[:, model_width:].astype(jnp.float32), axis=0)
+    caption_piece = project(text_grad, full_ckv.T)
     blocks = lambda grad: grad.reshape(4, 2, HD, -1)
     mix = jnp.concatenate(
         [proj_grad, cproj_grad, cquery_grad, ckv_grad, jnp.zeros((8 * HD, 384), jnp.bfloat16)],
@@ -940,7 +1024,9 @@
     sum_up, sum_mix, sum_att, flat = scatter_back(
         blocks(up_grad), blocks(mix), heads, grad_tok[0]
     )
-    sum_mix = jnp.concatenate([sum_mix, sum_att], axis=1)
+    up_one, mix_one, up_two, mix_two = jnp.split(sum_mix, (1024, 1536, 2560), axis=1)
+    sum_up = jnp.concatenate([sum_up, up_one, up_two], axis=1)
+    sum_mix = jnp.concatenate([mix_one, mix_two, sum_att], axis=1)
     grad_flat = flat[None]
     qkv_grad = pair_grad(normed_one[0], grad_flat[0])
     qbias_grad = token_sum(grad_flat[..., :model_width])
@@ -983,17 +1069,17 @@
         jnp.pad(blocks(small_sum.astype(jnp.bfloat16)), ((0, 0), (0, 0), (0, 0), (0, 111))),
         down_part.reshape(4, HD, model_width),
         jnp.pad(grad_mod.astype(jnp.bfloat16).reshape(-1, 128), ((0, 10), (0, 0))),
-        jnp.pad(caption_piece.astype(jnp.bfloat16), ((0, 1), (0, 0))),
+        caption_piece.astype(jnp.bfloat16),
     )
     wide = lambda part: part.astype(jnp.float32)
-    sum_small = wide(sum_v[:, 1408 : 1408 + 17])
+    sum_small = wide(sum_v[:, 896 : 896 + 17])
     return (
         block_out,
         grad_latents,
         sum_mod[:54].reshape(1, -1),
-        wide(caption_all[:, :text_piece].reshape(1, -1, model_width)),
+        wide(caption_all.reshape(1, -1, model_width)[:, : caption.shape[1]]),
         sum_small[:, :6].reshape(-1),
-        jnp.concatenate([wide(sum_q), wide(sum_k), wide(sum_v[:, :1408])], axis=1),
+        jnp.concatenate([wide(sum_q), wide(sum_k), wide(sum_v[:, :896])], axis=1),
         sum_small[:, 6],
         sum_small[:, 7],
         wide(sum_mix[:, :model_width]),

time: 566 us -> 517 us (0.913)
  matrix products: 117 us -> 56.1 us
  Pallas kernels: 337 us -> 367 us
  waiting for transfers between devices: 15.2 us -> 1.72 us
  local copies, waits for them, and re-layouts: 51.4 us -> 38.8 us
  other arithmetic: 14.5 us -> 23.1 us
    dot_general x26 -> x19, matrix products: 102 us -> 51.5 us  [project(): return jnp.dot(former, latter, preferred_element_type=jnp.float32)]
    pallas_call x3 -> x5, Pallas kernels: 295 us -> 326 us  [the longest x1 125 us: scatter_back(): pl.pallas_call(back_kernel, out_shape=(bf16(HD, 2560), bf16(HD, 3072), bf...]
    all_to_all x1, waiting for transfers between devices: 15.2 us -> 0.01 us  [on_device(): lax.all_to_all(grad_text.reshape(8, text_piece, grad_text.shape[1]), 'seq...]
    dot_general x5 -> x0, matrix products: 13.1 us -> none  [the longest x1 6.05 us: weight_grad(): jnp.einsum('bli,blo->io', former, latter, preferred_element_type=jnp.floa...]
    convert_element_type x1, other arithmetic: 0.21 us -> 6.78 us  [on_device(): (up_own.astype(jnp.float32) + up_received.astype(jnp.float32)).astype(jnp...]
  transfers between devices with their start and end apart: 9 -> 9, of which waited for: 1 -> 2; matrix products, arithmetic and copies ran while one was open for 23% -> 14% of each run, Pallas kernels for 23% -> 26%
where the time goes in v3:
time: 517 us; the launch traced here: 510 us
  Pallas kernels  367 us (71%)
  matrix products  56.1 us (11%)
  local copies, waits for them, and re-layouts  38.8 us (8%)
  other arithmetic  23.1 us (4%)
  between operations  15.9 us (3%)
  starting transfers between devices  6.79 us (1%)
    pallas_call x1, Pallas kernels, scatter_back(): pl.pallas_call(back_kernel, out_shape=(bf16(HD, 2560), bf16(HD, 3072), bf...  125 us
    pallas_call x1, Pallas kernels, gather_late(): pl.pallas_call(late_kernel, out_shape=full_shapes(shards) + (bf16(8, 128,...  116 us
    pallas_call x1, Pallas kernels, scatter_rest(): pl.pallas_call(rest_kernel, out_shape=(bf16(HD, 1536), bf16(HD, 1024), bf...  57.1 us
    dot_general x19, matrix products, project(): return jnp.dot(former, latter, preferred_element_type=jnp.float32)  51.5 us
    pallas_call x1, Pallas kernels, gather_early(): pl.pallas_call(early_kernel, out_shape=full_shapes(shards), in_specs=[ANY...  41.5 us
    pallas_call x1, Pallas kernels, mlp(): pl.pallas_call(mlp_kernel, grid=(units // size,), out_shape=(f32(tokens,...  21.9 us
    unnamed x155, local copies, waits for them, and re-layouts  11 us
  transfers between devices with their start and end apart: 9, of which 2 were waited for; matrix products, arithmetic and copies ran while one was open for 14% of the time, Pallas kernels for 26%

profile of v3, /device:TPU:0, one launch (start us, length us, event | category | flops | bytes accessed | tf_op | source)
XLA Modules:
  0.0 509.8 jit_solution(4110135422606334024)
XLA Ops:
  7.3 0.9 convert_reduce_fusion.9
  8.2 0.9 dynamic_update_slice.27
  9.0 0.8 dynamic_update_slice.28
  9.9 0.8 dynamic_update_slice.29
  10.7 0.8 dynamic_update_slice.30
  11.5 0.8 dynamic_update_slice.31
  12.4 0.8 dynamic_update_slice.32
  13.2 0.8 dynamic_update_slice.33
  14.0 0.8 dynamic_update_slice.34
  14.9 0.9 dynamic_update_slice.35
  15.9 1.0 copy-done.3
  16.9 41.5 %shard_map.347 = (bf16[4,2,2,72,3456]{4,3,2,1,0:T(8,128)(2,1)}, bf16[4,2,2,32,1152]{4,3,2,1,0:T(8,128)(2,1)S(1)}) custom-call(bf16[72,3456]{1,0:T(8,128)(2,1)S(1)} %copy-done.3, bf16[32,1152]{1,0:T(8,128)(2,1)S(1)} %reshape.476.small), custom_call_target="tpu_custom_call" | custom-call | tf_op jit(solution)/shard_map/pallas_call | solution.py:461
  60.8 4.8 fusion.1.packed
  65.7 115.5 %shard_map.348 = (bf16[4,2,2,72,4608]{4,3,2,1,0:T(8,128)(2,1)}, bf16[4,2,2,72,1152]{4,3,2,1,0:T(8,128)(2,1)}, bf16[4,2,2,72,2304]{4,3,2,1,0:T(8,128)(2,1)}, bf16...) custom-call(bf16[72,4608]{1,0:T(8,128)(2,1)S(1)} %copy-done, ...), custom_call_target="tpu_custom_call" | custom-call | tf_op jit(solution)/shard_map/pallas_call | solution.py:475
  181.3 3.6 fusion.2
  184.9 0.8 fusion.62
  187.9 1.2 copy.101
  189.1 1.1 fusion.65
  190.2 1.4 convolution_multiply_fusion
  191.9 2.0 convolution_convert_fusion.7
  193.9 2.6 fusion.66
  198.1 0.7 constant_dynamic-slice_fusion.8
  198.8 21.9 %shard_map.349 = (f32[128,1152]{1,0:T(8,128)S(1)}, f32[128,1152]{1,0:T(8,128)S(1)}, f32[1,4608]{1,0:T(1,128)S(1)}, bf16[576,4608]{1,0:T(8,128)(2,1)}, bf16[576,4...) custom-call(bf16[128,1152]{1,0:T(8,128)(2,1)S(1)} %fusion.101.rows, bf16[576,128]{1,0:T(8,128)(2,1)S(1)} %bitcast.197, ...), custom_call_target="tpu_custom_call" | custom-call | tf_op jit(solution)/shard_map/pallas_call | solution.py:852
  220.7 0.7 collective-permute-start
  221.6 2.0 split.25.weight
  223.7 0.8 fusion.26
  224.5 1.7 convert_reduce_fusion.2
  226.2 0.8 convert_reduce_fusion.3
  227.0 6.1 %shard_map.350 = (bf16[128,1152]{1,0:T(8,128)(2,1)S(1)}, bf16[128,2304]{1,0:T(8,128)(2,1)}) custom-call(bf16[128,1152]{1,0:T(8,128)(2,1)S(1)} %fusion.7.queries, bf16[128,2304]{1,0:T(8,128)(2,1)S(1)} %pad.17.text, bf16[128,1152]{1,0:T(8,128)(2,1)S(1)} %bitcast.195, bf16[1152,1152]{1,0:T(8,128)(2,1)S(1)} %split.25.weight), custom_call_target="tpu_custom_call" | custom-call | tf_op jit(solution)/shard_map/pallas_call | solution.py:390
  233.1 1.7 convert_reduce_fusion.5
  234.8 1.6 convolution_convert_fusion.4
  236.6 1.1 constant_dynamic-slice_fusion.4
  237.7 1.6 convolution_convert_fusion.3
  239.8 1.6 convolution_convert_fusion.2
  241.4 4.2 all-to-all-start
  246.4 3.8 fusion.8
  250.2 3.0 add_convert_fusion.5
  253.2 2.9 add_convert_fusion.4
  256.1 2.9 add_convert_fusion.3
  259.0 6.8 %add_convert_fusion = bf16[576,4608]{1,0:T(8,128)(2,1)} fusion(bf16[576,4608]{1,0:T(8,128)(2,1)} %collective-permute-done, bf16[576,4608]{1,0:T(8,128)(2,1)S(1)} %bitcast.221), kind=kLoop, calls=%fused_computation.1 | loop fusion | flops 10616832 | bytes 15925248 | tf_op jit(solution)/shard_map/convert_element_type | solution.py:983
  265.8 1.2 reduce_sum.243
  267.0 2.4 convolution_convert_fusion.1
  275.3 0.8 copy.116
  276.8 1.6 constant_dynamic-update-slice_fusion.2
  278.4 1.6 constant_dynamic-update-slice_fusion.1
  280.3 4.1 convolution_convert_fusion.6.cap
  284.4 2.8 fusion.3
  287.3 2.9 copy-done.14
  290.2 125.3 %shard_map.351 = (bf16[72,2560]{1,0:T(8,128)(2,1)S(1)}, bf16[72,3072]{1,0:T(8,128)(2,1)S(1)}, bf16[72,5120]{1,0:T(8,128)(2,1)S(1)}, bf16[128,3456]{1,0:T(8,128)(2,1)S(1)}) custom-call(bf16[4,2,72,4608]{3,2,1,0:T(8,128)(2,1)} %bitcast.208, bf16[4,2,72,6144]{3,2,1,0:T(8,128)(2,1)} %bitcast.213, bf16[8,128,432]{2,1,0:T(8,128)(2,1)S(1)} %get-tuple-element.72.heads, ...), custom_call_target="tpu_custom_call" | custom-call | tf_op jit(solution)/shard_map/pallas_call | solution.py:722
  415.7 2.6 fusion.23
  418.7 2.5 fusion.27
  421.2 1.2 copy.107
  422.5 3.1 convolution_convert_fusion
  427.9 1.0 slice_convert_fusion.2
  428.9 1.2 maximum_convert_fusion
  430.1 0.9 slice_convert_fusion
  431.1 1.6 collective-permute-done.6
  433.0 5.2 %add_convert_fusion.1 = bf16[576,3456]{1,0:T(8,128)(2,1)} fusion(bf16[576,3456]{1,0:T(8,128)(2,1)} %collective-permute-done.5, bf16[576,128]{1,0:T(8,128)(2,1)S(1)} %bitcast.237, bf16[128,3456]{1,0:T(8,128)(2,1)S(1)} %get-tuple-element.74), kind=kOutput, calls=%fused_computation.2 | convolution fusion | flops 515579904 | bytes 8994816 | tf_op jit(solution)/shard_map/dot_general | solution.py:36
  438.3 1.1 copy-done.2
  439.3 57.1 %shard_map.352 = (bf16[72,1536]{1,0:T(8,128)(2,1)S(1)}, bf16[72,1024]{1,0:T(8,128)(2,1)S(1)}, bf16[72,1024]{1,0:T(8,128)(2,1)S(1)}, bf16[4,72,1152]{2,1,0:T(8,12...) custom-call(bf16[4,2,72,3456]{3,2,1,0:T(8,128)(2,1)} %bitcast.207, ...), custom_call_target="tpu_custom_call" | custom-call | tf_op jit(solution)/shard_map/pallas_call | solution.py:792
  496.5 0.8 slice_reduce_fusion
  498.1 0.8 slice_convert_fusion.1
  500.3 1.2 bitcast_convert_fusion
  501.5 1.0 maximum_convert_fusion.1
  (250 shorter events, 20.1 us)
Async XLA Ops:
  7.2 52.7 %copy-start.9 = (bf16[1,128,1152]{2,1,0:T(8,128)(2,1)S(1)}, bf16[1,128,1152]{2,1,0:T(8,128)(2,1)}, u32[]{:S(2)}) copy-start(bf16[1,128,1152]{2,1,0:T(8,128)(2,1)} %param.20) | copy-start | bytes 884740
  7.2 431.1 %reduce-scatter.2.cloned.1.call-start = ((), (), s32[]{:S(2)}) async-start(), calls=%async_computation.2 | async-start | bytes 11280384 | tf_op jit(solution)/shard_map/reduce_scatter | solution.py:978
  16.9 43.4 %copy-start.31 = (bf16[72,1152]{1,0:T(8,128)(2,1)S(1)}, bf16[72,1152]{1,0:T(8,128)(2,1)}, u32[]{:S(2)}) copy-start(bf16[72,1152]{1,0:T(8,128)(2,1)} %param.33) | copy-start | bytes 497668
  16.9 43.4 %copy-start.32 = (bf16[72,1152]{1,0:T(8,128)(2,1)S(1)}, bf16[72,1152]{1,0:T(8,128)(2,1)}, u32[]{:S(2)}) copy-start(bf16[72,1152]{1,0:T(8,128)(2,1)} %param.27) | copy-start | bytes 497668
  59.9 5.8 %copy-start.25 = (f32[1152]{0:T(1024)}, f32[1152]{0:T(1024)S(1)}, u32[]{:S(2)}) copy-start(f32[1152]{0:T(1024)S(1)} %get-tuple-element.114) | copy-start | bytes 13828
  59.9 134.1 %copy-start.38 = (f32[1152]{0:T(1024)}, f32[1152]{0:T(1024)S(1)}, u32[]{:S(2)}) copy-start(f32[1152]{0:T(1024)S(1)} %get-tuple-element.115) | copy-start | bytes 13828
  60.8 4.9 copy-start
  60.8 4.9 copy-start.1
  60.8 4.9 copy-start.4
  60.8 4.9 copy-start.6
  65.7 115.6 %copy-start.27 = (bf16[1,120,1152]{2,1,0:T(8,128)(2,1)S(1)}, bf16[1,120,1152]{2,1,0:T(8,128)(2,1)}, u32[]{:S(2)}) copy-start(bf16[1,120,1152]{2,1,0:T(8,128)(2,1)} %param.22) | copy-start | bytes 829444
  181.3 4.4 copy-start.15
  184.9 2.2 copy-start.12
  186.3 7.6 %copy-start.18 = (f32[128,1152]{1,0:T(8,128)}, f32[128,1152]{1,0:T(8,128)S(1)}, u32[]{:S(2)}) copy-start(f32[128,1152]{1,0:T(8,128)S(1)} %get-tuple-element.148) | copy-start | bytes 1769476
  193.9 3.1 copy-start.23
  193.9 2.9 copy-start.29
  193.9 2.9 copy-start.40
  220.7 38.3 %collective-permute-start = (bf16[576,4608]{1,0:T(8,128)(2,1)}, bf16[576,4608]{1,0:T(8,128)(2,1)}, u32[]{:S(2)}, u32[]{:S(2)}) collective-permute-start(bf16[576,4608]{1,0:T(8,128)(2,1)} %get-tuple-element.66), channel_id=1, source_target_pairs={{0,1},{1,0},{2,3},{3,2},{4,5},{5,4},{6,7},{7,6},{8,9},{9,8},{10,11... | collective-permute-start | bytes 15925256 | tf_op jit(solution)/shard_map/ppermute | solution.py:977
  221.5 2.1 copy-start.20
  221.5 2.2 copy-start.8
  221.5 2.2 copy-start.30
  221.5 2.2 copy-start.59
  221.5 2.2 copy-start.61
  221.5 3.0 copy-start.65
  221.5 3.0 copy-start.34
  221.5 3.0 copy-start.45
  226.2 6.9 %copy-start.13 = (bf16[4,2,2,72,1152]{4,3,2,1,0:T(8,128)(2,1)S(1)}, bf16[4,2,2,72,1152]{4,3,2,1,0:T(8,128)(2,1)}, u32[]{:S(2)}) copy-start(bf16[4,2,2,72,1152]{4,3,2,1,0:T(8,128)(2,1)} %get-tuple-element.58) | copy-start | bytes 7962628
  226.2 6.9 %copy-start.39 = (f32[1152]{0:T(1024)S(1)}, f32[1152]{0:T(1024)}, u32[]{:S(2)}) copy-start(f32[1152]{0:T(1024)} %copy-done.38) | copy-start | bytes 13828
  233.0 3.3 copy-start.22
  236.4 13.8 %collective-permute-start.1 = (bf16[576,1152]{1,0:T(8,128)(2,1)}, bf16[576,1152]{1,0:T(8,128)(2,1)}, u32[]{:S(2)}, u32[]{:S(2)}) collective-permute-start(bf16[576,1152]{1,0:T(8,128)(2,1)} %convolution_convert_fusion.4), channel_id=1, source_target_pairs={{0,1},{1,0},{2,3},{3,2},{4,5},{5,4},{6,7},{7,6},{8,9},{9,8},{10,11... | collective-permute-start | bytes 3981320 | tf_op jit(solution)/shard_map/ppermute | solution.py:887
  237.7 7.9 %copy-start.28 = (bf16[1,120,1152]{2,1,0:T(8,128)(2,1)S(1)}, bf16[1,120,1152]{2,1,0:T(8,128)(2,1)}, u32[]{:S(2)}) copy-start(bf16[1,120,1152]{2,1,0:T(8,128)(2,1)} %param.22) | copy-start | bytes 829444
  239.3 13.9 %collective-permute-start.2 = (bf16[576,1152]{1,0:T(8,128)(2,1)}, bf16[576,1152]{1,0:T(8,128)(2,1)}, u32[]{:S(2)}, u32[]{:S(2)}) collective-permute-start(bf16[576,1152]{1,0:T(8,128)(2,1)} %convolution_convert_fusion.3), channel_id=1, source_target_pairs={{0,1},{1,0},{2,3},{3,2},{4,5},{5,4},{6,7},{7,6},{8,9},{9,8},{10,11... | collective-permute-start | bytes 3981320 | tf_op jit(solution)/shard_map/ppermute | solution.py:887
  241.4 14.7 %collective-permute-start.3 = (bf16[576,1152]{1,0:T(8,128)(2,1)}, bf16[576,1152]{1,0:T(8,128)(2,1)}, u32[]{:S(2)}, u32[]{:S(2)}) collective-permute-start(bf16[576,1152]{1,0:T(8,128)(2,1)} %convolution_convert_fusion.2), channel_id=1, source_target_pairs={{0,1},{1,0},{2,3},{3,2},{4,5},{5,4},{6,7},{7,6},{8,9},{9,8},{10,11... | collective-permute-start | bytes 3981320 | tf_op jit(solution)/shard_map/ppermute | solution.py:887
  241.4 24.4 %all-to-all-start = ((bf16[8,16,2304]{2,1,0:T(8,128)(2,1)}), bf16[8,16,2304]{2,1,0:T(8,128)(2,1)}, u32[]{:S(2)}, u32[]{:S(2)}) async-start(bf16[8,16,2304]{2,1,0:T(8,128)(2,1)} %bitcast.32), calls=%async_computation | async-start | bytes 1179648 | tf_op jit(solution)/shard_map/all_to_all | solution.py:998
  246.3 12.6 %slice-start.2 = ((s8[5308416]{0:T(1024)(128)(4,1)}), s8[4194304]{0:T(1024)(128)(4,1)S(1)}, s32[]{:S(2)}) async-start(s8[5308416]{0:T(1024)(128)(4,1)} %bitcast.220), calls=%async_computation.5 | async-start | bytes 8388608
  250.2 8.8 %slice-start.3 = ((s8[5308416]{0:T(1024)(128)(4,1)}), s8[1114112]{0:T(1024)(128)(4,1)S(1)}, s32[]{:S(2)}) async-start(s8[5308416]{0:T(1024)(128)(4,1)} %bitcast.220), calls=%async_computation.6 | async-start | bytes 2228224
  265.8 4.8 copy-start.42
  265.8 5.4 %copy-start.43 = (f32[1152]{0:T(1024)S(1)}, f32[1152]{0:T(1024)}, u32[]{:S(2)}) copy-start(f32[1152]{0:T(1024)} %get-tuple-element.93) | copy-start | bytes 13828
  265.8 7.4 %copy-start.44 = (f32[1152]{0:T(1024)S(1)}, f32[1152]{0:T(1024)}, u32[]{:S(2)}) copy-start(f32[1152]{0:T(1024)} %get-tuple-element.116) | copy-start | bytes 13828
  265.8 8.1 %copy-start.41 = (f32[1152]{0:T(1024)S(1)}, f32[1152]{0:T(1024)}, u32[]{:S(2)}) copy-start(f32[1152]{0:T(1024)} %get-tuple-element.92) | copy-start | bytes 13828
  269.4 15.0 %collective-permute-start.4 = (bf16[576,2304]{1,0:T(8,128)(2,1)}, bf16[576,2304]{1,0:T(8,128)(2,1)}, u32[]{:S(2)}, u32[]{:S(2)}) collective-permute-start(bf16[576,2304]{1,0:T(8,128)(2,1)} %convolution_convert_fusion.1), channel_id=1, source_target_pairs={{0,1},{1,0},{2,3},{3,2},{4,5},{5,4},{6,7},{7,6},{8,9},{9,8},{10,11... | collective-permute-start | bytes 7962632 | tf_op jit(solution)/shard_map/ppermute | solution.py:887
  276.8 3.3 copy-start.16
  284.4 5.8 %copy-start.5 = (bf16[1,128,1152]{2,1,0:T(8,128)(2,1)S(1)}, bf16[1,128,1152]{2,1,0:T(8,128)(2,1)}, u32[]{:S(2)}) copy-start(bf16[1,128,1152]{2,1,0:T(8,128)(2,1)} %fusion.8) | copy-start | bytes 884740
  284.4 131.2 %slice-start = ((s8[7962624]{0:T(1024)(128)(4,1)}), s8[4194304]{0:T(1024)(128)(4,1)S(1)}, s32[]{:S(2)}) async-start(s8[7962624]{0:T(1024)(128)(4,1)} %bitcast.204), calls=%async_computation.3 | async-start | bytes 8388608
  287.3 2.9 copy-start.14
  290.2 125.4 %slice-start.1 = ((s8[7962624]{0:T(1024)(128)(4,1)}), s8[3768320]{0:T(1024)(128)(4,1)S(1)}, s32[]{:S(2)}) async-start(s8[7962624]{0:T(1024)(128)(4,1)} %bitcast.204), calls=%async_computation.4 | async-start | bytes 7536640
  290.2 125.4 %copy-start.10 = (bf16[1,128,1152]{2,1,0:T(8,128)(2,1)S(1)}, bf16[1,128,1152]{2,1,0:T(8,128)(2,1)}, u32[]{:S(2)}) copy-start(bf16[1,128,1152]{2,1,0:T(8,128)(2,1)} %param.20) | copy-start | bytes 884740
  290.2 125.4 %copy-start.26 = (f32[1152]{0:T(1024)S(1)}, f32[1152]{0:T(1024)}, u32[]{:S(2)}) copy-start(f32[1152]{0:T(1024)} %copy-done.25) | copy-start | bytes 13828
  290.2 125.4 %copy-start.57 = (f32[128]{0:T(128)S(1)}, f32[128]{0:T(128)}, u32[]{:S(2)}) copy-start(f32[128]{0:T(128)} %copy-done.56) | copy-start | bytes 1540
  415.6 2.7 copy-start.63
  415.7 2.7 copy-start.11
  415.7 2.7 copy-start.52
  415.7 3.1 copy-start.37
  422.4 3.5 copy-start.53
  422.4 3.5 copy-start.54
  422.4 3.5 copy-start.55
  422.4 4.6 copy-start.48
  422.5 4.6 copy-start.49
  422.5 4.6 copy-start.50
  422.5 4.7 copy-start.47
  422.5 4.7 copy-start.46
  422.5 4.7 copy-start.35
  425.6 7.4 %collective-permute-start.5 = (bf16[576,3456]{1,0:T(8,128)(2,1)}, bf16[576,3456]{1,0:T(8,128)(2,1)}, u32[]{:S(2)}, u32[]{:S(2)}) collective-permute-start(bf16[576,3456]{1,0:T(8,128)(2,1)} %convolution_convert_fusion), channel_id=1, source_target_pairs={{0,1},{1,0},{2,3},{3,2},{4,5},{5,4},{6,7},{7,6},{8,9},{9,8},{10,11... | collective-permute-start | bytes 11943944 | tf_op jit(solution)/shard_map/ppermute | solution.py:887
  427.3 5.4 %collective-permute-start.6 = (bf16[576,17]{0,1:T(8,128)(2,1)S(1)}, bf16[576,17]{0,1:T(8,128)(2,1)S(1)}, u32[]{:S(2)}, u32[]{:S(2)}) collective-permute-start(bf16[576,17]{0,1:T(8,128)(2,1)S(1)} %convert_element_type.255), channel_id=1, source_target_pairs={{0,1},{1,0},{2,3},{3,2},{4,5},{5,4},{6,7},{7,6},{8,9},{9,8},{10,11... | collective-permute-start | bytes 58760 | tf_op jit(solution)/shard_map/ppermute | solution.py:1064
  (15 other events, 14.5 us)
Sparse Core Ops, SparseCore 0:
  221.6 150.5 reduce-scatter.1

commit v4 on v3

--- a/solution.py
+++ b/solution.py
@@ -397,15 +397,16 @@
 
 
 def late_kernel(
-    up, cq, ckv, pair, down, packed,
-    o_up, o_cq, o_ckv, o_pair, o_down, o_heads, o_rows,
+    up, cq, ckv, proj, cproj, down, packed,
+    o_up, o_cq, o_ckv, o_proj, o_cproj, o_down, o_heads, o_rows,
     sent, heads, mixed, joined, local, send, recv,
 ):
     height = down.shape[0]
     pieces = [
+        Piece(proj, o_proj, "z", 1, 0, proj.shape[1]),
         Piece(cq, o_cq, "z", 1, 0, cq.shape[1]),
-        Piece(ckv, o_ckv, "z", 1, 0, ckv.shape[1]),
-        Piece(pair, o_pair, "x", 1, 0, pair.shape[1]),
+        Piece(cproj, o_cproj, "z", 1, 0, cproj.shape[1]),
+        Piece(ckv, o_ckv, "x", 1, 0, ckv.shape[1]),
         Piece(up, o_up, "y", 1, 0, up.shape[1]),
         Piece(down, o_down, "x", 0, 128, height - 128),
         Piece(down, o_down, "y", 0, 0, 128),
@@ -416,15 +417,15 @@
     greet(unique(work.x, work.y, work.z, work.c, [work.sibling]))
     for to, what, at in head_slices(packed):
         sent[to, :, what] = packed[:, at]
-    own = exchange(copies, "in", seq, peers, sent, heads, local.at[6])
+    own = exchange(copies, "in", seq, peers, sent, heads, local.at[7])
     work.first()
     exchanged(copies, "in", seq, peers, heads, own)
-    keep = pltpu.make_async_copy(heads, o_heads, local.at[7])
+    keep = pltpu.make_async_copy(heads, o_heads, local.at[8])
     keep.start()
     attend(heads, 0, mixed)
     work.second()
     attend(heads, 1, mixed)
-    own = exchange(copies, "out", seq, peers, mixed, joined, local.at[8])
+    own = exchange(copies, "out", seq, peers, mixed, joined, local.at[9])
     work.third()
     work.fourth()
     exchanged(copies, "out", seq, peers, joined, own)
@@ -475,15 +476,15 @@
     outs = pl.pallas_call(
         late_kernel,
         out_shape=full_shapes(shards) + (bf16(8, 128, 3 * PAIR), bf16(128, 8 * PAIR)),
-        in_specs=[ANYWHERE] * 5 + [ON_CHIP],
-        out_specs=(ANYWHERE,) * 6 + (ON_CHIP,),
+        in_specs=[ANYWHERE] * 6 + [ON_CHIP],
+        out_specs=(ANYWHERE,) * 7 + (ON_CHIP,),
         scratch_shapes=[
             vmem(8, 128, 3 * PAIR), vmem(8, 128, 3 * PAIR), vmem(8, 128, PAIR), vmem(8, 128, PAIR),
         ]
-        + semaphores(9, 256, 256),
+        + semaphores(10, 256, 256),
         compiler_params=parameters(1),
     )(*shards, packed)
-    return tuple(whole(out) for out in outs[:5]) + outs[5:]
+    return tuple(whole(out) for out in outs[:6]) + outs[6:]
 
 
 def add_up(parts, out):
@@ -685,13 +686,14 @@
 
 
 def back_kernel(
-    up, mix, heads, grad_rows, o_up, o_mix, o_att, o_flat,
+    up, ckv, proj, cproj, cq, heads, grad_rows, o_up, o_mix, o_att, o_flat,
     sent, grads, mixed, joined, key_sum, value_sum, *rest,
 ):
     scratch, (local, send, recv) = rest[:18], rest[18:]
     copies, keep = Copies(send, recv), Stays(local)
     work = Scatter(
-        (up, 0, 2560), [(up, 2560, 2048), (mix, 0, 1024)], [(mix, 1024, 5120)],
+        (up, 0, 2560), [(up, 2560, 2048), (ckv, 0, 1024)],
+        [(ckv, 1024, 1280), (proj, 0, 1152), (cproj, 0, 1152), (cq, 0, 1152)],
         (o_up, o_mix, o_att), scratch, copies, keep,
     )
     seq, peers = seq_peers()
@@ -700,6 +702,8 @@
         sent[to, :, what] = grad_rows[:, at]
     own = exchange(copies, "in", seq, peers, sent, grads, local.at[16])
     work.first()
+    spare = scratch[6]
+    spare[:, :, :, 4736:] = jnp.zeros(spare.shape[:3] + (384,), spare.dtype)
     exchanged(copies, "in", seq, peers, grads, own)
     for h in (0, 1):
         attend_back(heads, grads, h, mixed, key_sum, value_sum)
@@ -716,7 +720,7 @@
     copies.finish()
 
 
-def scatter_back(up, mix, heads, grad_rows):
+def scatter_back(up, ckv, proj, cproj, cq, heads, grad_rows):
     bf16 = lambda *shape: jax.ShapeDtypeStruct(shape, jnp.bfloat16)
     vmem = lambda *shape: pltpu.VMEM(shape, jnp.bfloat16)
     return pl.pallas_call(
@@ -724,7 +728,7 @@
         out_shape=(
             bf16(HD, 2560), bf16(HD, 3072), bf16(HD, 5120), bf16(128, 24 * PAIR),
         ),
-        in_specs=[ANYWHERE] * 2 + [ON_CHIP] * 2,
+        in_specs=[ANYWHERE] * 5 + [ON_CHIP] * 2,
         out_specs=(ANYWHERE,) * 3 + (ON_CHIP,),
         scratch_shapes=[
             vmem(8, 128, PAIR), vmem(8, 128, PAIR), vmem(8, 128, 3 * PAIR), vmem(8, 128, 3 * PAIR),
@@ -733,7 +737,7 @@
         + Scatter.buffers(2560, 3072, 5120)
         + semaphores(18, 80, 80),
         compiler_params=parameters(2),
-    )(up, mix, heads, grad_rows)
+    )(up, ckv, proj, cproj, cq, heads, grad_rows)
 
 
 def rest_kernel(
@@ -743,7 +747,7 @@
     scratch, (local, send, recv) = rest[:18], rest[18:]
     copies, keep = Copies(send, recv), Stays(local)
     work = Scatter(
-        (qkv, 0, 1536), [(qkv, 1536, 1024)], [(qkv, 2560, 896), (small, 0, 128)],
+        (qkv, 0, 512), [(qkv, 512, 1024)], [(qkv, 1536, 1920), (small, 0, 128)],
         (o_up, o_mix, o_att), scratch, copies, keep,
     )
     seq, peers, along_y = work.seq, work.peers, work.along_y
@@ -792,7 +796,7 @@
     return pl.pallas_call(
         rest_kernel,
         out_shape=(
-            bf16(HD, 1536), bf16(HD, 1024), bf16(HD, 1024), bf16(4, HD, width),
+            bf16(HD, 512), bf16(HD, 1024), bf16(HD, 2048), bf16(4, HD, width),
             jax.ShapeDtypeStruct(mod.shape, jnp.float32), bf16(8, *cap.shape),
         ),
         in_specs=[ANYWHERE] * 5,
@@ -801,7 +805,7 @@
             vmem(4, HD, width), vmem(1, HD, width), vmem(1, HD, width), vmem(1, HD, width),
             vmem(8, *mod.shape),
         ]
-        + Scatter.buffers(1536, 1024, 1024)
+        + Scatter.buffers(512, 1024, 2048)
         + semaphores(18, 96, 96),
         compiler_params=parameters(3),
     )(qkv, small, down, mod, cap)
@@ -910,22 +914,23 @@
     down_bias,
     cotangent,
 ):
-    group = lax.axis_index("fsdp")
-    small = jnp.zeros((32 * HD * 16,), jnp.bfloat16)
-    at = 0
-    for vector in (
-        shift_table, query_bias, value_bias, proj_bias, cross_qbias, cross_vbias, cross_pbias,
-        down_bias, up_bias,
-    ):
-        small = lax.dynamic_update_slice(small, vector, (at + group * vector.shape[0],))
-        at += 16 * vector.shape[0]
-    full_qkv, each_small = gather_early(qkv_weight, small.reshape(32, -1))
-    full_small = jnp.sum(each_small.reshape(16, 32, -1).astype(jnp.float32), axis=0)
-    full_table = full_small[:6]
+    small = jnp.concatenate(
+        [
+            shift_table, query_bias, value_bias, proj_bias, cross_qbias, cross_vbias, cross_pbias,
+            down_bias, up_bias,
+        ]
+    ).reshape(-1, HD)
+    rows_used = small.shape[0]
+    full_qkv, each_small = gather_early(
+        qkv_weight, jnp.pad(small, ((0, 32 - rows_used), (0, 128 - HD)))
+    )
+    each_small = each_small.reshape(16, 32, 128)[:, :rows_used, :HD].astype(jnp.float32)
+    full_table = each_small[:, :6].reshape(6, -1)
+    full_biases = each_small[:, 6:13].transpose(1, 0, 2).reshape(7, -1)
     full_qbias, full_vbias, full_pbias, full_cqbias, full_cvbias, full_cpbias, full_dbias = (
-        full_small[6 + i] for i in range(7)
-    )
-    full_ubias = full_small[13:17].reshape(-1)
+        full_biases[i] for i in range(7)
+    )
+    full_ubias = each_small[:, 13:17].reshape(-1)
     latent_count, local_len, model_width = latents.shape
     inputs = latents.astype(jnp.float32)
     modulation = (full_table + timestep.astype(jnp.float32).reshape(6, model_width)).reshape(
@@ -939,17 +944,9 @@
         jnp.float32
     )
     packed = (project(normed_one, full_qkv) + qkv_bias).astype(jnp.bfloat16)
-    full_up, full_cquery, full_ckv, full_pair, full_down, heads, rows = gather_late(
-        (
-            up_weight,
-            cross_query,
-            cross_kv,
-            jnp.concatenate([proj_weight, cross_proj], axis=1),
-            down_weight,
-        ),
-        packed[0],
-    )
-    full_proj, full_cproj = jnp.split(full_pair, 2, axis=1)
+    full_up, full_cquery, full_ckv, full_proj, full_cproj, full_down, heads, rows = gather_late(
+        (up_weight, cross_query, cross_kv, proj_weight, cross_proj, down_weight), packed[0]
+    )
     tok_major = rows[None]
     branch_one = project(tok_major, full_proj) + full_pbias.astype(jnp.float32)
     after_one = inputs + gate_one * branch_one
@@ -1017,16 +1014,17 @@
     cvalue_bgrad = jnp.sum(text_grad[:, model_width:].astype(jnp.float32), axis=0)
     caption_piece = project(text_grad, full_ckv.T)
     blocks = lambda grad: grad.reshape(4, 2, HD, -1)
-    mix = jnp.concatenate(
-        [proj_grad, cproj_grad, cquery_grad, ckv_grad, jnp.zeros((8 * HD, 384), jnp.bfloat16)],
-        axis=1,
-    )
     sum_up, sum_mix, sum_att, flat = scatter_back(
-        blocks(up_grad), blocks(mix), heads, grad_tok[0]
-    )
-    up_one, mix_one, up_two, mix_two = jnp.split(sum_mix, (1024, 1536, 2560), axis=1)
+        *(blocks(grad) for grad in (up_grad, ckv_grad, proj_grad, cproj_grad, cquery_grad)),
+        heads,
+        grad_tok[0],
+    )
+    up_one, ckv_one, up_two, ckv_two = jnp.split(sum_mix, (1024, 1536, 2560), axis=1)
     sum_up = jnp.concatenate([sum_up, up_one, up_two], axis=1)
-    sum_mix = jnp.concatenate([mix_one, mix_two, sum_att], axis=1)
+    ckv_three, sum_proj, sum_cproj, sum_cquery, _ = jnp.split(
+        sum_att, (1280, 2432, 3584, 4736), axis=1
+    )
+    sum_ckv = jnp.concatenate([ckv_one, ckv_two, ckv_three], axis=1)
     grad_flat = flat[None]
     qkv_grad = pair_grad(normed_one[0], grad_flat[0])
     qbias_grad = token_sum(grad_flat[..., :model_width])
@@ -1072,23 +1070,23 @@
         caption_piece.astype(jnp.bfloat16),
     )
     wide = lambda part: part.astype(jnp.float32)
-    sum_small = wide(sum_v[:, 896 : 896 + 17])
+    sum_small = wide(sum_v[:, 1920 : 1920 + 17])
     return (
         block_out,
         grad_latents,
         sum_mod[:54].reshape(1, -1),
         wide(caption_all.reshape(1, -1, model_width)[:, : caption.shape[1]]),
         sum_small[:, :6].reshape(-1),
-        jnp.concatenate([wide(sum_q), wide(sum_k), wide(sum_v[:, :896])], axis=1),
+        jnp.concatenate([wide(sum_q), wide(sum_k), wide(sum_v[:, :1920])], axis=1),
         sum_small[:, 6],
         sum_small[:, 7],
-        wide(sum_mix[:, :model_width]),
+        wide(sum_proj),
         sum_small[:, 8],
-        wide(sum_mix[:, 2 * model_width : 3 * model_width]),
+        wide(sum_cquery),
         sum_small[:, 9],
-        wide(sum_mix[:, 3 * model_width : 5 * model_width]),
+        wide(sum_ckv),
         sum_small[:, 10],
-        wide(sum_mix[:, model_width : 2 * model_width]),
+        wide(sum_cproj),
         sum_small[:, 11],
         wide(sum_up),
         sum_small[:, 13:17].reshape(-1),

time: 517 us -> 519 us (level)
  Pallas kernels: 367 us -> 358 us
  local copies, waits for them, and re-layouts: 38.8 us -> 46.9 us
    dynamic_update_slice x9 -> x0, local copies, waits for them, and re-layouts: 7.58 us -> none  [on_device(): lax.dynamic_update_slice(small, vector, (at + group * vector.shape[0],))]
    concatenate x1, local copies, waits for them, and re-layouts: 0.08 us -> 6.14 us  [on_device(): jnp.concatenate([shift_table, query_bias, value_bias, proj_bias, cross_qb...]
    unnamed x155 -> x162, local copies, waits for them, and re-layouts: 11 us -> 8.26 us
  transfers between devices with their start and end apart: 9 -> 9, of which waited for: 2 -> 2; matrix products, arithmetic and copies ran while one was open for 14% -> 14% of each run, Pallas kernels for 26% -> 25%
where the time goes in v4:
time: 519 us; the launch traced here: 512 us
  Pallas kernels  358 us (69%)
  matrix products  56.5 us (11%)
  local copies, waits for them, and re-layouts  46.9 us (9%)
  other arithmetic  26.5 us (5%)
  between operations  15.5 us (3%)
  starting transfers between devices  6.53 us (1%)
    pallas_call x1, Pallas kernels, scatter_back(): pl.pallas_call(back_kernel, out_shape=(bf16(HD, 2560), bf16(HD, 3072), bf...  123 us
    pallas_call x1, Pallas kernels, gather_late(): pl.pallas_call(late_kernel, out_shape=full_shapes(shards) + (bf16(8, 128,...  116 us
    pallas_call x1, Pallas kernels, scatter_rest(): pl.pallas_call(rest_kernel, out_shape=(bf16(HD, 512), bf16(HD, 1024), bf1...  53.5 us
    dot_general x19, matrix products, project(): return jnp.dot(former, latter, preferred_element_type=jnp.float32)  51.8 us
    pallas_call x1, Pallas kernels, gather_early(): pl.pallas_call(early_kernel, out_shape=full_shapes(shards), in_specs=[ANY...  38.6 us
    pallas_call x1, Pallas kernels, mlp(): pl.pallas_call(mlp_kernel, grid=(units // size,), out_shape=(f32(tokens,...  21.9 us
  transfers between devices with their start and end apart: 9, of which 2 were waited for; matrix products, arithmetic and copies ran while one was open for 14% of the time, Pallas kernels for 25%

profile of v4, /device:TPU:0, one launch (start us, length us, event | category | flops | bytes accessed | tf_op | source)
XLA Modules:
  0.0 511.8 jit_solution(11504311528251083944)
XLA Ops:
  7.2 6.1 %concatenate.46 = bf16[1224]{0:T(1024)(128)(2,1)S(1)} concatenate(bf16[432]{0:T(512)(128)(2,1)} %param.23, bf16[72]{0:T(256)(128)(2,1)} %param.25, bf16[72]{0:T(256)(128)(2,1)} %param.26, bf16[72]{0:T(256)(128)(2,1)} %param.28, bf16[72]{0:T(256)(128)(2,1)} %param.30, bf16[72]{0:T(256)(128)(2,1)} %param.32, bf16[72]{0:T(256)(128)(2,1)} %param.34, bf16[72]{0:T(256)(128)(2,1)} %param.38, ...), dimensions={0} | concatenate | bytes 4896 | tf_op jit(solution)/shard_map/concatenate | solution.py:917
  13.5 1.0 copy-done.13
  14.5 38.6 %shard_map.347 = (bf16[4,2,2,72,3456]{4,3,2,1,0:T(8,128)(2,1)}, bf16[4,2,2,32,128]{4,3,2,1,0:T(8,128)(2,1)S(1)}) custom-call(bf16[72,3456]{1,0:T(8,128)(2,1)S(1)} %copy-done.13, bf16[32,128]{1,0:T(8,128)(2,1)S(1)} %pad.21.small), custom_call_target="tpu_custom_call" | custom-call | tf_op jit(solution)/shard_map/pallas_call | solution.py:462
  53.9 0.8 convert_reduce_fusion.8
  56.3 1.1 convert_reduce_fusion
  57.4 1.2 fusion.19
  59.3 4.9 fusion.1.packed
  64.4 115.6 %shard_map.348 = (bf16[4,2,2,72,4608]{4,3,2,1,0:T(8,128)(2,1)}, bf16[4,2,2,72,1152]{4,3,2,1,0:T(8,128)(2,1)}, bf16[4,2,2,72,2304]{4,3,2,1,0:T(8,128)(2,1)}, bf16...) custom-call(bf16[72,4608]{1,0:T(8,128)(2,1)S(1)} %copy-done.8, ...), custom_call_target="tpu_custom_call" | custom-call | tf_op jit(solution)/shard_map/pallas_call | solution.py:476
  180.0 3.8 fusion.2
  183.9 0.8 copy-done.36
  186.2 1.4 add.246
  187.6 1.4 fusion.27
  190.8 1.1 fusion.59
  192.0 1.4 convolution_multiply_fusion
  194.1 0.9 copy.99
  195.0 2.1 convolution_convert_fusion.7
  197.1 1.9 fusion.60
  199.8 0.9 fusion.97
  200.7 1.5 slice.164
  202.2 0.9 copy.103
  203.1 1.2 copy.102
  204.3 1.5 reshape_reshape.8.bias
  206.5 1.8 constant_dynamic-slice_fusion.8
  209.0 21.9 %shard_map.349 = (f32[128,1152]{1,0:T(8,128)S(1)}, f32[128,1152]{1,0:T(8,128)S(1)}, f32[1,4608]{1,0:T(1,128)S(1)}, bf16[576,4608]{1,0:T(8,128)(2,1)}, bf16[576,4...) custom-call(bf16[128,1152]{1,0:T(8,128)(2,1)S(1)} %fusion.98.rows, bf16[576,128]{1,0:T(8,128)(2,1)S(1)} %bitcast.206, ...), custom_call_target="tpu_custom_call" | custom-call | tf_op jit(solution)/shard_map/pallas_call | solution.py:856
  231.0 0.8 copy-done.11
  232.4 1.0 collective-permute-start
  233.4 1.4 add.263
  234.8 1.2 pad.22.text
  236.0 2.0 fusion.23
  238.7 2.4 convert_reduce_fusion.1
  241.4 6.1 %shard_map.350 = (bf16[128,1152]{1,0:T(8,128)(2,1)S(1)}, bf16[128,2304]{1,0:T(8,128)(2,1)}) custom-call(bf16[128,1152]{1,0:T(8,128)(2,1)S(1)} %copy-done.4, bf16[128,2304]{1,0:T(8,128)(2,1)S(1)} %pad.22.text, bf16[128,1152]{1,0:T(8,128)(2,1)S(1)} %bitcast.202, bf16[1152,1152]{1,0:T(8,128)(2,1)S(1)} %bitcast.200), custom_call_target="tpu_custom_call" | custom-call | tf_op jit(solution)/shard_map/pallas_call | solution.py:390
  247.5 2.3 convert_reduce_fusion.4
  250.4 0.9 copy.104
  251.3 1.8 constant_dynamic-slice_fusion.4
  253.1 1.6 convolution_convert_fusion.3
  255.1 1.6 convolution_convert_fusion.2
  256.7 3.7 all-to-all-start
  260.4 1.4 fusion.38
  261.8 1.6 reshape.554
  263.4 1.9 dynamic-slice_reduce_fusion
  265.3 1.5 reshape.556
  266.8 3.5 fusion.7
  270.4 1.9 add_convert_fusion.5
  272.3 3.0 add_convert_fusion.4
  275.3 2.9 add_convert_fusion.3
  278.2 6.1 %add_convert_fusion = bf16[576,4608]{1,0:T(8,128)(2,1)} fusion(bf16[576,4608]{1,0:T(8,128)(2,1)} %collective-permute-done, bf16[576,4608]{1,0:T(8,128)(2,1)S(1)} %bitcast.228), kind=kLoop, calls=%fused_computation.1 | loop fusion | flops 10616832 | bytes 15925248 | tf_op jit(solution)/shard_map/convert_element_type | solution.py:980
  284.4 2.3 convolution_convert_fusion.1
  291.2 4.2 convolution_convert_fusion.6.cap
  295.5 4.2 add_convert_fusion.2
  299.8 122.5 %shard_map.351 = (bf16[72,2560]{1,0:T(8,128)(2,1)S(1)}, bf16[72,3072]{1,0:T(8,128)(2,1)S(1)}, bf16[72,5120]{1,0:T(8,128)(2,1)S(1)}, bf16[128,3456]{1,0:T(8,128)(2,1)S(1)}) custom-call(bf16[4,2,72,4608]{3,2,1,0:T(8,128)(2,1)} %bitcast.215, bf16[4,2,72,2304]{3,2,1,0:T(8,128)(2,1)} %bitcast.216, bf16[4,2,72,1152]{3,2,1,0:T(8,128)(2,1)S(1)} %bitcast.201, ...), custom_call_target="tpu_custom_call" | custom-call | tf_op jit(solution)/shard_map/pallas_call | solution.py:726
  422.4 2.6 fusion.20
  425.5 2.4 fusion.24
  428.2 3.2 convolution_convert_fusion
  433.6 0.9 maximum_convert_fusion.2
  434.5 1.0 slice_convert_fusion.1
  435.5 1.2 maximum_convert_fusion
  436.8 1.6 collective-permute-done.6
  438.8 5.3 %add_convert_fusion.1 = bf16[576,3456]{1,0:T(8,128)(2,1)} fusion(bf16[576,3456]{1,0:T(8,128)(2,1)} %collective-permute-done.5, bf16[576,128]{1,0:T(8,128)(2,1)S(1)} %bitcast.244, bf16[128,3456]{1,0:T(8,128)(2,1)S(1)} %get-tuple-element.76), kind=kOutput, calls=%fused_computation.2 | convolution fusion | flops 515579904 | bytes 8994816 | tf_op jit(solution)/shard_map/dot_general | solution.py:36
  444.1 1.1 copy-done.10
  445.2 53.5 %shard_map.352 = (bf16[72,512]{1,0:T(8,128)(2,1)S(1)}, bf16[72,1024]{1,0:T(8,128)(2,1)S(1)}, bf16[72,2048]{1,0:T(8,128)(2,1)S(1)}, bf16[4,72,1152]{2,1,0:T(8,128...) custom-call(bf16[4,2,72,3456]{3,2,1,0:T(8,128)(2,1)} %bitcast.214, ...), custom_call_target="tpu_custom_call" | custom-call | tf_op jit(solution)/shard_map/pallas_call | solution.py:796
  498.7 0.8 slice_reduce_fusion
  500.3 0.8 slice_convert_fusion
  502.6 1.2 bitcast_convert_fusion
  503.8 1.0 maximum_convert_fusion.1
  (259 shorter events, 21.9 us)
Async XLA Ops:
  7.2 436.9 %reduce-scatter.2.cloned.1.call-start = ((), (), s32[]{:S(2)}) async-start(), calls=%async_computation.2 | async-start | bytes 11280384 | tf_op jit(solution)/shard_map/reduce_scatter | solution.py:975
  55.4 8.9 %copy-start.50 = (f32[1152]{0:T(1024)}, f32[1152]{0:T(1024)S(1)}, u32[]{:S(2)}) copy-start(f32[1152]{0:T(1024)S(1)} %get-tuple-element.115) | copy-start | bytes 13828
  55.4 132.2 %copy-start.46 = (f32[1152]{0:T(1024)}, f32[1152]{0:T(1024)S(1)}, u32[]{:S(2)}) copy-start(f32[1152]{0:T(1024)S(1)} %get-tuple-element.117) | copy-start | bytes 13828
  57.4 6.9 %copy-start.65 = (f32[128]{0:T(128)}, f32[128]{0:T(128)S(1)}, u32[]{:S(2)}) copy-start(f32[128]{0:T(128)S(1)} %broadcast_multiply_fusion.1) | copy-start | bytes 1540
  59.1 5.2 %copy-start.60 = (f32[128]{0:T(128)}, f32[128]{0:T(128)S(1)}, u32[]{:S(2)}) copy-start(f32[128]{0:T(128)S(1)} %fusion.42) | copy-start | bytes 1540
  59.3 5.0 copy-start.8
  59.3 5.0 copy-start.9
  59.3 5.0 copy-start.16
  59.3 5.0 copy-start.17
  59.3 5.0 copy-start.18
  59.3 5.0 copy-start.19
  64.4 115.6 %copy-start.45 = (bf16[1,120,1152]{2,1,0:T(8,128)(2,1)S(1)}, bf16[1,120,1152]{2,1,0:T(8,128)(2,1)}, u32[]{:S(2)}) copy-start(bf16[1,120,1152]{2,1,0:T(8,128)(2,1)} %param.22) | copy-start | bytes 829444
  180.0 3.9 copy-start.6
  180.0 7.6 %copy-start.23 = (bf16[1,128,1152]{2,1,0:T(8,128)(2,1)S(1)}, bf16[1,128,1152]{2,1,0:T(8,128)(2,1)}, u32[]{:S(2)}) copy-start(bf16[1,128,1152]{2,1,0:T(8,128)(2,1)} %param.20) | copy-start | bytes 884740
  180.0 7.6 %copy-start.28 = (bf16[4,2,2,72,1152]{4,3,2,1,0:T(8,128)(2,1)S(1)}, bf16[4,2,2,72,1152]{4,3,2,1,0:T(8,128)(2,1)}, u32[]{:S(2)}) copy-start(bf16[4,2,2,72,1152]{4,3,2,1,0:T(8,128)(2,1)} %get-tuple-element.57) | copy-start | bytes 7962628
  190.3 3.0 copy-start.58
  193.4 3.7 copy-start
  199.0 6.8 %copy-start.31 = (bf16[1,128,1152]{2,1,0:T(8,128)(2,1)S(1)}, bf16[1,128,1152]{2,1,0:T(8,128)(2,1)}, u32[]{:S(2)}) copy-start(bf16[1,128,1152]{2,1,0:T(8,128)(2,1)} %param.39) | copy-start | bytes 884740
  199.3 3.0 copy-start.71
  199.3 3.0 copy-start.68
  232.4 45.8 %collective-permute-start = (bf16[576,4608]{1,0:T(8,128)(2,1)}, bf16[576,4608]{1,0:T(8,128)(2,1)}, u32[]{:S(2)}, u32[]{:S(2)}) collective-permute-start(bf16[576,4608]{1,0:T(8,128)(2,1)} %get-tuple-element.68), channel_id=1, source_target_pairs={{0,1},{1,0},{2,3},{3,2},{4,5},{5,4},{6,7},{7,6},{8,9},{9,8},{10,11... | collective-permute-start | bytes 15925256 | tf_op jit(solution)/shard_map/ppermute | solution.py:974
  233.4 5.3 %copy-start.32 = (bf16[1,128,1152]{2,1,0:T(8,128)(2,1)S(1)}, bf16[1,128,1152]{2,1,0:T(8,128)(2,1)}, u32[]{:S(2)}) copy-start(bf16[1,128,1152]{2,1,0:T(8,128)(2,1)} %param.39) | copy-start | bytes 884740
  234.8 3.9 copy-start.12
  234.8 3.9 copy-start.27
  236.0 5.3 %copy-start.4 = (bf16[128,1152]{1,0:T(8,128)(2,1)S(1)}, bf16[128,1152]{1,0:T(8,128)(2,1)}, u32[]{:S(2)}) copy-start(bf16[128,1152]{1,0:T(8,128)(2,1)} %copy-done.3) | copy-start | bytes 884740
  241.2 6.3 %copy-start.30 = (bf16[4,2,2,72,1152]{4,3,2,1,0:T(8,128)(2,1)S(1)}, bf16[4,2,2,72,1152]{4,3,2,1,0:T(8,128)(2,1)}, u32[]{:S(2)}) copy-start(bf16[4,2,2,72,1152]{4,3,2,1,0:T(8,128)(2,1)} %get-tuple-element.59) | copy-start | bytes 7962628
  241.2 6.3 %copy-start.33 = (bf16[1,128,1152]{2,1,0:T(8,128)(2,1)S(1)}, bf16[1,128,1152]{2,1,0:T(8,128)(2,1)}, u32[]{:S(2)}) copy-start(bf16[1,128,1152]{2,1,0:T(8,128)(2,1)} %param.39) | copy-start | bytes 884740
  241.2 6.3 %copy-start.47 = (f32[1152]{0:T(1024)S(1)}, f32[1152]{0:T(1024)}, u32[]{:S(2)}) copy-start(f32[1152]{0:T(1024)} %copy-done.46) | copy-start | bytes 13828
  241.3 8.5 %copy-start.1 = (bf16[1,128,1152]{2,1,0:T(8,128)(2,1)}, bf16[1,128,1152]{2,1,0:T(8,128)(2,1)S(1)}, u32[]{:S(2)}) copy-start(bf16[1,128,1152]{2,1,0:T(8,128)(2,1)S(1)} %get-tuple-element.119) | copy-start | bytes 884740
  247.5 3.0 copy-start.35
  247.5 3.8 copy-start.38
  249.8 5.3 %copy-start.2 = (bf16[1,128,1152]{2,1,0:T(8,128)(2,1)S(1)}, bf16[1,128,1152]{2,1,0:T(8,128)(2,1)}, u32[]{:S(2)}) copy-start(bf16[1,128,1152]{2,1,0:T(8,128)(2,1)} %copy-done.1) | copy-start | bytes 884740
  250.3 20.0 %collective-permute-start.1 = (bf16[576,1152]{1,0:T(8,128)(2,1)S(1)}, bf16[576,1152]{1,0:T(8,128)(2,1)}, u32[]{:S(2)}, u32[]{:S(2)}) collective-permute-start(bf16[576,1152]{1,0:T(8,128)(2,1)S(1)} %convolution_convert_fusion.4), channel_id=1, source_target_pairs={{0,1},{1,0},{2,3},{3,2},{4,5},{5,4},{6,7},{7,6},{8,9},{9,8},{10,11... | collective-permute-start | bytes 3981320 | tf_op jit(solution)/shard_map/ppermute | solution.py:891
  254.7 17.6 %collective-permute-start.2 = (bf16[576,1152]{1,0:T(8,128)(2,1)}, bf16[576,1152]{1,0:T(8,128)(2,1)}, u32[]{:S(2)}, u32[]{:S(2)}) collective-permute-start(bf16[576,1152]{1,0:T(8,128)(2,1)} %convolution_convert_fusion.3), channel_id=1, source_target_pairs={{0,1},{1,0},{2,3},{3,2},{4,5},{5,4},{6,7},{7,6},{8,9},{9,8},{10,11... | collective-permute-start | bytes 3981320 | tf_op jit(solution)/shard_map/ppermute | solution.py:891
  256.7 13.7 %copy-start.41 = (bf16[8,1,72,128]{3,2,1,0:T(8,128)(2,1)S(1)}, bf16[8,1,72,128]{3,2,1,0:T(8,128)(2,1)}, u32[]{:S(2)}) copy-start(bf16[8,1,72,128]{3,2,1,0:T(8,128)(2,1)} %get-tuple-element.145) | copy-start | bytes 442372
  256.7 18.6 %collective-permute-start.3 = (bf16[576,1152]{1,0:T(8,128)(2,1)}, bf16[576,1152]{1,0:T(8,128)(2,1)}, u32[]{:S(2)}, u32[]{:S(2)}) collective-permute-start(bf16[576,1152]{1,0:T(8,128)(2,1)} %convolution_convert_fusion.2), channel_id=1, source_target_pairs={{0,1},{1,0},{2,3},{3,2},{4,5},{5,4},{6,7},{7,6},{8,9},{9,8},{10,11... | collective-permute-start | bytes 3981320 | tf_op jit(solution)/shard_map/ppermute | solution.py:891
  256.7 27.6 %all-to-all-start = ((bf16[8,16,2304]{2,1,0:T(8,128)(2,1)}), bf16[8,16,2304]{2,1,0:T(8,128)(2,1)S(1)}, u32[]{:S(2)}, u32[]{:S(2)}) async-start(bf16[8,16,2304]{2,1,0:T(8,128)(2,1)} %bitcast.34), calls=%async_computation | async-start | bytes 1179648 | tf_op jit(solution)/shard_map/all_to_all | solution.py:995
  266.8 5.5 %copy-start.44 = (bf16[8,1,72,128]{3,2,1,0:T(8,128)(2,1)S(1)}, bf16[8,1,72,128]{3,2,1,0:T(8,128)(2,1)}, u32[]{:S(2)}) copy-start(bf16[8,1,72,128]{3,2,1,0:T(8,128)(2,1)} %get-tuple-element.156) | copy-start | bytes 442372
  266.8 11.4 %slice-start.2 = ((s8[5308416]{0:T(1024)(128)(4,1)}), s8[4194304]{0:T(1024)(128)(4,1)S(1)}, s32[]{:S(2)}) async-start(s8[5308416]{0:T(1024)(128)(4,1)} %bitcast.227), calls=%async_computation.5 | async-start | bytes 8388608
  270.4 4.9 copy-start.43
  270.4 7.8 %slice-start.3 = ((s8[5308416]{0:T(1024)(128)(4,1)}), s8[1114112]{0:T(1024)(128)(4,1)S(1)}, s32[]{:S(2)}) async-start(s8[5308416]{0:T(1024)(128)(4,1)} %bitcast.227), calls=%async_computation.6 | async-start | bytes 2228224
  278.2 6.2 %copy-start.49 = (bf16[576,16]{0,1:T(8,128)(2,1)S(1)}, bf16[576,16]{0,1:T(8,128)(2,1)}, u32[]{:S(2)}) copy-start(bf16[576,16]{0,1:T(8,128)(2,1)} %reshape.556) | copy-start | bytes 55300
  284.3 3.0 copy-start.48
  284.3 3.7 copy-start.54
  284.3 4.3 copy-start.55
  284.3 4.9 copy-start.56
  284.3 5.8 %copy-start.53 = (f32[1152]{0:T(1024)S(1)}, f32[1152]{0:T(1024)}, u32[]{:S(2)}) copy-start(f32[1152]{0:T(1024)} %get-tuple-element.94) | copy-start | bytes 13828
  284.3 5.9 %copy-start.22 = (f32[1,4608]{1,0:T(1,128)S(1)}, f32[1,4608]{1,0:T(1,128)}, u32[]{:S(2)}) copy-start(f32[1,4608]{1,0:T(1,128)} %copy-done.21) | copy-start | bytes 55300
  286.8 8.7 %collective-permute-start.4 = (bf16[576,2304]{1,0:T(8,128)(2,1)}, bf16[576,2304]{1,0:T(8,128)(2,1)}, u32[]{:S(2)}, u32[]{:S(2)}) collective-permute-start(bf16[576,2304]{1,0:T(8,128)(2,1)} %convolution_convert_fusion.1), channel_id=1, source_target_pairs={{0,1},{1,0},{2,3},{3,2},{4,5},{5,4},{6,7},{7,6},{8,9},{9,8},{10,11... | collective-permute-start | bytes 7962632 | tf_op jit(solution)/shard_map/ppermute | solution.py:891
  295.5 4.3 copy-start.5
  295.5 4.3 copy-start.7
  295.5 126.8 %slice-start = ((s8[7962624]{0:T(1024)(128)(4,1)}), s8[4194304]{0:T(1024)(128)(4,1)S(1)}, s32[]{:S(2)}) async-start(s8[7962624]{0:T(1024)(128)(4,1)} %bitcast.211), calls=%async_computation.3 | async-start | bytes 8388608
  299.8 122.6 %slice-start.1 = ((s8[7962624]{0:T(1024)(128)(4,1)}), s8[3768320]{0:T(1024)(128)(4,1)S(1)}, s32[]{:S(2)}) async-start(s8[7962624]{0:T(1024)(128)(4,1)} %bitcast.211), calls=%async_computation.4 | async-start | bytes 7536640
  299.8 122.6 %copy-start.24 = (bf16[1,128,1152]{2,1,0:T(8,128)(2,1)S(1)}, bf16[1,128,1152]{2,1,0:T(8,128)(2,1)}, u32[]{:S(2)}) copy-start(bf16[1,128,1152]{2,1,0:T(8,128)(2,1)} %param.20) | copy-start | bytes 884740
  299.8 122.6 %copy-start.66 = (f32[128]{0:T(128)S(1)}, f32[128]{0:T(128)}, u32[]{:S(2)}) copy-start(f32[128]{0:T(128)} %copy-done.65) | copy-start | bytes 1540
  422.4 2.7 copy-start.25
  422.4 3.1 copy-start.51
  428.2 3.5 copy-start.62
  428.2 3.5 copy-start.63
  428.2 3.5 copy-start.64
  428.2 4.6 copy-start.59
  431.4 7.4 %collective-permute-start.5 = (bf16[576,3456]{1,0:T(8,128)(2,1)}, bf16[576,3456]{1,0:T(8,128)(2,1)}, u32[]{:S(2)}, u32[]{:S(2)}) collective-permute-start(bf16[576,3456]{1,0:T(8,128)(2,1)} %convolution_convert_fusion), channel_id=1, source_target_pairs={{0,1},{1,0},{2,3},{3,2},{4,5},{5,4},{6,7},{7,6},{8,9},{9,8},{10,11... | collective-permute-start | bytes 11943944 | tf_op jit(solution)/shard_map/ppermute | solution.py:891
  432.2 3.3 copy-start.15
  433.0 5.4 %collective-permute-start.6 = (bf16[576,17]{0,1:T(8,128)(2,1)S(1)}, bf16[576,17]{0,1:T(8,128)(2,1)S(1)}, u32[]{:S(2)}, u32[]{:S(2)}) collective-permute-start(bf16[576,17]{0,1:T(8,128)(2,1)S(1)} %convert_element_type.256), channel_id=1, source_target_pairs={{0,1},{1,0},{2,3},{3,2},{4,5},{5,4},{6,7},{7,6},{8,9},{9,8},{10,11... | collective-permute-start | bytes 58760 | tf_op jit(solution)/shard_map/ppermute | solution.py:1062
  (21 other events, 31.9 us)
Sparse Core Ops, SparseCore 0:
  233.5 143.5 reduce-scatter.1

commit v5 on v4

--- a/solution.py
+++ b/solution.py
@@ -914,23 +914,22 @@
     down_bias,
     cotangent,
 ):
-    small = jnp.concatenate(
-        [
-            shift_table, query_bias, value_bias, proj_bias, cross_qbias, cross_vbias, cross_pbias,
-            down_bias, up_bias,
-        ]
-    ).reshape(-1, HD)
-    rows_used = small.shape[0]
-    full_qkv, each_small = gather_early(
-        qkv_weight, jnp.pad(small, ((0, 32 - rows_used), (0, 128 - HD)))
-    )
-    each_small = each_small.reshape(16, 32, 128)[:, :rows_used, :HD].astype(jnp.float32)
-    full_table = each_small[:, :6].reshape(6, -1)
-    full_biases = each_small[:, 6:13].transpose(1, 0, 2).reshape(7, -1)
+    group = lax.axis_index("fsdp")
+    small = jnp.zeros((32 * HD * 16,), jnp.bfloat16)
+    at = 0
+    for vector in (
+        shift_table, query_bias, value_bias, proj_bias, cross_qbias, cross_vbias, cross_pbias,
+        down_bias, up_bias,
+    ):
+        small = lax.dynamic_update_slice(small, vector, (at + group * vector.shape[0],))
+        at += 16 * vector.shape[0]
+    full_qkv, each_small = gather_early(qkv_weight, small.reshape(32, -1))
+    full_small = jnp.sum(each_small.reshape(16, 32, -1).astype(jnp.float32), axis=0)
+    full_table = full_small[:6]
     full_qbias, full_vbias, full_pbias, full_cqbias, full_cvbias, full_cpbias, full_dbias = (
-        full_biases[i] for i in range(7)
-    )
-    full_ubias = each_small[:, 13:17].reshape(-1)
+        full_small[6 + i] for i in range(7)
+    )
+    full_ubias = full_small[13:17].reshape(-1)
     latent_count, local_len, model_width = latents.shape
     inputs = latents.astype(jnp.float32)
     modulation = (full_table + timestep.astype(jnp.float32).reshape(6, model_width)).reshape(

time: 519 us -> 515 us (level)
  local copies, waits for them, and re-layouts: 46.9 us -> 41.3 us
    dynamic_update_slice x0 -> x9, local copies, waits for them, and re-layouts: none -> 7.58 us  [on_device(): lax.dynamic_update_slice(small, vector, (at + group * vector.shape[0],))]
    concatenate x1 -> x0, local copies, waits for them, and re-layouts: 6.14 us -> none  [on_device(): jnp.concatenate([shift_table, query_bias, value_bias, proj_bias, cross_qb...]
where the time goes in v5:
time: 515 us; the launch traced here: 508 us
  Pallas kernels  361 us (70%)
  matrix products  56.3 us (11%)
  local copies, waits for them, and re-layouts  41.3 us (8%)
  other arithmetic  24.7 us (5%)
  between operations  15.5 us (3%)
  starting transfers between devices  6.73 us (1%)
    pallas_call x1, Pallas kernels, scatter_back(): pl.pallas_call(back_kernel, out_shape=(bf16(HD, 2560), bf16(HD, 3072), bf...  123 us
    pallas_call x1, Pallas kernels, gather_late(): pl.pallas_call(late_kernel, out_shape=full_shapes(shards) + (bf16(8, 128,...  116 us
    pallas_call x1, Pallas kernels, scatter_rest(): pl.pallas_call(rest_kernel, out_shape=(bf16(HD, 512), bf16(HD, 1024), bf1...  53.2 us
    dot_general x19, matrix products, project(): return jnp.dot(former, latter, preferred_element_type=jnp.float32)  51.6 us
    pallas_call x1, Pallas kernels, gather_early(): pl.pallas_call(early_kernel, out_shape=full_shapes(shards), in_specs=[ANY...  41.5 us
    pallas_call x1, Pallas kernels, mlp(): pl.pallas_call(mlp_kernel, grid=(units // size,), out_shape=(f32(tokens,...  21.9 us
  transfers between devices with their start and end apart: 9, of which 2 were waited for; matrix products, arithmetic and copies ran while one was open for 14% of the time, Pallas kernels for 25%

profile of v5, /device:TPU:0, one launch (start us, length us, event | category | flops | bytes accessed | tf_op | source)
XLA Modules:
  0.0 507.5 jit_solution(11376578026455381150)
XLA Ops:
  7.3 0.9 convert_reduce_fusion.9
  8.2 0.9 dynamic_update_slice.27
  9.9 0.8 dynamic_update_slice.29
  11.5 0.8 dynamic_update_slice.31
  12.4 0.8 dynamic_update_slice.32
  13.2 0.8 dynamic_update_slice.33
  14.0 0.8 dynamic_update_slice.34
  14.9 0.9 dynamic_update_slice.35
  15.9 1.0 copy-done.13
  16.9 41.5 %shard_map.347 = (bf16[4,2,2,72,3456]{4,3,2,1,0:T(8,128)(2,1)}, bf16[4,2,2,32,1152]{4,3,2,1,0:T(8,128)(2,1)S(1)}) custom-call(bf16[72,3456]{1,0:T(8,128)(2,1)S(1)} %copy-done.13, bf16[32,1152]{1,0:T(8,128)(2,1)S(1)} %reshape.488.small), custom_call_target="tpu_custom_call" | custom-call | tf_op jit(solution)/shard_map/pallas_call | solution.py:462
  60.8 4.9 fusion.1.packed
  65.8 115.6 %shard_map.348 = (bf16[4,2,2,72,4608]{4,3,2,1,0:T(8,128)(2,1)}, bf16[4,2,2,72,1152]{4,3,2,1,0:T(8,128)(2,1)}, bf16[4,2,2,72,2304]{4,3,2,1,0:T(8,128)(2,1)}, bf16...) custom-call(bf16[72,4608]{1,0:T(8,128)(2,1)S(1)} %copy-done.8, ...), custom_call_target="tpu_custom_call" | custom-call | tf_op jit(solution)/shard_map/pallas_call | solution.py:476
  181.4 3.8 fusion.2
  185.3 1.4 fusion.27
  188.5 1.1 fusion.60
  189.6 1.4 convolution_multiply_fusion
  191.0 0.9 copy.99
  191.9 2.1 convolution_convert_fusion.7
  194.1 1.9 fusion.61
  196.8 0.9 fusion.98
  197.7 1.5 slice_bitcast_fusion.1
  199.2 0.9 copy.103
  200.1 1.2 copy.102
  201.2 1.4 copy.120
  203.3 1.8 constant_dynamic-slice_fusion.8
  205.8 21.9 %shard_map.349 = (f32[128,1152]{1,0:T(8,128)S(1)}, f32[128,1152]{1,0:T(8,128)S(1)}, f32[1,4608]{1,0:T(1,128)S(1)}, bf16[576,4608]{1,0:T(8,128)(2,1)}, bf16[576,4...) custom-call(bf16[128,1152]{1,0:T(8,128)(2,1)S(1)} %fusion.99.rows, bf16[576,128]{1,0:T(8,128)(2,1)S(1)} %bitcast.209, ...), custom_call_target="tpu_custom_call" | custom-call | tf_op jit(solution)/shard_map/pallas_call | solution.py:856
  229.2 1.0 collective-permute-start
  230.3 1.2 pad.17.text
  231.5 2.0 fusion.23
  234.2 2.4 convert_reduce_fusion.2
  236.8 6.1 %shard_map.350 = (bf16[128,1152]{1,0:T(8,128)(2,1)S(1)}, bf16[128,2304]{1,0:T(8,128)(2,1)}) custom-call(bf16[128,1152]{1,0:T(8,128)(2,1)S(1)} %copy-done.4, bf16[128,2304]{1,0:T(8,128)(2,1)S(1)} %pad.17.text, bf16[128,1152]{1,0:T(8,128)(2,1)S(1)} %bitcast.205, bf16[1152,1152]{1,0:T(8,128)(2,1)S(1)} %bitcast.203), custom_call_target="tpu_custom_call" | custom-call | tf_op jit(solution)/shard_map/pallas_call | solution.py:390
  242.9 2.3 convert_reduce_fusion.5
  245.8 0.9 copy.104
  246.7 1.9 constant_dynamic-slice_fusion.4
  248.6 1.6 convolution_convert_fusion.3
  250.6 1.6 convolution_convert_fusion.2
  252.2 3.7 all-to-all-start
  255.9 1.4 fusion.39
  257.3 1.5 reshape.521
  258.9 1.9 dynamic-slice_reduce_fusion
  260.8 1.5 reshape.523
  262.3 3.5 fusion.7
  265.8 1.9 add_convert_fusion.5
  267.8 2.9 add_convert_fusion.4
  270.7 2.9 add_convert_fusion.3
  273.6 6.1 %add_convert_fusion = bf16[576,4608]{1,0:T(8,128)(2,1)} fusion(bf16[576,4608]{1,0:T(8,128)(2,1)} %collective-permute-done, bf16[576,4608]{1,0:T(8,128)(2,1)S(1)} %bitcast.231), kind=kLoop, calls=%fused_computation.1 | loop fusion | flops 10616832 | bytes 15925248 | tf_op jit(solution)/shard_map/convert_element_type | solution.py:979
  279.9 2.3 convolution_convert_fusion.1
  286.8 4.1 convolution_convert_fusion.6.cap
  291.0 4.2 add_convert_fusion.2
  295.3 123.0 %shard_map.351 = (bf16[72,2560]{1,0:T(8,128)(2,1)S(1)}, bf16[72,3072]{1,0:T(8,128)(2,1)S(1)}, bf16[72,5120]{1,0:T(8,128)(2,1)S(1)}, bf16[128,3456]{1,0:T(8,128)(2,1)S(1)}) custom-call(bf16[4,2,72,4608]{3,2,1,0:T(8,128)(2,1)} %bitcast.218, bf16[4,2,72,2304]{3,2,1,0:T(8,128)(2,1)} %bitcast.219, bf16[4,2,72,1152]{3,2,1,0:T(8,128)(2,1)S(1)} %bitcast.204, ...), custom_call_target="tpu_custom_call" | custom-call | tf_op jit(solution)/shard_map/pallas_call | solution.py:726
  418.3 2.6 fusion.20
  421.4 2.4 fusion.24
  424.1 3.2 convolution_convert_fusion
  429.6 0.9 maximum_convert_fusion.2
  430.5 1.0 slice_convert_fusion.1
  431.4 1.2 maximum_convert_fusion
  432.8 1.6 collective-permute-done.6
  434.7 5.3 %add_convert_fusion.1 = bf16[576,3456]{1,0:T(8,128)(2,1)} fusion(bf16[576,3456]{1,0:T(8,128)(2,1)} %collective-permute-done.5, bf16[576,128]{1,0:T(8,128)(2,1)S(1)} %bitcast.247, bf16[128,3456]{1,0:T(8,128)(2,1)S(1)} %get-tuple-element.76), kind=kOutput, calls=%fused_computation.2 | convolution fusion | flops 515579904 | bytes 8994816 | tf_op jit(solution)/shard_map/dot_general | solution.py:36
  440.0 1.1 copy-done.10
  441.1 53.2 %shard_map.352 = (bf16[72,512]{1,0:T(8,128)(2,1)S(1)}, bf16[72,1024]{1,0:T(8,128)(2,1)S(1)}, bf16[72,2048]{1,0:T(8,128)(2,1)S(1)}, bf16[4,72,1152]{2,1,0:T(8,128...) custom-call(bf16[4,2,72,3456]{3,2,1,0:T(8,128)(2,1)} %bitcast.217, ...), custom_call_target="tpu_custom_call" | custom-call | tf_op jit(solution)/shard_map/pallas_call | solution.py:796
  494.4 0.8 slice_reduce_fusion
  496.0 0.8 slice_convert_fusion
  498.2 1.2 bitcast_convert_fusion
  499.4 1.0 maximum_convert_fusion.1
  (251 shorter events, 21.7 us)
Async XLA Ops:
  7.2 52.7 %copy-start.23 = (bf16[1,128,1152]{2,1,0:T(8,128)(2,1)S(1)}, bf16[1,128,1152]{2,1,0:T(8,128)(2,1)}, u32[]{:S(2)}) copy-start(bf16[1,128,1152]{2,1,0:T(8,128)(2,1)} %param.20) | copy-start | bytes 884740
  7.2 432.8 %reduce-scatter.2.cloned.1.call-start = ((), (), s32[]{:S(2)}) async-start(), calls=%async_computation.2 | async-start | bytes 11280384 | tf_op jit(solution)/shard_map/reduce_scatter | solution.py:974
  59.9 5.8 %copy-start.49 = (f32[1152]{0:T(1024)}, f32[1152]{0:T(1024)S(1)}, u32[]{:S(2)}) copy-start(f32[1152]{0:T(1024)S(1)} %get-tuple-element.115) | copy-start | bytes 13828
  59.9 125.4 %copy-start.45 = (f32[1152]{0:T(1024)}, f32[1152]{0:T(1024)S(1)}, u32[]{:S(2)}) copy-start(f32[1152]{0:T(1024)S(1)} %get-tuple-element.117) | copy-start | bytes 13828
  60.8 4.9 copy-start.8
  60.8 4.9 copy-start.9
  60.8 4.9 copy-start.16
  60.8 4.9 copy-start.17
  60.8 4.9 copy-start.18
  60.8 4.9 copy-start.19
  65.7 115.6 %copy-start.44 = (bf16[1,120,1152]{2,1,0:T(8,128)(2,1)S(1)}, bf16[1,120,1152]{2,1,0:T(8,128)(2,1)}, u32[]{:S(2)}) copy-start(bf16[1,120,1152]{2,1,0:T(8,128)(2,1)} %param.22) | copy-start | bytes 829444
  181.3 3.9 copy-start.6
  181.4 4.0 copy-start.28
  186.7 2.9 copy-start.34
  191.0 3.0 copy-start
  196.0 6.6 %copy-start.31 = (bf16[1,128,1152]{2,1,0:T(8,128)(2,1)S(1)}, bf16[1,128,1152]{2,1,0:T(8,128)(2,1)}, u32[]{:S(2)}) copy-start(bf16[1,128,1152]{2,1,0:T(8,128)(2,1)} %param.39) | copy-start | bytes 884740
  196.2 3.0 copy-start.68
  196.2 2.9 copy-start.65
  229.2 44.4 %collective-permute-start = (bf16[576,4608]{1,0:T(8,128)(2,1)}, bf16[576,4608]{1,0:T(8,128)(2,1)}, u32[]{:S(2)}, u32[]{:S(2)}) collective-permute-start(bf16[576,4608]{1,0:T(8,128)(2,1)} %get-tuple-element.68), channel_id=1, source_target_pairs={{0,1},{1,0},{2,3},{3,2},{4,5},{5,4},{6,7},{7,6},{8,9},{9,8},{10,11... | collective-permute-start | bytes 15925256 | tf_op jit(solution)/shard_map/ppermute | solution.py:973
  230.2 3.9 copy-start.32
  230.2 3.9 copy-start.12
  230.3 3.9 copy-start.27
  231.5 5.3 %copy-start.4 = (bf16[128,1152]{1,0:T(8,128)(2,1)S(1)}, bf16[128,1152]{1,0:T(8,128)(2,1)}, u32[]{:S(2)}) copy-start(bf16[128,1152]{1,0:T(8,128)(2,1)} %copy-done.3) | copy-start | bytes 884740
  236.6 6.3 %copy-start.30 = (bf16[4,2,2,72,1152]{4,3,2,1,0:T(8,128)(2,1)S(1)}, bf16[4,2,2,72,1152]{4,3,2,1,0:T(8,128)(2,1)}, u32[]{:S(2)}) copy-start(bf16[4,2,2,72,1152]{4,3,2,1,0:T(8,128)(2,1)} %get-tuple-element.59) | copy-start | bytes 7962628
  236.6 6.3 %copy-start.33 = (bf16[1,128,1152]{2,1,0:T(8,128)(2,1)S(1)}, bf16[1,128,1152]{2,1,0:T(8,128)(2,1)}, u32[]{:S(2)}) copy-start(bf16[1,128,1152]{2,1,0:T(8,128)(2,1)} %param.39) | copy-start | bytes 884740
  236.6 6.3 %copy-start.46 = (f32[1152]{0:T(1024)S(1)}, f32[1152]{0:T(1024)}, u32[]{:S(2)}) copy-start(f32[1152]{0:T(1024)} %copy-done.45) | copy-start | bytes 13828
  236.8 8.5 %copy-start.1 = (bf16[1,128,1152]{2,1,0:T(8,128)(2,1)}, bf16[1,128,1152]{2,1,0:T(8,128)(2,1)S(1)}, u32[]{:S(2)}) copy-start(bf16[1,128,1152]{2,1,0:T(8,128)(2,1)S(1)} %get-tuple-element.119) | copy-start | bytes 884740
  242.9 3.0 copy-start.35
  242.9 3.8 copy-start.38
  245.2 5.3 %copy-start.2 = (bf16[1,128,1152]{2,1,0:T(8,128)(2,1)S(1)}, bf16[1,128,1152]{2,1,0:T(8,128)(2,1)}, u32[]{:S(2)}) copy-start(bf16[1,128,1152]{2,1,0:T(8,128)(2,1)} %copy-done.1) | copy-start | bytes 884740
  245.7 20.1 %collective-permute-start.1 = (bf16[576,1152]{1,0:T(8,128)(2,1)S(1)}, bf16[576,1152]{1,0:T(8,128)(2,1)}, u32[]{:S(2)}, u32[]{:S(2)}) collective-permute-start(bf16[576,1152]{1,0:T(8,128)(2,1)S(1)} %convolution_convert_fusion.4), channel_id=1, source_target_pairs={{0,1},{1,0},{2,3},{3,2},{4,5},{5,4},{6,7},{7,6},{8,9},{9,8},{10,11... | collective-permute-start | bytes 3981320 | tf_op jit(solution)/shard_map/ppermute | solution.py:891
  250.1 17.6 %collective-permute-start.2 = (bf16[576,1152]{1,0:T(8,128)(2,1)}, bf16[576,1152]{1,0:T(8,128)(2,1)}, u32[]{:S(2)}, u32[]{:S(2)}) collective-permute-start(bf16[576,1152]{1,0:T(8,128)(2,1)} %convolution_convert_fusion.3), channel_id=1, source_target_pairs={{0,1},{1,0},{2,3},{3,2},{4,5},{5,4},{6,7},{7,6},{8,9},{9,8},{10,11... | collective-permute-start | bytes 3981320 | tf_op jit(solution)/shard_map/ppermute | solution.py:891
  252.1 13.7 %copy-start.39 = (bf16[8,1,72,128]{3,2,1,0:T(8,128)(2,1)S(1)}, bf16[8,1,72,128]{3,2,1,0:T(8,128)(2,1)}, u32[]{:S(2)}) copy-start(bf16[8,1,72,128]{3,2,1,0:T(8,128)(2,1)} %get-tuple-element.145) | copy-start | bytes 442372
  252.1 18.6 %collective-permute-start.3 = (bf16[576,1152]{1,0:T(8,128)(2,1)}, bf16[576,1152]{1,0:T(8,128)(2,1)}, u32[]{:S(2)}, u32[]{:S(2)}) collective-permute-start(bf16[576,1152]{1,0:T(8,128)(2,1)} %convolution_convert_fusion.2), channel_id=1, source_target_pairs={{0,1},{1,0},{2,3},{3,2},{4,5},{5,4},{6,7},{7,6},{8,9},{9,8},{10,11... | collective-permute-start | bytes 3981320 | tf_op jit(solution)/shard_map/ppermute | solution.py:891
  252.2 27.5 %all-to-all-start = ((bf16[8,16,2304]{2,1,0:T(8,128)(2,1)}), bf16[8,16,2304]{2,1,0:T(8,128)(2,1)S(1)}, u32[]{:S(2)}, u32[]{:S(2)}) async-start(bf16[8,16,2304]{2,1,0:T(8,128)(2,1)} %bitcast.33), calls=%async_computation | async-start | bytes 1179648 | tf_op jit(solution)/shard_map/all_to_all | solution.py:994
  262.3 5.5 %copy-start.42 = (bf16[8,1,72,128]{3,2,1,0:T(8,128)(2,1)S(1)}, bf16[8,1,72,128]{3,2,1,0:T(8,128)(2,1)}, u32[]{:S(2)}) copy-start(bf16[8,1,72,128]{3,2,1,0:T(8,128)(2,1)} %get-tuple-element.156) | copy-start | bytes 442372
  262.3 11.3 %slice-start.2 = ((s8[5308416]{0:T(1024)(128)(4,1)}), s8[4194304]{0:T(1024)(128)(4,1)S(1)}, s32[]{:S(2)}) async-start(s8[5308416]{0:T(1024)(128)(4,1)} %bitcast.230), calls=%async_computation.5 | async-start | bytes 8388608
  265.8 4.9 copy-start.40
  265.8 7.8 %slice-start.3 = ((s8[5308416]{0:T(1024)(128)(4,1)}), s8[1114112]{0:T(1024)(128)(4,1)S(1)}, s32[]{:S(2)}) async-start(s8[5308416]{0:T(1024)(128)(4,1)} %bitcast.230), calls=%async_computation.6 | async-start | bytes 2228224
  273.6 6.2 %copy-start.48 = (bf16[576,16]{0,1:T(8,128)(2,1)S(1)}, bf16[576,16]{0,1:T(8,128)(2,1)}, u32[]{:S(2)}) copy-start(bf16[576,16]{0,1:T(8,128)(2,1)} %reshape.523) | copy-start | bytes 55300
  279.7 3.1 copy-start.47
  279.7 3.8 copy-start.53
  279.7 4.4 copy-start.54
  279.7 5.0 copy-start.55
  279.7 6.0 %copy-start.52 = (f32[1152]{0:T(1024)S(1)}, f32[1152]{0:T(1024)}, u32[]{:S(2)}) copy-start(f32[1152]{0:T(1024)} %get-tuple-element.94) | copy-start | bytes 13828
  279.8 6.1 %copy-start.22 = (f32[1,4608]{1,0:T(1,128)S(1)}, f32[1,4608]{1,0:T(1,128)}, u32[]{:S(2)}) copy-start(f32[1,4608]{1,0:T(1,128)} %copy-done.21) | copy-start | bytes 55300
  282.2 8.8 %collective-permute-start.4 = (bf16[576,2304]{1,0:T(8,128)(2,1)}, bf16[576,2304]{1,0:T(8,128)(2,1)}, u32[]{:S(2)}, u32[]{:S(2)}) collective-permute-start(bf16[576,2304]{1,0:T(8,128)(2,1)} %convolution_convert_fusion.1), channel_id=1, source_target_pairs={{0,1},{1,0},{2,3},{3,2},{4,5},{5,4},{6,7},{7,6},{8,9},{9,8},{10,11... | collective-permute-start | bytes 7962632 | tf_op jit(solution)/shard_map/ppermute | solution.py:891
  290.9 4.3 copy-start.5
  290.9 4.3 copy-start.7
  291.0 127.3 %slice-start = ((s8[7962624]{0:T(1024)(128)(4,1)}), s8[4194304]{0:T(1024)(128)(4,1)S(1)}, s32[]{:S(2)}) async-start(s8[7962624]{0:T(1024)(128)(4,1)} %bitcast.214), calls=%async_computation.3 | async-start | bytes 8388608
  295.2 123.0 %slice-start.1 = ((s8[7962624]{0:T(1024)(128)(4,1)}), s8[3768320]{0:T(1024)(128)(4,1)S(1)}, s32[]{:S(2)}) async-start(s8[7962624]{0:T(1024)(128)(4,1)} %bitcast.214), calls=%async_computation.4 | async-start | bytes 7536640
  295.2 123.0 %copy-start.24 = (bf16[1,128,1152]{2,1,0:T(8,128)(2,1)S(1)}, bf16[1,128,1152]{2,1,0:T(8,128)(2,1)}, u32[]{:S(2)}) copy-start(bf16[1,128,1152]{2,1,0:T(8,128)(2,1)} %param.20) | copy-start | bytes 884740
  295.3 123.0 %copy-start.63 = (f32[128]{0:T(128)S(1)}, f32[128]{0:T(128)}, u32[]{:S(2)}) copy-start(f32[128]{0:T(128)} %copy-done.62) | copy-start | bytes 1540
  418.2 2.7 copy-start.14
  418.3 2.7 copy-start.25
  418.3 2.7 copy-start.58
  418.3 3.1 copy-start.50
  424.1 3.5 copy-start.59
  424.1 3.5 copy-start.60
  424.1 3.5 copy-start.61
  424.1 4.6 copy-start.56
  427.3 7.4 %collective-permute-start.5 = (bf16[576,3456]{1,0:T(8,128)(2,1)}, bf16[576,3456]{1,0:T(8,128)(2,1)}, u32[]{:S(2)}, u32[]{:S(2)}) collective-permute-start(bf16[576,3456]{1,0:T(8,128)(2,1)} %convolution_convert_fusion), channel_id=1, source_target_pairs={{0,1},{1,0},{2,3},{3,2},{4,5},{5,4},{6,7},{7,6},{8,9},{9,8},{10,11... | collective-permute-start | bytes 11943944 | tf_op jit(solution)/shard_map/ppermute | solution.py:891
  428.2 3.3 copy-start.15
  428.9 5.4 %collective-permute-start.6 = (bf16[576,17]{0,1:T(8,128)(2,1)S(1)}, bf16[576,17]{0,1:T(8,128)(2,1)S(1)}, u32[]{:S(2)}, u32[]{:S(2)}) collective-permute-start(bf16[576,17]{0,1:T(8,128)(2,1)S(1)} %convert_element_type.255), channel_id=1, source_target_pairs={{0,1},{1,0},{2,3},{3,2},{4,5},{5,4},{6,7},{7,6},{8,9},{9,8},{10,11... | collective-permute-start | bytes 58760 | tf_op jit(solution)/shard_map/ppermute | solution.py:1061
  (18 other events, 24.9 us)
Sparse Core Ops, SparseCore 0:
  230.4 138.3 reduce-scatter.1
